TPU v7x, 512 devices: a whole 4x8x8 slice. The times are simulated.
512 devices in a mesh: section: 8 (over z), seq: 16 (over y, core), dp: 4 (over x).
Axes of the slice: x: 4, y: 8, z: 8, core: 2. Of those that a mesh axis runs over, the one named last changes fastest.
Arguments:
- wave: bfloat16 [4, 16, 40], P('dp', 'seq'), may hold values from -6 to 6
- lengths: int32 [4, 16], P('dp'), may hold values from 10 to 40, as said below
- assign: int32 [4, 16], P('dp'), may hold values from 0 to 15, each once within a row
- conv_weight: bfloat16 [512, 10], replicated, may hold values from -2 to 2
- conv_bias: float32 [512], replicated, may hold values from -3 to 3
- conv_gain: float32 [512], replicated, may hold values from 0.1 to 1.9
- conv_shift: float32 [512], replicated, may hold values from -3 to 3
- feat_gain: float32 [512], replicated, may hold values from 0.1 to 1.9
- feat_shift: float32 [512], replicated, may hold values from -3 to 3
- proj_weight: bfloat16 [512, 4096], P(None, 'seq'), may hold values from -0.25 to 0.25
- proj_bias: float32 [4096], P('seq'), may hold values from -3 to 3
- norm_gain: float32 [8, 4096], P('section'), may hold values from 0.1 to 1.9
- norm_shift: float32 [8, 4096], P('section'), may hold values from -3 to 3
- query_weight: bfloat16 [8, 4096, 2048], P('section', None, 'seq'), may hold values from -1 to 1
- key_weight: bfloat16 [8, 4096, 2048], P('section', None, 'seq'), may hold values from -1 to 1
- value_weight: bfloat16 [8, 4096, 2048], P('section', None, 'seq'), may hold values from -0.09375 to 0.09375
- out_weight: bfloat16 [8, 2048, 4096], P('section', None, 'seq'), may hold values from -0.125 to 0.125
- out_bias: float32 [8, 4096], P('section', 'seq'), may hold values from -3 to 3
- feat_grad: bfloat16 [4, 16, 8, 512], P('dp', 'seq'), may hold values from -0.25 to 0.25
Outputs:
- section_out: bfloat16 [8, 4, 2, 64, 4096], P('section', 'dp', None, None, 'seq')
- conv_weight_grad: float32 [512, 10], replicated
- conv_bias_grad: float32 [512], replicated
- conv_gain_grad: float32 [512], replicated
- conv_shift_grad: float32 [512], replicated
Inputs may be any that keep to these rules, and one draw needn't show every extreme that they name: `lengths`: one utterance has length 40 and one has length 10. `assign`: each row holds every number below 16 once.
All inputs are finite; a program needn't handle non-finite values.
Results may differ from a plain program's by a relative error of at most 0.04.
Values may be sent and summed in bfloat16 or wider, within the bound.
No kernel may reach another device: no remote copies, remote signals or barrier semaphores. Data moves between devices by JAX's collectives and lax.ppermute only.
A program may use at most 64 MiB of HBM per device.

v0:
```python
import jax
import jax.numpy as jnp
from jax import lax
from jax.sharding import PartitionSpec as P

HEAD_DIM = 128
KERNEL = 10
STRIDE = 5
MICRO = 2


def from_behind(shard, axis, by):
    length = lax.axis_size(axis)
    pairs = [(i, i + by) for i in range(length) if 0 <= i + by < length]
    return lax.ppermute(shard, axis, pairs)


def layer_norm(values, gain, shift):
    average = jnp.mean(values, axis=-1, keepdims=True)
    centered = values - average
    spread = jnp.mean(centered * centered, axis=-1, keepdims=True)
    return centered * lax.rsqrt(spread + 1e-05) * gain + shift


def frame_counts(lengths):
    return (lengths - KERNEL) // STRIDE + 1


def frontend(weight, bias, gain, shift, framed, live):
    convolved = (
        jnp.einsum("...fk,ck->...fc", framed, weight, precision=lax.Precision.HIGHEST) + bias
    )
    active = jax.nn.gelu(layer_norm(convolved, gain, shift), approximate=False)
    return jnp.where(live[..., None], active, jnp.zeros_like(active))


def attend(
    current, counts, gain, shift, query_weight, key_weight, value_weight, out_weight, out_bias
):
    gathered_rows = lax.all_gather(current, "seq", axis=1, tiled=True)
    row_count = gathered_rows.shape[0]
    owners = counts.shape[0]
    frames = row_count // owners
    head_count = query_weight.shape[1] // HEAD_DIM
    normed = layer_norm(gathered_rows.astype(jnp.float32), gain, shift).astype(jnp.bfloat16)
    queries = (
        jnp.dot(normed, query_weight, preferred_element_type=jnp.float32) * HEAD_DIM ** (-0.5)
    ).astype(jnp.bfloat16)
    key_rows = jnp.dot(normed, key_weight, preferred_element_type=jnp.float32).astype(jnp.bfloat16)
    value_rows = jnp.dot(normed, value_weight, preferred_element_type=jnp.float32).astype(
        jnp.bfloat16
    )
    split_shape = (owners, frames, head_count, HEAD_DIM)
    scores = jnp.einsum(
        "ufhd,ughd->uhfg",
        queries.reshape(split_shape),
        key_rows.reshape(split_shape),
        preferred_element_type=jnp.float32,
    )
    is_live = lax.broadcasted_iota(jnp.int32, (owners, frames), 1) < counts[:, None]
    scores = jnp.where(is_live[:, None, None, :], scores, -jnp.inf)
    row_max = jnp.max(scores, axis=-1, keepdims=True)
    raised = jnp.exp(scores - row_max)
    attention = (raised / jnp.sum(raised, axis=-1, keepdims=True)).astype(jnp.bfloat16)
    mixture = jnp.einsum(
        "uhfg,ughd->ufhd",
        attention,
        value_rows.reshape(split_shape),
        preferred_element_type=jnp.float32,
    )
    mixture = mixture.astype(jnp.bfloat16).reshape(row_count, head_count * HEAD_DIM)
    branch = jnp.dot(
        lax.all_gather(mixture, "seq", axis=1, tiled=True),
        out_weight,
        preferred_element_type=jnp.float32,
    )
    return (current.astype(jnp.float32) + branch + out_bias).astype(jnp.bfloat16)


def on_device(
    wave,
    lengths,
    assign,
    conv_weight,
    conv_bias,
    conv_gain,
    conv_shift,
    feat_gain,
    feat_shift,
    proj_weight,
    proj_bias,
    norm_gain,
    norm_shift,
    query_weight,
    key_weight,
    value_weight,
    out_weight,
    out_bias,
    feat_grad,
):
    seq_index = lax.axis_index("seq")
    local_replicas = wave.shape[0]
    owned = wave.shape[1]
    frame_total = wave.shape[2] // STRIDE
    own_lengths = lax.dynamic_slice_in_dim(lengths, seq_index * owned, owned, 1)
    positions = lax.broadcasted_iota(jnp.int32, wave.shape, 2)
    cleaned = jnp.where(positions < own_lengths[:, :, None], wave, jnp.zeros_like(wave))
    blocks = cleaned.reshape(local_replicas, owned, frame_total, STRIDE).astype(jnp.float32)
    after = jnp.concatenate(
        [blocks[:, :, 1:], jnp.zeros((local_replicas, owned, 1, STRIDE), jnp.float32)], axis=2
    )
    framed = jnp.concatenate([blocks, after], axis=3)
    own_counts = frame_counts(own_lengths)
    live = (
        lax.broadcasted_iota(jnp.int32, (local_replicas, owned, frame_total), 2)
        < own_counts[:, :, None]
    )

    def frontend_at(weight, bias, gain, shift):
        return frontend(weight, bias, gain, shift, framed, live)

    features, pullback = jax.vjp(
        frontend_at, conv_weight.astype(jnp.float32), conv_bias, conv_gain, conv_shift
    )
    partial_grads = pullback(feat_grad.astype(jnp.float32))
    gradients = lax.psum(
        (partial_grads[0], partial_grads[1], partial_grads[2], partial_grads[3]), ("seq", "dp")
    )
    gathered = lax.all_gather(features.astype(jnp.bfloat16), "seq", axis=1, tiled=True)
    batch_size = lengths.shape[1]
    counts = frame_counts(lengths)
    slot_ids = lax.broadcasted_iota(jnp.int32, (1, 1, batch_size), 2)
    chosen = assign[:, :, None] == slot_ids
    ordered = jnp.sum(
        jnp.where(chosen[:, :, :, None, None], gathered.astype(jnp.float32)[:, :, None], 0.0),
        axis=1,
    ).astype(jnp.bfloat16)[0]
    slot_counts = jnp.sum(jnp.where(chosen, counts[:, :, None], 0), axis=1)[0]
    utt_frames = ordered.shape[1]
    columns = proj_weight.shape[1]
    normed = layer_norm(ordered.astype(jnp.float32), feat_gain, feat_shift).astype(jnp.bfloat16)
    projected = (
        jnp.dot(
            normed.reshape(batch_size * utt_frames, normed.shape[2]),
            proj_weight,
            preferred_element_type=jnp.float32,
        )
        + proj_bias
    )
    projected = projected.astype(jnp.bfloat16)
    split_count = 1
    pieces = MICRO * split_count
    piece_rows = batch_size * utt_frames // pieces
    entering = projected.reshape(pieces, piece_rows, columns)
    piece_counts = slot_counts.reshape(pieces, batch_size // pieces)
    section_id = lax.axis_index("section")
    tick_count = lax.axis_size("section") + pieces - 1
    layer_gain = norm_gain[0]
    layer_shift = norm_shift[0]
    query_part = query_weight[0]
    key_part = key_weight[0]
    value_part = value_weight[0]
    out_part = out_weight[0]
    bias_part = out_bias[0]

    def advance(tick_num, loop_state):
        previous, outputs = loop_state
        arrived = from_behind(previous, "section", 1)
        piece_num = tick_num - section_id
        slot_index = jnp.clip(piece_num, 0, pieces - 1)
        fresh = lax.dynamic_index_in_dim(entering, slot_index, 0, keepdims=False)
        current = jnp.where(section_id == 0, fresh, arrived)
        counts_now = lax.dynamic_index_in_dim(piece_counts, slot_index, 0, keepdims=False)
        result = attend(
            current,
            counts_now,
            layer_gain,
            layer_shift,
            query_part,
            key_part,
            value_part,
            out_part,
            bias_part,
        )
        is_live = (piece_num >= 0) & (piece_num < pieces)
        retained = lax.dynamic_index_in_dim(outputs, slot_index, 0, keepdims=False)
        outputs = lax.dynamic_update_index_in_dim(
            outputs, jnp.where(is_live, result, retained), slot_index, 0
        )
        return (result, outputs)

    start_state = (
        jnp.zeros((piece_rows, columns), jnp.bfloat16),
        jnp.zeros((pieces, piece_rows, columns), jnp.bfloat16),
    )
    collected = lax.fori_loop(0, tick_count, advance, start_state)[1]
    section_out = collected.reshape(1, 1, MICRO, batch_size * utt_frames // MICRO, columns)
    return (section_out, gradients[0], gradients[1], gradients[2], gradients[3])


def solution(mesh):
    return jax.shard_map(
        on_device,
        mesh=mesh,
        in_specs=(
            P("dp", "seq", None),
            P("dp", None),
            P("dp", None),
            P(),
            P(),
            P(),
            P(),
            P(),
            P(),
            P(None, "seq"),
            P("seq"),
            P("section", None),
            P("section", None),
            P("section", None, "seq"),
            P("section", None, "seq"),
            P("section", None, "seq"),
            P("section", None, "seq"),
            P("section", "seq"),
            P("dp", "seq", None, None),
        ),
        out_specs=(P("section", "dp", None, None, "seq"), P(), P(), P(), P()),
        check_vma=False,
    )
```

profile of v0, /device:TPU:449, one launch (start us, length us, event | category | flops | bytes accessed | tf_op | source)
XLA Modules:
  0.0 658.5 jit_solution(17524780394851380961)
XLA Ops:
  2.0 1.3 fusion.57
  8.9 247.0 %all-reduce.1 = (f32[512,10]{0,1:T(8,128)}, f32[512]{0:T(512)}, f32[512]{0:T(512)}, f32[512]{0:T(512)}) all-reduce(f32[512,10]{0,1:T(8,128)S(1)} %fusion.38, f32[512]{0:T(512)S(1)} %add_reduce_fusion, f32[512]{0:T(512)S(1)} %get-tuple-element.322, ...), channel_id=1, replica_groups=mesh['section'=8,'seq'=16,'dp'=4] {'seq','dp'}, use_global_device_ids=true, to_apply=%region_14.15 | all-reduce | flops 6656 | bytes 53248 | tf_op jit(solution)/shard_map/psum | solution.py:126
  256.8 19.3 %all-gather = bf16[128,512]{1,0:T(8,128)(2,1)S(1)} all-gather(bf16[8,512]{1,0:T(8,128)(2,1)S(1)} %select_convert_fusion), channel_id=2, replica_groups=mesh['section'=8,'seq'=16,'dp'=4] {'seq'}, dimensions={0}, use_global_device_ids=true | all-gather | bytes 139264 | tf_op jit(solution)/shard_map/all_gather | solution.py:129
  278.4 379.4 %while.17 = (s32[]{:T(128)}, bf16[64,256]{1,0:T(8,128)(2,1)S(1)}, bf16[2,64,256]{2,1,0:T(8,128)(2,1)S(1)}, pred[]{:T(512)}, s32[]{:T(128)}, /*index=5*/bf16[2,64...) while((s32[]{:T(128)}, bf16[64,256]{1,0:T(8,128)(2,1)S(1)}, ...), condition=%wide.region_11.12_spmd.clone, body=%wide.region_6.11_spmd.clone.sunk | while | flops 275147392 | bytes 12756246 | solution.py:196
  278.4 1.3 collective-permute-start
  279.8 3.3 collective-permute-done
  283.1 18.7 %all_gather.24 = bf16[64,4096]{1,0:T(8,128)(2,1)S(1)} all-gather(bf16[64,256]{1,0:T(8,128)(2,1)S(1)} %bitcast_select_fusion.3), channel_id=1, replica_groups=mesh['section'=8,'seq'=16,'dp'=4] {'seq'}, dimensions={1}, use_global_device_ids=true | all-gather | bytes 557056 | tf_op jit(solution)/shard_map/while/body/eval_jaxpr/all_gather | solution.py:40
  302.7 1.8 fusion.108
  305.0 15.2 %all_gather.25 = bf16[64,2048]{1,0:T(8,128)(2,1)S(1)} all-gather(bf16[64,128]{1,0:T(8,128)(2,1)S(1)} %fusion.109), channel_id=1, replica_groups=mesh['section'=8,'seq'=16,'dp'=4] {'seq'}, dimensions={1}, use_global_device_ids=true | all-gather | bytes 278528 | tf_op jit(solution)/shard_map/while/body/eval_jaxpr/all_gather | solution.py:73
  320.5 1.3 collective-permute-start
  321.9 3.3 collective-permute-done
  325.2 18.4 %all_gather.24 = bf16[64,4096]{1,0:T(8,128)(2,1)S(1)} all-gather(bf16[64,256]{1,0:T(8,128)(2,1)S(1)} %bitcast_select_fusion.3), channel_id=1, replica_groups=mesh['section'=8,'seq'=16,'dp'=4] {'seq'}, dimensions={1}, use_global_device_ids=true | all-gather | bytes 557056 | tf_op jit(solution)/shard_map/while/body/eval_jaxpr/all_gather | solution.py:40
  344.5 1.8 fusion.108
  346.8 15.2 %all_gather.25 = bf16[64,2048]{1,0:T(8,128)(2,1)S(1)} all-gather(bf16[64,128]{1,0:T(8,128)(2,1)S(1)} %fusion.109), channel_id=1, replica_groups=mesh['section'=8,'seq'=16,'dp'=4] {'seq'}, dimensions={1}, use_global_device_ids=true | all-gather | bytes 278528 | tf_op jit(solution)/shard_map/while/body/eval_jaxpr/all_gather | solution.py:73
  362.3 1.3 collective-permute-start
  363.7 3.3 collective-permute-done
  367.0 18.4 %all_gather.24 = bf16[64,4096]{1,0:T(8,128)(2,1)S(1)} all-gather(bf16[64,256]{1,0:T(8,128)(2,1)S(1)} %bitcast_select_fusion.3), channel_id=1, replica_groups=mesh['section'=8,'seq'=16,'dp'=4] {'seq'}, dimensions={1}, use_global_device_ids=true | all-gather | bytes 557056 | tf_op jit(solution)/shard_map/while/body/eval_jaxpr/all_gather | solution.py:40
  386.3 1.8 fusion.108
  388.6 15.2 %all_gather.25 = bf16[64,2048]{1,0:T(8,128)(2,1)S(1)} all-gather(bf16[64,128]{1,0:T(8,128)(2,1)S(1)} %fusion.109), channel_id=1, replica_groups=mesh['section'=8,'seq'=16,'dp'=4] {'seq'}, dimensions={1}, use_global_device_ids=true | all-gather | bytes 278528 | tf_op jit(solution)/shard_map/while/body/eval_jaxpr/all_gather | solution.py:73
  404.1 1.3 collective-permute-start
  405.5 3.3 collective-permute-done
  408.8 18.4 %all_gather.24 = bf16[64,4096]{1,0:T(8,128)(2,1)S(1)} all-gather(bf16[64,256]{1,0:T(8,128)(2,1)S(1)} %bitcast_select_fusion.3), channel_id=1, replica_groups=mesh['section'=8,'seq'=16,'dp'=4] {'seq'}, dimensions={1}, use_global_device_ids=true | all-gather | bytes 557056 | tf_op jit(solution)/shard_map/while/body/eval_jaxpr/all_gather | solution.py:40
  428.1 1.8 fusion.108
  430.4 15.2 %all_gather.25 = bf16[64,2048]{1,0:T(8,128)(2,1)S(1)} all-gather(bf16[64,128]{1,0:T(8,128)(2,1)S(1)} %fusion.109), channel_id=1, replica_groups=mesh['section'=8,'seq'=16,'dp'=4] {'seq'}, dimensions={1}, use_global_device_ids=true | all-gather | bytes 278528 | tf_op jit(solution)/shard_map/while/body/eval_jaxpr/all_gather | solution.py:73
  445.9 1.3 collective-permute-start
  447.3 3.3 collective-permute-done
  450.6 18.4 %all_gather.24 = bf16[64,4096]{1,0:T(8,128)(2,1)S(1)} all-gather(bf16[64,256]{1,0:T(8,128)(2,1)S(1)} %bitcast_select_fusion.3), channel_id=1, replica_groups=mesh['section'=8,'seq'=16,'dp'=4] {'seq'}, dimensions={1}, use_global_device_ids=true | all-gather | bytes 557056 | tf_op jit(solution)/shard_map/while/body/eval_jaxpr/all_gather | solution.py:40
  469.9 1.8 fusion.108
  472.2 15.2 %all_gather.25 = bf16[64,2048]{1,0:T(8,128)(2,1)S(1)} all-gather(bf16[64,128]{1,0:T(8,128)(2,1)S(1)} %fusion.109), channel_id=1, replica_groups=mesh['section'=8,'seq'=16,'dp'=4] {'seq'}, dimensions={1}, use_global_device_ids=true | all-gather | bytes 278528 | tf_op jit(solution)/shard_map/while/body/eval_jaxpr/all_gather | solution.py:73
  487.7 1.3 collective-permute-start
  489.1 3.3 collective-permute-done
  492.4 18.4 %all_gather.24 = bf16[64,4096]{1,0:T(8,128)(2,1)S(1)} all-gather(bf16[64,256]{1,0:T(8,128)(2,1)S(1)} %bitcast_select_fusion.3), channel_id=1, replica_groups=mesh['section'=8,'seq'=16,'dp'=4] {'seq'}, dimensions={1}, use_global_device_ids=true | all-gather | bytes 557056 | tf_op jit(solution)/shard_map/while/body/eval_jaxpr/all_gather | solution.py:40
  511.7 1.8 fusion.108
  514.0 15.2 %all_gather.25 = bf16[64,2048]{1,0:T(8,128)(2,1)S(1)} all-gather(bf16[64,128]{1,0:T(8,128)(2,1)S(1)} %fusion.109), channel_id=1, replica_groups=mesh['section'=8,'seq'=16,'dp'=4] {'seq'}, dimensions={1}, use_global_device_ids=true | all-gather | bytes 278528 | tf_op jit(solution)/shard_map/while/body/eval_jaxpr/all_gather | solution.py:73
  529.5 1.3 collective-permute-start
  531.0 4.3 collective-permute-done
  535.3 17.8 %all_gather.24 = bf16[64,4096]{1,0:T(8,128)(2,1)S(1)} all-gather(bf16[64,256]{1,0:T(8,128)(2,1)S(1)} %bitcast_select_fusion.3), channel_id=1, replica_groups=mesh['section'=8,'seq'=16,'dp'=4] {'seq'}, dimensions={1}, use_global_device_ids=true | all-gather | bytes 557056 | tf_op jit(solution)/shard_map/while/body/eval_jaxpr/all_gather | solution.py:40
  554.0 1.8 fusion.108
  556.3 15.2 %all_gather.25 = bf16[64,2048]{1,0:T(8,128)(2,1)S(1)} all-gather(bf16[64,128]{1,0:T(8,128)(2,1)S(1)} %fusion.109), channel_id=1, replica_groups=mesh['section'=8,'seq'=16,'dp'=4] {'seq'}, dimensions={1}, use_global_device_ids=true | all-gather | bytes 278528 | tf_op jit(solution)/shard_map/while/body/eval_jaxpr/all_gather | solution.py:73
  571.8 1.3 collective-permute-start
  573.2 5.0 collective-permute-done
  578.3 17.8 %all_gather.24 = bf16[64,4096]{1,0:T(8,128)(2,1)S(1)} all-gather(bf16[64,256]{1,0:T(8,128)(2,1)S(1)} %bitcast_select_fusion.3), channel_id=1, replica_groups=mesh['section'=8,'seq'=16,'dp'=4] {'seq'}, dimensions={1}, use_global_device_ids=true | all-gather | bytes 557056 | tf_op jit(solution)/shard_map/while/body/eval_jaxpr/all_gather | solution.py:40
  597.0 1.8 fusion.108
  599.3 15.2 %all_gather.25 = bf16[64,2048]{1,0:T(8,128)(2,1)S(1)} all-gather(bf16[64,128]{1,0:T(8,128)(2,1)S(1)} %fusion.109), channel_id=1, replica_groups=mesh['section'=8,'seq'=16,'dp'=4] {'seq'}, dimensions={1}, use_global_device_ids=true | all-gather | bytes 278528 | tf_op jit(solution)/shard_map/while/body/eval_jaxpr/all_gather | solution.py:73
  616.3 5.0 collective-permute-done
  621.3 17.8 %all_gather.24 = bf16[64,4096]{1,0:T(8,128)(2,1)S(1)} all-gather(bf16[64,256]{1,0:T(8,128)(2,1)S(1)} %bitcast_select_fusion.3), channel_id=1, replica_groups=mesh['section'=8,'seq'=16,'dp'=4] {'seq'}, dimensions={1}, use_global_device_ids=true | all-gather | bytes 557056 | tf_op jit(solution)/shard_map/while/body/eval_jaxpr/all_gather | solution.py:40
  640.0 1.8 fusion.108
  642.3 15.2 %all_gather.25 = bf16[64,2048]{1,0:T(8,128)(2,1)S(1)} all-gather(bf16[64,128]{1,0:T(8,128)(2,1)S(1)} %fusion.109), channel_id=1, replica_groups=mesh['section'=8,'seq'=16,'dp'=4] {'seq'}, dimensions={1}, use_global_device_ids=true | all-gather | bytes 278528 | tf_op jit(solution)/shard_map/while/body/eval_jaxpr/all_gather | solution.py:73
  (181 shorter events, 26.4 us)
Async XLA Ops:
  0.6 277.2 %copy-start = (bf16[512,256]{1,0:T(8,128)(2,1)S(1)}, bf16[512,256]{1,0:T(8,128)(2,1)}, u32[]{:S(2)}) copy-start(bf16[512,256]{1,0:T(8,128)(2,1)} %param.30) | copy-start | bytes 786436
  0.6 277.2 %copy-start.11 = (f32[512]{0:T(512)S(1)}, f32[512]{0:T(512)}, u32[]{:S(2)}) copy-start(f32[512]{0:T(512)} %param.28) | copy-start | bytes 6148
  0.7 277.2 %copy-start.10 = (f32[512]{0:T(512)S(1)}, f32[512]{0:T(512)}, u32[]{:S(2)}) copy-start(f32[512]{0:T(512)} %param.29) | copy-start | bytes 6148
  0.7 277.2 %copy-start.12 = (f32[256]{0:T(256)S(1)}, f32[256]{0:T(256)}, u32[]{:S(2)}) copy-start(f32[256]{0:T(256)} %param.31) | copy-start | bytes 3076
  8.6 269.5 %copy-start.5 = (s32[1,16]{1,0:T(1,128)S(1)}, s32[1,16]{1,0:T(1,128)}, u32[]{:S(2)}) copy-start(s32[1,16]{1,0:T(1,128)} %param.22) | copy-start | bytes 196
  8.6 269.6 %copy-start.4 = (s32[1,16]{1,0:T(1,128)S(1)}, s32[1,16]{1,0:T(1,128)}, u32[]{:S(2)}) copy-start(s32[1,16]{1,0:T(1,128)} %param.23) | copy-start | bytes 196
  8.6 269.8 %copy-start.6 = (bf16[1,4096,128]{2,1,0:T(8,128)(2,1)S(1)}, bf16[1,4096,128]{2,1,0:T(8,128)(2,1)}, u32[]{:S(2)}) copy-start(bf16[1,4096,128]{2,1,0:T(8,128)(2,1)} %param.36) | copy-start | bytes 3145732
  8.9 269.5 %copy-start.1 = (bf16[1,2048,256]{2,1,0:T(8,128)(2,1)S(1)}, bf16[1,2048,256]{2,1,0:T(8,128)(2,1)}, u32[]{:S(2)}) copy-start(bf16[1,2048,256]{2,1,0:T(8,128)(2,1)} %param.37) | copy-start | bytes 3145732
  8.9 269.5 %copy-start.3 = (f32[1,256]{1,0:T(1,128)S(1)}, f32[1,256]{1,0:T(1,128)}, u32[]{:S(2)}) copy-start(f32[1,256]{1,0:T(1,128)} %param.38) | copy-start | bytes 3076
  8.9 269.5 %copy-start.8 = (f32[1,4096]{1,0:T(1,128)S(1)}, f32[1,4096]{1,0:T(1,128)}, u32[]{:S(2)}) copy-start(f32[1,4096]{1,0:T(1,128)} %param.32) | copy-start | bytes 49156
  8.9 269.4 %copy-start.9 = (f32[1,4096]{1,0:T(1,128)S(1)}, f32[1,4096]{1,0:T(1,128)}, u32[]{:S(2)}) copy-start(f32[1,4096]{1,0:T(1,128)} %param.33) | copy-start | bytes 49156
  278.4 4.7 collective-permute-start
  279.8 22.5 %copy-start.7 = (bf16[4096,128]{1,0:T(8,128)(2,1)S(1)}, bf16[4096,128]{1,0:T(8,128)(2,1)}, u32[]{:S(2)}) copy-start(bf16[4096,128]{1,0:T(8,128)(2,1)} %get-tuple-element.507) | copy-start | bytes 3145732 | tf_op jit(solution)/shard_map/while
  320.5 4.7 collective-permute-start
  321.9 22.2 %copy-start.7 = (bf16[4096,128]{1,0:T(8,128)(2,1)S(1)}, bf16[4096,128]{1,0:T(8,128)(2,1)}, u32[]{:S(2)}) copy-start(bf16[4096,128]{1,0:T(8,128)(2,1)} %get-tuple-element.507) | copy-start | bytes 3145732 | tf_op jit(solution)/shard_map/while
  362.3 4.7 collective-permute-start
  363.7 22.2 %copy-start.7 = (bf16[4096,128]{1,0:T(8,128)(2,1)S(1)}, bf16[4096,128]{1,0:T(8,128)(2,1)}, u32[]{:S(2)}) copy-start(bf16[4096,128]{1,0:T(8,128)(2,1)} %get-tuple-element.507) | copy-start | bytes 3145732 | tf_op jit(solution)/shard_map/while
  404.1 4.7 collective-permute-start
  405.5 22.2 %copy-start.7 = (bf16[4096,128]{1,0:T(8,128)(2,1)S(1)}, bf16[4096,128]{1,0:T(8,128)(2,1)}, u32[]{:S(2)}) copy-start(bf16[4096,128]{1,0:T(8,128)(2,1)} %get-tuple-element.507) | copy-start | bytes 3145732 | tf_op jit(solution)/shard_map/while
  445.9 4.7 collective-permute-start
  447.3 22.2 %copy-start.7 = (bf16[4096,128]{1,0:T(8,128)(2,1)S(1)}, bf16[4096,128]{1,0:T(8,128)(2,1)}, u32[]{:S(2)}) copy-start(bf16[4096,128]{1,0:T(8,128)(2,1)} %get-tuple-element.507) | copy-start | bytes 3145732 | tf_op jit(solution)/shard_map/while
  487.7 4.7 collective-permute-start
  489.1 22.2 %copy-start.7 = (bf16[4096,128]{1,0:T(8,128)(2,1)S(1)}, bf16[4096,128]{1,0:T(8,128)(2,1)}, u32[]{:S(2)}) copy-start(bf16[4096,128]{1,0:T(8,128)(2,1)} %get-tuple-element.507) | copy-start | bytes 3145732 | tf_op jit(solution)/shard_map/while
  529.5 5.7 collective-permute-start
  530.9 22.6 %copy-start.7 = (bf16[4096,128]{1,0:T(8,128)(2,1)S(1)}, bf16[4096,128]{1,0:T(8,128)(2,1)}, u32[]{:S(2)}) copy-start(bf16[4096,128]{1,0:T(8,128)(2,1)} %get-tuple-element.507) | copy-start | bytes 3145732 | tf_op jit(solution)/shard_map/while
  571.8 6.4 collective-permute-start
  573.2 23.4 %copy-start.7 = (bf16[4096,128]{1,0:T(8,128)(2,1)S(1)}, bf16[4096,128]{1,0:T(8,128)(2,1)}, u32[]{:S(2)}) copy-start(bf16[4096,128]{1,0:T(8,128)(2,1)} %get-tuple-element.507) | copy-start | bytes 3145732 | tf_op jit(solution)/shard_map/while
  614.8 6.4 collective-permute-start
  616.2 23.4 %copy-start.7 = (bf16[4096,128]{1,0:T(8,128)(2,1)S(1)}, bf16[4096,128]{1,0:T(8,128)(2,1)}, u32[]{:S(2)}) copy-start(bf16[4096,128]{1,0:T(8,128)(2,1)} %get-tuple-element.507) | copy-start | bytes 3145732 | tf_op jit(solution)/shard_map/while
  657.8 0.6 copy-start.2
where the time goes:
time: 668 us; the launch traced here: 658 us
  blocking collectives  567 us (85%)
  waiting for transfers between devices  33.9 us (5%)
  matrix products  28.6 us (4%)
  other arithmetic  12.6 us (2%)
  starting transfers between devices  11.6 us (2%)
    psum x1, blocking collectives, on_device(): lax.psum((partial_grads[0], partial_grads[1], partial_grads[2], partial_g...  247 us
    all_gather x9, blocking collectives, attend(): gathered_rows = lax.all_gather(current, 'seq', axis=1, tiled=True)  164 us
    all_gather x9, blocking collectives, attend(): lax.all_gather(mixture, 'seq', axis=1, tiled=True)  137 us
    ppermute x9, waiting for transfers between devices, from_behind(): return lax.ppermute(shard, axis, pairs)  33.9 us
    all_gather x1, blocking collectives, on_device(): lax.all_gather(features.astype(jnp.bfloat16), 'seq', axis=1, tiled=True)  19.3 us
    sub x9, matrix products, attend(): raised = jnp.exp(scores - row_max)  16 us
  transfers between devices with their start and end apart: 9, of which 9 were waited for; matrix products, arithmetic and copies ran while one was open for 0% of the time, Pallas kernels for 0%

commit v1 on v0

v1 whole, which is shorter than its diff:
```python
import functools

import jax
import jax.numpy as jnp
from jax import lax
from jax.sharding import Mesh, PartitionSpec as P

HEAD_DIM = 128
KERNEL = 10
STRIDE = 5
MICRO = 2
CORES = 2


def layer_norm(values, gain, shift):
    average = jnp.mean(values, axis=-1, keepdims=True)
    centered = values - average
    spread = jnp.mean(centered * centered, axis=-1, keepdims=True)
    return centered * lax.rsqrt(spread + 1e-05) * gain + shift


def frame_counts(lengths):
    return (lengths - KERNEL) // STRIDE + 1


def framed_of(wave, lengths):
    owners, samples = wave.shape
    positions = lax.broadcasted_iota(jnp.int32, wave.shape, 1)
    cleaned = jnp.where(positions < lengths[:, None], wave, jnp.zeros_like(wave))
    blocks = cleaned.reshape(owners, samples // STRIDE, STRIDE)
    after = jnp.concatenate([blocks[:, 1:], jnp.zeros_like(blocks[:, :1])], axis=1)
    return jnp.concatenate([blocks, after], axis=2)


def live_of(lengths, frame_total):
    counts = frame_counts(lengths)
    return lax.broadcasted_iota(jnp.int32, (lengths.shape[0], frame_total), 1) < counts[:, None]


def frontend(weight, bias, gain, shift, framed, live):
    convolved = (
        jnp.einsum("...fk,ck->...fc", framed, weight, precision=lax.Precision.HIGHEST) + bias
    )
    active = jax.nn.gelu(layer_norm(convolved, gain, shift), approximate=False)
    return jnp.where(live[..., None], active, jnp.zeros_like(active))


def one_head(normed, counts, query_weight, key_weight, value_weight):
    rows = normed.shape[0]
    owners = counts.shape[0]
    frames = rows // owners
    product = functools.partial(jnp.dot, preferred_element_type=jnp.float32)
    queries = (product(normed, query_weight) * HEAD_DIM ** (-0.5)).astype(jnp.bfloat16)
    key_rows = product(normed, key_weight).astype(jnp.bfloat16)
    value_rows = product(normed, value_weight).astype(jnp.bfloat16)
    split = (owners, frames, HEAD_DIM)
    scores = jnp.einsum(
        "ufd,ugd->ufg",
        queries.reshape(split),
        key_rows.reshape(split),
        preferred_element_type=jnp.float32,
    )
    live = lax.broadcasted_iota(jnp.int32, (owners, frames), 1) < counts[:, None]
    scores = jnp.where(live[:, None, :], scores, -jnp.inf)
    raised = jnp.exp(scores - jnp.max(scores, axis=-1, keepdims=True))
    attention = (raised / jnp.sum(raised, axis=-1, keepdims=True)).astype(jnp.bfloat16)
    mixture = jnp.einsum(
        "ufg,ugd->ufd",
        attention,
        value_rows.reshape(split),
        preferred_element_type=jnp.float32,
    )
    return mixture.astype(jnp.bfloat16).reshape(rows, HEAD_DIM)


def on_device(
    wave,
    lengths,
    assign,
    conv_weight,
    conv_bias,
    conv_gain,
    conv_shift,
    feat_gain,
    feat_shift,
    proj_weight,
    proj_bias,
    norm_gain,
    norm_shift,
    query_weight,
    key_weight,
    value_weight,
    out_weight,
    out_bias,
    feat_grad,
):
    section = lax.axis_index("section")
    core = lax.axis_index("core")
    sections = lax.axis_size("section")
    seq_index = lax.axis_index("y") * CORES + core
    samples = wave.shape[2]
    frame_total = samples // STRIDE
    batch_size = lengths.shape[1]
    utts = batch_size // MICRO

    def swapped(value):
        return lax.ppermute(value, "core", [(0, 1), (1, 0)])

    def in_order(mine, others):
        return jnp.where(core == 0, jnp.stack([mine, others]), jnp.stack([others, mine]))

    waves = lax.all_gather(wave[0], ("y", "core"), axis=0, tiled=True)
    proj_other = swapped(proj_weight)
    bias_mine = jnp.stack([proj_bias, out_bias[0]])
    bias_other = swapped(bias_mine)
    query_pair = (query_weight[0], swapped(query_weight[0]))
    key_pair = (key_weight[0], swapped(key_weight[0]))
    value_pair = (value_weight[0], swapped(value_weight[0]))
    out_pair = (out_weight[0], swapped(out_weight[0]))

    slots = core * utts + lax.broadcasted_iota(jnp.int32, (batch_size, utts), 1)
    chosen = assign[0][:, None] == slots
    slot_lengths = jnp.sum(jnp.where(chosen, lengths[0][:, None], 0), axis=0)
    slot_waves = jnp.sum(
        jnp.where(chosen[:, :, None], waves[:, None].astype(jnp.float32), 0.0), axis=0
    ).astype(jnp.bfloat16)
    framed = framed_of(slot_waves, slot_lengths)
    convolved = (
        jnp.einsum("ufk,ck->ufc", framed, conv_weight, preferred_element_type=jnp.float32)
        + conv_bias
    )
    active = jax.nn.gelu(layer_norm(convolved, conv_gain, conv_shift), approximate=False)
    live = live_of(slot_lengths, frame_total)
    frames = jnp.where(live[..., None], active, 0.0).astype(jnp.bfloat16)
    frames = frames.reshape(utts * frame_total, frames.shape[2])
    normed_frames = layer_norm(frames.astype(jnp.float32), feat_gain, feat_shift).astype(
        jnp.bfloat16
    )

    def projected(weight, bias):
        total = jnp.dot(normed_frames, weight, preferred_element_type=jnp.float32)
        return (total + bias).astype(jnp.bfloat16)

    entering = in_order(projected(proj_weight, proj_bias), projected(proj_other, bias_other[0]))
    counts = frame_counts(slot_lengths)

    def attend(current):
        gathered = lax.all_gather(current, "y", axis=0, tiled=False)
        rows = gathered.shape[2]
        whole = gathered.transpose(2, 0, 1, 3).reshape(rows, -1)
        normed = layer_norm(whole.astype(jnp.float32), norm_gain[0], norm_shift[0]).astype(
            jnp.bfloat16
        )
        mine, others = (
            one_head(normed, counts, query_pair[i], key_pair[i], value_pair[i]) for i in range(2)
        )
        mixed = lax.all_gather(in_order(mine, others), "y", axis=0, tiled=False)
        mixed = mixed.transpose(2, 0, 1, 3).reshape(rows, -1)
        branches = in_order(
            jnp.dot(mixed, out_pair[0], preferred_element_type=jnp.float32) + bias_mine[1],
            jnp.dot(mixed, out_pair[1], preferred_element_type=jnp.float32) + bias_other[1],
        )
        return (current.astype(jnp.float32) + branches).astype(jnp.bfloat16)

    def gradients_of():
        own_lengths = lax.dynamic_slice_in_dim(lengths[0], seq_index, 1, 0)
        own_framed = framed_of(wave[0], own_lengths).astype(jnp.float32)
        own_live = live_of(own_lengths, frame_total)

        def frontend_at(weight, bias, gain, shift):
            return frontend(weight, bias, gain, shift, own_framed, own_live)

        _, pullback = jax.vjp(
            frontend_at, conv_weight.astype(jnp.float32), conv_bias, conv_gain, conv_shift
        )
        partial = pullback(feat_grad[0].astype(jnp.float32))
        packed = jnp.concatenate(
            [partial[0].T, partial[1][None], partial[2][None], partial[3][None]], axis=0
        )
        packed = jnp.pad(packed, ((0, 16 - packed.shape[0]), (0, 0)))
        packed = lax.psum(packed, "core")
        packed = lax.psum(packed, "dp")
        return lax.psum(packed, "y")

    early = section >= sections // 2
    packed = lax.cond(
        early, gradients_of, lambda: jnp.zeros((16, conv_bias.shape[0]), jnp.float32)
    )
    entering, packed = lax.optimization_barrier((entering, packed))

    current, result = entering, entering
    for tick in range(sections):
        result = lax.cond(section == tick, lambda now, was: attend(now), lambda now, was: was, current, result)
        if tick < sections - 1:
            current = lax.ppermute(result, "section", [(tick, tick + 1)])

    result, packed = lax.optimization_barrier((result, packed))
    packed = lax.cond(early, lambda: packed, gradients_of)
    mine = lax.dynamic_index_in_dim(result, core, 0, keepdims=False)
    leaving = lax.dynamic_index_in_dim(result, 1 - core, 0, keepdims=False)
    section_out = in_order(mine, swapped(leaving))[None, None]
    return (section_out, packed[:KERNEL].T, packed[KERNEL], packed[KERNEL + 1], packed[KERNEL + 2])


def solution(mesh):
    sizes = dict(mesh.shape)
    split = Mesh(
        mesh.devices.reshape(
            sizes["section"], sizes["seq"] // CORES, CORES, sizes["dp"]
        ),
        ("section", "y", "core", "dp"),
    )
    seq = ("y", "core")
    return jax.shard_map(
        on_device,
        mesh=split,
        in_specs=(
            P("dp", seq, None),
            P("dp", None),
            P("dp", None),
            P(),
            P(),
            P(),
            P(),
            P(),
            P(),
            P(None, seq),
            P(seq),
            P("section", None),
            P("section", None),
            P("section", None, seq),
            P("section", None, seq),
            P("section", None, seq),
            P("section", None, seq),
            P("section", seq),
            P("dp", seq, None, None),
        ),
        out_specs=(P("section", "dp", None, None, seq), P(), P(), P(), P()),
        check_vma=False,
    )
```

time: 668 us -> 563 us (0.84)
  blocking collectives: 567 us -> 86.5 us
  waiting for transfers between devices: 33.9 us -> 311 us
  starting transfers between devices: 11.6 us -> 106 us
  matrix products: 28.6 us -> 10.1 us
  loops' own time: 0.75 us -> 18 us
  local copies, waits for them, and re-layouts: 1.18 us -> 14.3 us
    ppermute x9 -> x14, waiting for transfers between devices: 33.9 us -> 311 us  [the longest x7 311 us: on_device(): current = lax.ppermute(result, 'section', [(tick, tick + 1)])]
    all_gather x19 -> x3, blocking collectives: 320 us -> 48.9 us  [the longest x1 19.2 us: attend(): gathered = lax.all_gather(current, 'y', axis=0, tiled=False)]
    psum x1 -> x3, blocking collectives: 247 us -> 37.6 us  [the longest x1 20.7 us: gradients_of(): return lax.psum(packed, 'y')]
    ppermute x9 -> x14, starting transfers between devices: 11.6 us -> 106 us  [the longest x7 101 us: swapped(): return lax.ppermute(value, 'core', [(0, 1), (1, 0)])]
    another operation x1 -> x10, loops' own time: 0.75 us -> 18 us  [the longest x8 16 us: on_device(): lax.cond(section == tick, lambda now, was: attend(now), lambda now, was:...]
    sub x9 -> x2, matrix products: 16 us -> 2.14 us  [one_head(): raised = jnp.exp(scores - jnp.max(scores, axis=-1, keepdims=True))]
    unnamed x24 -> x66, local copies, waits for them, and re-layouts: 0.69 us -> 8.53 us
  transfers between devices with their start and end apart: 9 -> 14, of which waited for: 9 -> 1; matrix products, arithmetic and copies ran while one was open for 0% -> 2% of each run, Pallas kernels for 0% -> 0%
where the time goes in v1:
time: 563 us; the launch traced here: 556 us
  waiting for transfers between devices  311 us (55%)
  starting transfers between devices  106 us (19%)
  blocking collectives  86.5 us (15%)
  loops' own time  18 us (3%)
  local copies, waits for them, and re-layouts  14.3 us (3%)
  matrix products  10.1 us (2%)
  other arithmetic  7.56 us (1%)
    ppermute x7, waiting for transfers between devices, on_device(): current = lax.ppermute(result, 'section', [(tick, tick + 1)])  311 us
    ppermute x7, starting transfers between devices, swapped(): return lax.ppermute(value, 'core', [(0, 1), (1, 0)])  101 us
    psum x1, blocking collectives, gradients_of(): return lax.psum(packed, 'y')  20.7 us
    all_gather x1, blocking collectives, attend(): gathered = lax.all_gather(current, 'y', axis=0, tiled=False)  19.2 us
    all_gather x1, blocking collectives, on_device(): waves = lax.all_gather(wave[0], ('y', 'core'), axis=0, tiled=True)  17.3 us
    another operation x8, loops' own time, on_device(): lax.cond(section == tick, lambda now, was: attend(now), lambda now, was:...  16 us
    psum x1, blocking collectives, gradients_of(): packed = lax.psum(packed, 'dp')  13.3 us
    all_gather x1, blocking collectives, attend(): mixed = lax.all_gather(in_order(mine, others), 'y', axis=0, tiled=False)  12.5 us
  transfers between devices with their start and end apart: 14, of which 1 were waited for; matrix products, arithmetic and copies ran while one was open for 2% of the time, Pallas kernels for 0%

profile of v1, /device:TPU:449, one launch (start us, length us, event | category | flops | bytes accessed | tf_op | source)
XLA Modules:
  0.0 555.6 jit_solution(13144620908168407991)
XLA Ops:
  0.6 0.7 copy-done.47
  1.3 0.7 pad_maximum_fusion
  2.0 2.6 collective-permute-start.1
  4.6 1.9 collective-permute-start.2
  6.5 2.4 collective-permute-start.3
  8.9 1.9 collective-permute-start.4
  10.9 2.4 collective-permute-start.5
  13.3 0.6 copy-done.69
  14.0 0.7 copy-done.67
  15.5 17.3 %all-gather.8 = bf16[16,1,40]{2,1,0:T(2,128)(2,1)S(1)} all-gather(bf16[1,1,40]{2,1,0:T(2,128)(2,1)S(1)} %copy-done.71), channel_id=10, replica_groups=mesh['section'=8,'y'=8,'core'=2,'dp'=4] {'y','core'}, dimensions={0}, use_global_device_ids=true | all-gather | bytes 1360 | tf_op jit(solution)/shard_map/all_gather | solution.py:112
  33.2 0.6 copy-done.46
  35.1 2.1 collective-permute-start
  37.4 43.5 %conditional.10 = (f32[16,512]{1,0:T(8,128)S(1)}) conditional(s32[]{:T(128)} %convert_element_type.524, () %tuple.70, (s32[]{:T(128)}, s32[1,16]{1,0:T(1,128)S(1)}, bf16[1,1,40]{2,1,0:T(2,128)(2,1)S(1)}, bf16[512,10]{0,1:T(8,128)(2,1)S(1)}, f32[512]{0:T(512)S(1)}, /*index=5*/f32[512]{0:T(512)S(1)}, f32[512]{0:T(512)S(1)}, ...), branch_computations={%region_6.7_spmd, %region_7.18_spmd} | conditional | flops 1064621 | bytes 458474 | solution.py:186
  38.5 0.7 reduce.76
  39.2 0.6 fusion.227
  43.2 3.5 psum.36
  46.8 13.3 %psum.37 = f32[16,512]{1,0:T(8,128)S(1)} all-reduce(f32[16,512]{1,0:T(8,128)S(1)} %psum.36), channel_id=1, replica_groups=mesh['section'=8,'y'=8,'core'=2,'dp'=4] {'dp'}, use_global_device_ids=true, to_apply=%region_16.16 | all-reduce | flops 8192 | bytes 65536 | tf_op jit(solution)/shard_map/cond/branch_1_fun/psum | solution.py:182
  60.1 20.7 %psum.38 = f32[16,512]{1,0:T(8,128)S(1)} all-reduce(f32[16,512]{1,0:T(8,128)S(1)} %psum.37), channel_id=1, replica_groups=mesh['section'=8,'y'=8,'core'=2,'dp'=4] {'y'}, use_global_device_ids=true, to_apply=%region_17.17 | all-reduce | flops 8192 | bytes 65536 | tf_op jit(solution)/shard_map/cond/branch_1_fun/psum | solution.py:183
  80.9 1.2 fusion.263
  83.0 0.7 collective-permute-start.6
  83.7 0.7 copy-done.76
  84.4 7.9 %conditional.12 = (bf16[2,64,256]{2,1,0:T(8,128)(2,1)S(1)}) conditional(s32[]{:T(128)} %convert_element_type.512, bf16[2,64,256]{2,1,0:T(8,128)(2,1)S(1)} %get-tuple-element.538, (bf16[2,64,256]{2,1,0:T(8,128)(2,1)S(1)}, s32[]{:T(128)}, s32[8]{0:T(128)S(1)}, f32[1,4096]{1,0:T(1,128)S(1)}, f32[1,4096]{1,0:T(1,128)S(1)}, ...), branch_computations={%region_26.27_spmd, %region_27.34_spmd} | conditional | flops 540742784 | bytes 35114676 | solution.py:193
  92.3 0.7 collective-permute-start.7
  93.0 0.7 copy-done.77
  93.6 0.7 collective-permute-start.8
  94.3 0.7 copy-done.78
  95.0 0.7 collective-permute-start.9
  95.6 0.7 copy-done.79
  96.3 7.6 %conditional.15 = (bf16[2,64,256]{2,1,0:T(8,128)(2,1)S(1)}) conditional(s32[]{:T(128)} %convert_element_type.509, bf16[2,64,256]{2,1,0:T(8,128)(2,1)S(1)} %get-tuple-element.541, (bf16[2,64,256]{2,1,0:T(8,128)(2,1)S(1)}, s32[]{:T(128)}, s32[8]{0:T(128)S(1)}, f32[1,4096]{1,0:T(1,128)S(1)}, f32[1,4096]{1,0:T(1,128)S(1)}, ...), branch_computations={%region_50.51_spmd, %region_51.58_spmd} | conditional | flops 540742784 | bytes 35114676 | solution.py:193
  103.9 0.7 collective-permute-start.10
  104.6 0.7 copy-done.80
  105.3 0.7 collective-permute-start.11
  106.0 0.7 copy-done.81
  106.6 1.3 collective-permute-start.12
  108.0 311.3 %collective-permute-done.12 = bf16[2,64,256]{2,1,0:T(8,128)(2,1)S(1)} collective-permute-done((bf16[2,64,256]{2,1,0:T(8,128)(2,1)S(1)}, bf16[2,64,256]{2,1,0:T(8,128)(2,1)S(1)}, u32[]{:S(2)}, u32[]{:S(2)}) %collective-permute-start.12) | collective-permute-done | bytes 65568 | tf_op jit(solution)/shard_map/ppermute | solution.py:195
  419.3 45.8 %conditional.18 = (bf16[2,64,256]{2,1,0:T(8,128)(2,1)S(1)}) conditional(s32[]{:T(128)} %convert_element_type.506, bf16[2,64,256]{2,1,0:T(8,128)(2,1)S(1)} %get-tuple-element.544, (bf16[2,64,256]{2,1,0:T(8,128)(2,1)S(1)}, s32[]{:T(128)}, s32[8]{0:T(128)S(1)}, f32[1,4096]{1,0:T(1,128)S(1)}, f32[1,4096]{1,0:T(1,128)S(1)}, ...), branch_computations={%region_74.75_spmd, %region_75.82_spmd} | conditional | flops 540742784 | bytes 30391848 | solution.py:193
  419.3 19.2 %all-gather.7 = bf16[16,64,256]{2,1,0:T(8,128)(2,1)S(1)} all-gather(bf16[2,64,256]{2,1,0:T(8,128)(2,1)S(1)} %get-tuple-element.424), channel_id=9, replica_groups=mesh['section'=8,'y'=8,'core'=2,'dp'=4] {'y'}, dimensions={0}, use_global_device_ids=true | all-gather | bytes 589824 | tf_op jit(solution)/shard_map/cond/branch_1_fun/all_gather | solution.py:148
  439.0 0.8 copy.240
  439.8 1.8 reshape.1661
  441.6 1.5 add_convert_fusion.7
  444.0 0.7 copy-done.9
  445.1 1.5 fusion.194
  446.6 1.7 fusion.315
  448.3 1.6 fusion.197
  450.2 12.5 %all_gather.81 = bf16[8,2,64,128]{3,1,0,2:T(2,128)(2,1)S(1)} all-gather(bf16[1,2,64,128]{3,1,0,2:T(2,128)(2,1)S(1)} %broadcast_select_fusion.7), channel_id=1, replica_groups=mesh['section'=8,'y'=8,'core'=2,'dp'=4] {'y'}, dimensions={0}, use_global_device_ids=true | all-gather | bytes 294912 | tf_op jit(solution)/shard_map/cond/branch_1_fun/all_gather | solution.py:157
  462.9 1.5 fusion.184
  465.8 87.4 %collective-permute-start.13 = (bf16[64,256]{1,0:T(8,128)(2,1)S(1)}, bf16[64,256]{1,0:T(8,128)(2,1)S(1)}, u32[]{:S(2)}, u32[]{:S(2)}) collective-permute-start(bf16[64,256]{1,0:T(8,128)(2,1)S(1)} %get-tuple-element.531), channel_id=1, source_target_pairs={{0,4},{4,0},{1,5},{5,1},{2,6},{6,2},{3,7},{7,3},{8,12},{12,8},{9,1... | collective-permute-start | bytes 98312 | tf_op jit(solution)/shard_map/ppermute | solution.py:107
  554.4 0.6 maximum_select_fusion.9
  (137 shorter events, 10.5 us)
Async XLA Ops:
  0.6 0.7 copy-start.47
  2.0 33.1 %collective-permute-start.1 = (f32[2,256]{1,0:T(2,128)S(1)}, f32[2,256]{1,0:T(2,128)S(1)}, u32[]{:S(2)}, u32[]{:S(2)}) collective-permute-start(f32[2,256]{1,0:T(2,128)S(1)} %pad_maximum_fusion), channel_id=1, source_target_pairs={{0,4},{4,0},{1,5},{5,1},{2,6},{6,2},{3,7},{7,3},{8,12},{12,8},{9,1... | collective-permute-start | bytes 6152 | tf_op jit(solution)/shard_map/ppermute | solution.py:107
  4.6 77.7 %collective-permute-start.2 = (bf16[4096,128]{1,0:T(8,128)(2,1)}, bf16[4096,128]{1,0:T(8,128)(2,1)}, u32[]{:S(2)}, u32[]{:S(2)}) collective-permute-start(bf16[4096,128]{1,0:T(8,128)(2,1)} %bitcast.560), channel_id=1, source_target_pairs={{0,4},{4,0},{1,5},{5,1},{2,6},{6,2},{3,7},{7,3},{8,12},{12,8},{9,1... | collective-permute-start | bytes 3145736 | tf_op jit(solution)/shard_map/ppermute | solution.py:107
  6.5 75.8 %collective-permute-start.3 = (bf16[4096,128]{1,0:T(8,128)(2,1)}, bf16[4096,128]{1,0:T(8,128)(2,1)}, u32[]{:S(2)}, u32[]{:S(2)}) collective-permute-start(bf16[4096,128]{1,0:T(8,128)(2,1)} %bitcast.569), channel_id=1, source_target_pairs={{0,4},{4,0},{1,5},{5,1},{2,6},{6,2},{3,7},{7,3},{8,12},{12,8},{9,1... | collective-permute-start | bytes 3145736 | tf_op jit(solution)/shard_map/ppermute | solution.py:107
  8.9 73.4 %collective-permute-start.4 = (bf16[4096,128]{1,0:T(8,128)(2,1)}, bf16[4096,128]{1,0:T(8,128)(2,1)}, u32[]{:S(2)}, u32[]{:S(2)}) collective-permute-start(bf16[4096,128]{1,0:T(8,128)(2,1)} %bitcast.578), channel_id=1, source_target_pairs={{0,4},{4,0},{1,5},{5,1},{2,6},{6,2},{3,7},{7,3},{8,12},{12,8},{9,1... | collective-permute-start | bytes 3145736 | tf_op jit(solution)/shard_map/ppermute | solution.py:107
  10.9 71.5 %collective-permute-start.5 = (bf16[2048,256]{1,0:T(8,128)(2,1)}, bf16[2048,256]{1,0:T(8,128)(2,1)}, u32[]{:S(2)}, u32[]{:S(2)}) collective-permute-start(bf16[2048,256]{1,0:T(8,128)(2,1)} %bitcast.587), channel_id=1, source_target_pairs={{0,4},{4,0},{1,5},{5,1},{2,6},{6,2},{3,7},{7,3},{8,12},{12,8},{9,1... | collective-permute-start | bytes 3145736 | tf_op jit(solution)/shard_map/ppermute | solution.py:107
  13.3 0.7 copy-start.69
  14.9 0.7 copy-start.71
  33.0 50.0 %copy-start.75 = (s32[8]{0:T(128)}, s32[8]{0:T(128)S(1)}, u32[]{:S(2)}) copy-start(s32[8]{0:T(128)S(1)} %fusion.290) | copy-start | bytes 100
  33.1 0.7 copy-start.46
  33.1 0.7 copy-start.63
  33.1 1.3 copy-start.56
  33.1 1.3 copy-start.65
  33.1 4.2 copy-start.61
  33.8 47.0 %copy-start.70 = (f32[256]{0:T(256)S(1)}, f32[256]{0:T(256)}, u32[]{:S(2)}) copy-start(f32[256]{0:T(256)} %param.49) | copy-start | bytes 3076
  33.8 47.0 %copy-start.73 = (f32[512]{0:T(512)S(1)}, f32[512]{0:T(512)}, u32[]{:S(2)}) copy-start(f32[512]{0:T(512)} %param.47) | copy-start | bytes 6148
  33.8 47.0 %copy-start.74 = (f32[512]{0:T(512)S(1)}, f32[512]{0:T(512)}, u32[]{:S(2)}) copy-start(f32[512]{0:T(512)} %param.46) | copy-start | bytes 6148
  33.8 48.5 %copy-start.1 = (bf16[1,4096,128]{2,1,0:T(8,128)(2,1)S(1)}, bf16[1,4096,128]{2,1,0:T(8,128)(2,1)}, u32[]{:S(2)}) copy-start(bf16[1,4096,128]{2,1,0:T(8,128)(2,1)} %param.53) | copy-start | bytes 3145732
  34.1 48.2 %copy-start = (bf16[1,4096,128]{2,1,0:T(8,128)(2,1)S(1)}, bf16[1,4096,128]{2,1,0:T(8,128)(2,1)}, u32[]{:S(2)}) copy-start(bf16[1,4096,128]{2,1,0:T(8,128)(2,1)} %param.52) | copy-start | bytes 3145732
  35.1 47.9 %copy-start.58 = (f32[2,256]{1,0:T(2,128)}, f32[2,256]{1,0:T(2,128)S(1)}, u32[]{:S(2)}) copy-start(f32[2,256]{1,0:T(2,128)S(1)} %collective-permute-done.1) | copy-start | bytes 6148
  35.1 46.9 %collective-permute-start = (bf16[512,256]{1,0:T(8,128)(2,1)}, bf16[512,256]{1,0:T(8,128)(2,1)S(1)}, u32[]{:S(2)}, u32[]{:S(2)}) collective-permute-start(bf16[512,256]{1,0:T(8,128)(2,1)} %param.48), channel_id=1, source_target_pairs={{0,4},{4,0},{1,5},{5,1},{2,6},{6,2},{3,7},{7,3},{8,12},{12,8},{9,1... | collective-permute-start | bytes 786440 | tf_op jit(solution)/shard_map/ppermute | solution.py:107
  82.3 0.7 copy-start.32
  82.3 0.7 copy-start.33
  83.0 0.7 collective-permute-start.6
  83.7 0.7 copy-start.76
  92.3 0.7 collective-permute-start.7
  92.9 0.7 copy-start.77
  93.6 0.7 collective-permute-start.8
  94.3 0.7 copy-start.78
  95.0 0.7 collective-permute-start.9
  95.6 0.7 copy-start.79
  103.9 0.7 collective-permute-start.10
  104.6 0.7 copy-start.80
  105.3 0.7 collective-permute-start.11
  105.9 0.7 copy-start.81
  106.6 312.7 %collective-permute-start.12 = (bf16[2,64,256]{2,1,0:T(8,128)(2,1)S(1)}, bf16[2,64,256]{2,1,0:T(8,128)(2,1)S(1)}, u32[]{:S(2)}, u32[]{:S(2)}) collective-permute-start(bf16[2,64,256]{2,1,0:T(8,128)(2,1)S(1)} %get-tuple-element.544), channel_id=1, source_target_pairs={{384,448},{385,449},{386,450},{387,451},{388,452},{389,453},{390,4... | collective-permute-start | bytes 196616 | tf_op jit(solution)/shard_map/ppermute | solution.py:195
  107.9 311.4 %copy-start.59 = (f32[2,256]{1,0:T(2,128)S(1)}, f32[2,256]{1,0:T(2,128)}, u32[]{:S(2)}) copy-start(f32[2,256]{1,0:T(2,128)} %copy-done.58) | copy-start | bytes 6148
  107.9 311.4 %copy-start.48 = (f32[1,256]{1,0:T(1,128)S(1)}, f32[1,256]{1,0:T(1,128)}, u32[]{:S(2)}) copy-start(f32[1,256]{1,0:T(1,128)} %param.56) | copy-start | bytes 3076
  107.9 311.4 %copy-start.82 = (s32[8]{0:T(128)S(1)}, s32[8]{0:T(128)}, u32[]{:S(2)}) copy-start(s32[8]{0:T(128)} %copy-done.75) | copy-start | bytes 100
  443.4 1.2 copy-start.9
  450.2 14.2 %copy-start.17 = (bf16[2048,256]{1,0:T(8,128)(2,1)S(1)}, bf16[2048,256]{1,0:T(8,128)(2,1)}, u32[]{:S(2)}) copy-start(bf16[2048,256]{1,0:T(8,128)(2,1)} %get-tuple-element.435) | copy-start | bytes 3145732 | tf_op jit(solution)/shard_map/cond
  465.1 0.7 copy-start.57
  465.1 0.7 copy-start.62
  465.1 0.7 copy-start.64
  465.1 0.7 copy-start.66
  465.1 0.7 copy-start.68
  465.2 0.7 copy-start.72
  465.8 88.6 %collective-permute-start.13 = (bf16[64,256]{1,0:T(8,128)(2,1)S(1)}, bf16[64,256]{1,0:T(8,128)(2,1)S(1)}, u32[]{:S(2)}, u32[]{:S(2)}) collective-permute-start(bf16[64,256]{1,0:T(8,128)(2,1)S(1)} %get-tuple-element.531), channel_id=1, source_target_pairs={{0,4},{4,0},{1,5},{5,1},{2,6},{6,2},{3,7},{7,3},{8,12},{12,8},{9,1... | collective-permute-start | bytes 98312 | tf_op jit(solution)/shard_map/ppermute | solution.py:107
  (1 other events, 0.7 us)

commit v2 on v1

v2 whole, which is shorter than its diff:
```python
import functools

import jax
import jax.numpy as jnp
from jax import lax
from jax.experimental import pallas as pl
from jax.experimental.pallas import tpu as pltpu
from jax.sharding import Mesh, PartitionSpec as P

HEAD_DIM = 128
KERNEL = 10
STRIDE = 5
MICRO = 2
CORES = 2
LANES = 128


def layer_norm(values, gain, shift):
    average = jnp.mean(values, axis=-1, keepdims=True)
    centered = values - average
    spread = jnp.mean(centered * centered, axis=-1, keepdims=True)
    return centered * lax.rsqrt(spread + 1e-05) * gain + shift


def frame_counts(lengths):
    return (lengths - KERNEL) // STRIDE + 1


def framed_of(wave, lengths):
    owners, samples = wave.shape
    positions = lax.broadcasted_iota(jnp.int32, wave.shape, 1)
    cleaned = jnp.where(positions < lengths[:, None], wave, jnp.zeros_like(wave))
    blocks = cleaned.reshape(owners, samples // STRIDE, STRIDE)
    after = jnp.concatenate([blocks[:, 1:], jnp.zeros_like(blocks[:, :1])], axis=1)
    return jnp.concatenate([blocks, after], axis=2)


def live_of(lengths, frame_total):
    counts = frame_counts(lengths)
    return lax.broadcasted_iota(jnp.int32, (lengths.shape[0], frame_total), 1) < counts[:, None]


def frontend(weight, bias, gain, shift, framed, live):
    convolved = (
        jnp.einsum("...fk,ck->...fc", framed, weight, precision=lax.Precision.HIGHEST) + bias
    )
    active = jax.nn.gelu(layer_norm(convolved, gain, shift), approximate=False)
    return jnp.where(live[..., None], active, jnp.zeros_like(active))


def product(left, right):
    return jnp.dot(left, right, preferred_element_type=jnp.float32)


def mixing_kernel(chips, place, *refs):
    blocks = refs[:chips]
    gain, shift, weights_mine, weights_other, masking, out, held, sems = refs[chips:]
    chip, core = place[0], place[1]
    order = [lax.rem(chip - j + chips, chips) for j in range(chips)]
    copies = []
    for j in range(chips):
        for side, weights in enumerate((weights_mine, weights_other)):
            copy = pltpu.make_async_copy(
                weights.at[order[j], 0:3], held.at[j, side], sems.at[j, side]
            )
            copy.start()
            copies.append(copy)
    rows, width = blocks[0].shape
    total = sum(jnp.sum(b[...].astype(jnp.float32), axis=-1, keepdims=True) for b in blocks)
    average = total / (chips * width)
    spread = jnp.zeros_like(average)
    for b in blocks:
        centered = b[...].astype(jnp.float32) - average
        spread += jnp.sum(centered * centered, axis=-1, keepdims=True)
    scale = lax.rsqrt(spread / (chips * width) + 1e-05)
    sums = [jnp.zeros((rows, 2 * HEAD_DIM), jnp.float32) for _ in range(3)]
    for j in range(chips):
        centered = blocks[j][...].astype(jnp.float32) - average
        normed = (centered * scale * gain[order[j]] + shift[order[j]]).astype(jnp.bfloat16)
        copies[2 * j].wait()
        copies[2 * j + 1].wait()
        for i in range(3):
            both = jnp.concatenate([held[j, 0, i], held[j, 1, i]], axis=1)
            sums[i] += product(normed, both)
    queries = (sums[0] * HEAD_DIM ** (-0.5)).astype(jnp.bfloat16)
    key_rows = sums[1].astype(jnp.bfloat16)
    value_rows = sums[2].astype(jnp.bfloat16)
    for side in range(2):
        own = slice(side * HEAD_DIM, (side + 1) * HEAD_DIM)
        scores = lax.dot_general(
            queries[:, own],
            key_rows[:, own],
            (((1,), (1,)), ((), ())),
            preferred_element_type=jnp.float32,
        )
        scores = jnp.where(masking[...] > 0, scores, -jnp.inf)
        raised = jnp.exp(scores - jnp.max(scores, axis=-1, keepdims=True))
        attention = (raised / jnp.sum(raised, axis=-1, keepdims=True)).astype(jnp.bfloat16)
        mixture = product(attention, value_rows[:, own]).astype(jnp.bfloat16)
        lane = pl.multiple_of((core if side == 0 else 1 - core) * HEAD_DIM, HEAD_DIM)
        out[:, pl.ds(lane, HEAD_DIM)] = mixture


def leaving_kernel(chips, place, mixed, current, weights_mine, weights_other, bias, out, held, sems):
    core = place[1]
    copies = []
    for side, weights in enumerate((weights_mine, weights_other)):
        for i in range(chips):
            copy = pltpu.make_async_copy(weights.at[i, 3], held.at[side, i], sems.at[side, i])
            copy.start()
            copies.append(copy)
    depth = mixed.shape[2]
    columns = 2 * LANES
    for side in range(2):
        total = jnp.zeros((mixed.shape[1], columns), jnp.float32)
        for i in range(chips):
            copies[side * chips + i].wait()
            both = jnp.concatenate([held[side, i, :depth], held[side, i, depth:]], axis=1)
            total += product(mixed[i], both)
        lane = pl.multiple_of((core if side == 0 else 1 - core) * columns, columns)
        mine = pl.ds(lane, columns)
        out[:, mine] = (current[:, mine].astype(jnp.float32) + total + bias[:, mine]).astype(
            jnp.bfloat16
        )


def on_device(
    wave,
    lengths,
    assign,
    conv_weight,
    conv_bias,
    conv_gain,
    conv_shift,
    feat_gain,
    feat_shift,
    proj_weight,
    proj_bias,
    norm_gain,
    norm_shift,
    query_weight,
    key_weight,
    value_weight,
    out_weight,
    out_bias,
    feat_grad,
):
    section, chip, core = (lax.axis_index(name) for name in ("section", "y", "core"))
    sections, chips = lax.axis_size("section"), lax.axis_size("y")
    samples = wave.shape[2]
    frame_total = samples // STRIDE
    batch_size = lengths.shape[1]
    utts = batch_size // MICRO
    rows = utts * frame_total
    width = query_weight.shape[1] // chips
    columns = proj_weight.shape[1]
    vmem, smem, anywhere = (
        pl.BlockSpec(memory_space=space) for space in (pltpu.VMEM, pltpu.SMEM, pl.ANY)
    )

    def swapped(value):
        return lax.ppermute(value, "core", [(0, 1), (1, 0)])

    depth = out_weight.shape[1] // chips
    halves = out_weight[0].reshape(chips, depth, 2, LANES).transpose(0, 2, 1, 3)
    weights_mine = jnp.stack(
        [
            query_weight[0].reshape(chips, width, HEAD_DIM),
            key_weight[0].reshape(chips, width, HEAD_DIM),
            value_weight[0].reshape(chips, width, HEAD_DIM),
            halves.reshape(chips, width, LANES),
        ],
        axis=1,
    )
    weights_other = swapped(weights_mine)
    proj_other = swapped(proj_weight)

    small = jnp.concatenate([wave[0].astype(jnp.float32), proj_bias[None], out_bias], axis=1)
    small = lax.all_gather(small, ("y", "core"), axis=0, tiled=True)
    waves = small[:, :samples]
    pair = lax.dynamic_slice_in_dim(small, chip * CORES, CORES, 0)
    proj_bias_pair = pair[:, samples : samples + columns].reshape(1, CORES * columns)
    out_bias_pair = pair[:, samples + columns :].reshape(1, CORES * columns)

    slots = core * utts + lax.broadcasted_iota(jnp.int32, (batch_size, utts), 1)
    chosen = assign[0][:, None] == slots
    slot_lengths = jnp.sum(jnp.where(chosen, lengths[0][:, None], 0), axis=0)
    slot_waves = jnp.sum(jnp.where(chosen[:, :, None], waves[:, None], 0.0), axis=0)
    framed = framed_of(slot_waves.astype(jnp.bfloat16), slot_lengths)
    convolved = (
        jnp.einsum("ufk,ck->ufc", framed, conv_weight, preferred_element_type=jnp.float32)
        + conv_bias
    )
    active = jax.nn.gelu(layer_norm(convolved, conv_gain, conv_shift), approximate=False)
    live = live_of(slot_lengths, frame_total)
    frames = jnp.where(live[..., None], active, 0.0).astype(jnp.bfloat16)
    frames = frames.reshape(rows, frames.shape[2])
    normed_frames = layer_norm(frames.astype(jnp.float32), feat_gain, feat_shift).astype(
        jnp.bfloat16
    )
    proj_mine, proj_theirs = product(normed_frames, proj_weight), product(normed_frames, proj_other)
    entering = (
        jnp.where(
            core == 0,
            jnp.concatenate([proj_mine, proj_theirs], axis=1),
            jnp.concatenate([proj_theirs, proj_mine], axis=1),
        )
        + proj_bias_pair
    ).astype(jnp.bfloat16)

    owner = lax.broadcasted_iota(jnp.int32, (rows, rows), 0) // frame_total
    column = lax.broadcasted_iota(jnp.int32, (rows, rows), 1)
    live_keys = live.reshape(1, rows)
    masking = jnp.where((owner == column // frame_total) & live_keys, 1.0, 0.0)
    place = jnp.stack([chip, core]).astype(jnp.int32)
    gain = norm_gain.reshape(chips, 1, width)
    shift = norm_shift.reshape(chips, 1, width)

    def spread_out(block, pairs_of):
        return tuple(
            lax.ppermute(
                block,
                ("section", "y"),
                [
                    (source * chips + y, target * chips + (y + j) % chips)
                    for source, target in pairs_of
                    for y in range(chips)
                ],
            )
            for j in range(chips)
        )

    mixing = pl.pallas_call(
        functools.partial(mixing_kernel, chips),
        out_shape=jax.ShapeDtypeStruct((rows, 2 * HEAD_DIM), jnp.bfloat16),
        in_specs=[smem] + [vmem] * (chips + 2) + [anywhere] * 2 + [vmem],
        out_specs=vmem,
        scratch_shapes=[
            pltpu.VMEM((chips, 2, 3, width, HEAD_DIM), jnp.bfloat16),
            pltpu.SemaphoreType.DMA((chips, 2)),
        ],
        compiler_params=pltpu.CompilerParams(vmem_limit_bytes=24 * 2**20),
    )
    leaving = pl.pallas_call(
        functools.partial(leaving_kernel, chips),
        out_shape=jax.ShapeDtypeStruct((rows, CORES * columns), jnp.bfloat16),
        in_specs=[smem, vmem, vmem, anywhere, anywhere, vmem],
        out_specs=vmem,
        scratch_shapes=[
            pltpu.VMEM((2, chips, width, LANES), jnp.bfloat16),
            pltpu.SemaphoreType.DMA((2, chips)),
        ],
        compiler_params=pltpu.CompilerParams(vmem_limit_bytes=24 * 2**20),
    )

    def attend(received, _):
        mixture = mixing(place, *received, gain, shift, weights_mine, weights_other, masking)
        mixed = lax.all_gather(mixture, "y", axis=0, tiled=False)
        return leaving(place, mixed, received[0], weights_mine, weights_other, out_bias_pair)

    def gradients_of():
        own_lengths = lax.dynamic_slice_in_dim(lengths[0], chip * CORES + core, 1, 0)
        own_framed = framed_of(wave[0], own_lengths).astype(jnp.float32)
        own_live = live_of(own_lengths, frame_total)

        def frontend_at(weight, bias, gain, shift):
            return frontend(weight, bias, gain, shift, own_framed, own_live)

        _, pullback = jax.vjp(
            frontend_at, conv_weight.astype(jnp.float32), conv_bias, conv_gain, conv_shift
        )
        partial = pullback(feat_grad[0].astype(jnp.float32))
        packed = jnp.concatenate(
            [partial[0].T, partial[1][None], partial[2][None], partial[3][None]], axis=0
        )
        packed = jnp.pad(packed, ((0, 16 - packed.shape[0]), (0, 0)))
        return lax.psum(lax.psum(lax.psum(packed, "core"), "dp"), "y")

    late = section >= sections // 2
    packed = lax.cond(
        late, gradients_of, lambda: jnp.zeros((16, conv_bias.shape[0]), jnp.float32)
    )
    entering, packed = lax.optimization_barrier((entering, packed))

    received = spread_out(entering, [(0, 0)])
    result = entering
    for tick in range(sections):
        result = lax.cond(section == tick, attend, lambda now, was: was, received, result)
        if tick < sections - 1:
            received = spread_out(result, [(tick, tick + 1)])

    result, packed = lax.optimization_barrier((result, packed))
    packed = lax.cond(late, lambda: packed, gradients_of)
    mine = lax.dynamic_slice_in_dim(result, core * columns, columns, 1)
    others = swapped(lax.dynamic_slice_in_dim(result, (1 - core) * columns, columns, 1))
    section_out = jnp.where(core == 0, jnp.stack([mine, others]), jnp.stack([others, mine]))
    return (
        section_out[None, None],
        packed[:KERNEL].T,
        packed[KERNEL],
        packed[KERNEL + 1],
        packed[KERNEL + 2],
    )


def solution(mesh):
    sizes = dict(mesh.shape)
    split = Mesh(
        mesh.devices.reshape(
            sizes["section"], sizes["seq"] // CORES, CORES, sizes["dp"]
        ),
        ("section", "y", "core", "dp"),
    )
    seq = ("y", "core")
    return jax.shard_map(
        on_device,
        mesh=split,
        in_specs=(
            P("dp", seq, None),
            P("dp", None),
            P("dp", None),
            P(),
            P(),
            P(),
            P(),
            P(),
            P(),
            P(None, seq),
            P(seq),
            P("section", None),
            P("section", None),
            P("section", None, seq),
            P("section", None, seq),
            P("section", None, seq),
            P("section", None, seq),
            P("section", seq),
            P("dp", seq, None, None),
        ),
        out_specs=(P("section", "dp", None, None, seq), P(), P(), P(), P()),
        check_vma=False,
    )
```

time: 563 us -> 969 us (1.72)
  the two profiles are of different devices: /device:TPU:449 before, /device:TPU:64 now
where the time goes in v2:
time: 969 us; the launch traced here: 968 us
  starting transfers between devices  782 us (81%)
  blocking collectives  94.1 us (10%)
  waiting for transfers between devices  67.4 us (7%)
    ppermute x64, starting transfers between devices, spread_out(): lax.ppermute(block, ('section', 'y'), [(source * chips + y, target * chip...  759 us
    ppermute x64, waiting for transfers between devices, spread_out(): lax.ppermute(block, ('section', 'y'), [(source * chips + y, target * chip...  67.4 us
    psum x3, blocking collectives, gradients_of(): return lax.psum(lax.psum(lax.psum(packed, 'core'), 'dp'), 'y')  50.7 us
    all_gather x1, blocking collectives, attend(): mixed = lax.all_gather(mixture, 'y', axis=0, tiled=False)  25 us
    ppermute x3, starting transfers between devices, swapped(): return lax.ppermute(value, 'core', [(0, 1), (1, 0)])  22.3 us
  transfers between devices with their start and end apart: 67, of which 7 were waited for; matrix products, arithmetic and copies ran while one was open for 1% of the time, Pallas kernels for 0%

profile of v2, /device:TPU:64, one launch (start us, length us, event | category | flops | bytes accessed | tf_op | source)
XLA Modules:
  0.0 967.6 jit_solution(6260304223286431343)
XLA Ops:
  4.5 3.4 pad_maximum_fusion
  7.9 18.2 %collective-permute-start.9 = (bf16[8,4,512,128]{3,2,1,0:T(8,128)(2,1)}, bf16[8,4,512,128]{3,2,1,0:T(8,128)(2,1)}, u32[]{:S(2)}, u32[]{:S(2)}) collective-permute-start(bf16[8,4,512,128]{3,2,1,0:T(8,128)(2,1)} %pad_maximum_fusion), channel_id=1, source_target_pairs={{0,4},{4,0},{1,5},{5,1},{2,6},{6,2},{3,7},{7,3},{8,12},{12,8},{9,1... | collective-permute-start | bytes 12582920 | tf_op jit(solution)/shard_map/ppermute | solution.py:162
  26.3 18.4 %all-gather.8 = f32[16,1,552]{2,1,0:T(1,128)S(1)} all-gather(f32[1,1,552]{2,1,0:T(1,128)S(1)} %maximum_bitcast_fusion), channel_id=1, replica_groups=mesh['section'=8,'y'=8,'core'=2,'dp'=4] {'y','core'}, dimensions={0}, use_global_device_ids=true | all-gather | bytes 37536 | tf_op jit(solution)/shard_map/all_gather | solution.py:179
  59.6 56.5 %collective-permute-done.10 = bf16[64,512]{1,0:T(8,128)(2,1)S(1)} collective-permute-done((bf16[64,512]{1,0:T(8,128)(2,1)S(1)}, bf16[64,512]{1,0:T(8,128)(2,1)S(1)}, u32[]{:S(2)}, u32[]{:S(2)}) %collective-permute-start.10) | collective-permute-done | bytes 65568 | tf_op jit(solution)/shard_map/ppermute | solution.py:221
  120.9 4.4 collective-permute-done.14
  128.1 32.1 %conditional.12 = (bf16[64,512]{1,0:T(8,128)(2,1)S(1)}) conditional(s32[]{:T(128)} %convert_element_type.95, bf16[64,512]{1,0:T(8,128)(2,1)S(1)} %get-tuple-element.500, (s32[2]{0:T(128)S(1)}, bf16[64,512]{1,0:T(8,128)(2,1)S(1)}, bf16[64,512]{1,0:T(8,128)(2,1)S(1)}, bf16[64,512]{1,0:T(8,128)(2,1)S(1)}, bf16[64,512]{1,0:T(8,128)(2,1)S(1)}, ...), branch_computations={%region_20.21_spmd, %region_21.22_spmd} | conditional | bytes 294920 | solution.py:288
  128.1 4.4 branch_1_fun.18
  132.5 25.0 %all-gather.1 = bf16[512,256]{1,0:T(8,128)(2,1)S(1)} all-gather(bf16[64,256]{1,0:T(8,128)(2,1)S(1)} %branch_1_fun.18), channel_id=3, replica_groups=mesh['section'=8,'y'=8,'core'=2,'dp'=4] {'y'}, dimensions={0}, use_global_device_ids=true | all-gather | bytes 294912 | tf_op jit(solution)/shard_map/cond/branch_1_fun/all_gather | solution.py:258
  157.5 2.7 branch_1_fun.19
  166.8 3.1 collective-permute-start.23
  179.9 50.5 %collective-permute-start.32 = (bf16[64,512]{1,0:T(8,128)(2,1)S(1)}, bf16[64,512]{1,0:T(8,128)(2,1)S(1)}, u32[]{:S(2)}, u32[]{:S(2)}) collective-permute-start(bf16[64,512]{1,0:T(8,128)(2,1)S(1)} %get-tuple-element.502), channel_id=1, source_target_pairs={{128,240},{136,248},{144,192},{152,200},{160,208},{168,216},{176,2... | collective-permute-start | bytes 196616 | tf_op jit(solution)/shard_map/ppermute | solution.py:221
  230.4 16.1 %collective-permute-start.33 = (bf16[64,512]{1,0:T(8,128)(2,1)S(1)}, bf16[64,512]{1,0:T(8,128)(2,1)S(1)}, u32[]{:S(2)}, u32[]{:S(2)}) collective-permute-start(bf16[64,512]{1,0:T(8,128)(2,1)S(1)} %get-tuple-element.502), channel_id=1, source_target_pairs={{128,248},{136,192},{144,200},{152,208},{160,216},{168,224},{176,2... | collective-permute-start | bytes 196616 | tf_op jit(solution)/shard_map/ppermute | solution.py:221
  246.5 48.5 %collective-permute-start.34 = (bf16[64,512]{1,0:T(8,128)(2,1)S(1)}, bf16[64,512]{1,0:T(8,128)(2,1)S(1)}, u32[]{:S(2)}, u32[]{:S(2)}) collective-permute-start(bf16[64,512]{1,0:T(8,128)(2,1)S(1)} %get-tuple-element.503), channel_id=1, source_target_pairs={{192,256},{200,264},{208,272},{216,280},{224,288},{232,296},{240,3... | collective-permute-start | bytes 196616 | tf_op jit(solution)/shard_map/ppermute | solution.py:221
  295.1 16.1 %collective-permute-start.35 = (bf16[64,512]{1,0:T(8,128)(2,1)S(1)}, bf16[64,512]{1,0:T(8,128)(2,1)S(1)}, u32[]{:S(2)}, u32[]{:S(2)}) collective-permute-start(bf16[64,512]{1,0:T(8,128)(2,1)S(1)} %get-tuple-element.503), channel_id=1, source_target_pairs={{192,264},{200,272},{208,280},{216,288},{224,296},{232,304},{240,3... | collective-permute-start | bytes 196616 | tf_op jit(solution)/shard_map/ppermute | solution.py:221
  311.2 16.1 %collective-permute-start.36 = (bf16[64,512]{1,0:T(8,128)(2,1)S(1)}, bf16[64,512]{1,0:T(8,128)(2,1)S(1)}, u32[]{:S(2)}, u32[]{:S(2)}) collective-permute-start(bf16[64,512]{1,0:T(8,128)(2,1)S(1)} %get-tuple-element.503), channel_id=1, source_target_pairs={{192,272},{200,280},{208,288},{216,296},{224,304},{232,312},{240,2... | collective-permute-start | bytes 196616 | tf_op jit(solution)/shard_map/ppermute | solution.py:221
  327.2 16.1 %collective-permute-start.37 = (bf16[64,512]{1,0:T(8,128)(2,1)S(1)}, bf16[64,512]{1,0:T(8,128)(2,1)S(1)}, u32[]{:S(2)}, u32[]{:S(2)}) collective-permute-start(bf16[64,512]{1,0:T(8,128)(2,1)S(1)} %get-tuple-element.503), channel_id=1, source_target_pairs={{192,280},{200,288},{208,296},{216,304},{224,312},{232,256},{240,2... | collective-permute-start | bytes 196616 | tf_op jit(solution)/shard_map/ppermute | solution.py:221
  343.3 16.1 %collective-permute-start.38 = (bf16[64,512]{1,0:T(8,128)(2,1)S(1)}, bf16[64,512]{1,0:T(8,128)(2,1)S(1)}, u32[]{:S(2)}, u32[]{:S(2)}) collective-permute-start(bf16[64,512]{1,0:T(8,128)(2,1)S(1)} %get-tuple-element.503), channel_id=1, source_target_pairs={{192,288},{200,296},{208,304},{216,312},{224,256},{232,264},{240,2... | collective-permute-start | bytes 196616 | tf_op jit(solution)/shard_map/ppermute | solution.py:221
  359.4 16.1 %collective-permute-start.39 = (bf16[64,512]{1,0:T(8,128)(2,1)S(1)}, bf16[64,512]{1,0:T(8,128)(2,1)S(1)}, u32[]{:S(2)}, u32[]{:S(2)}) collective-permute-start(bf16[64,512]{1,0:T(8,128)(2,1)S(1)} %get-tuple-element.503), channel_id=1, source_target_pairs={{192,296},{200,304},{208,312},{216,256},{224,264},{232,272},{240,2... | collective-permute-start | bytes 196616 | tf_op jit(solution)/shard_map/ppermute | solution.py:221
  375.5 16.1 %collective-permute-start.40 = (bf16[64,512]{1,0:T(8,128)(2,1)S(1)}, bf16[64,512]{1,0:T(8,128)(2,1)S(1)}, u32[]{:S(2)}, u32[]{:S(2)}) collective-permute-start(bf16[64,512]{1,0:T(8,128)(2,1)S(1)} %get-tuple-element.503), channel_id=1, source_target_pairs={{192,304},{200,312},{208,256},{216,264},{224,272},{232,280},{240,2... | collective-permute-start | bytes 196616 | tf_op jit(solution)/shard_map/ppermute | solution.py:221
  391.6 16.1 %collective-permute-start.41 = (bf16[64,512]{1,0:T(8,128)(2,1)S(1)}, bf16[64,512]{1,0:T(8,128)(2,1)S(1)}, u32[]{:S(2)}, u32[]{:S(2)}) collective-permute-start(bf16[64,512]{1,0:T(8,128)(2,1)S(1)} %get-tuple-element.503), channel_id=1, source_target_pairs={{192,312},{200,256},{208,264},{216,272},{224,280},{232,288},{240,2... | collective-permute-start | bytes 196616 | tf_op jit(solution)/shard_map/ppermute | solution.py:221
  407.8 51.2 %collective-permute-start.42 = (bf16[64,512]{1,0:T(8,128)(2,1)S(1)}, bf16[64,512]{1,0:T(8,128)(2,1)S(1)}, u32[]{:S(2)}, u32[]{:S(2)}) collective-permute-start(bf16[64,512]{1,0:T(8,128)(2,1)S(1)} %get-tuple-element.504), channel_id=1, source_target_pairs={{256,320},{264,328},{272,336},{280,344},{288,352},{296,360},{304,3... | collective-permute-start | bytes 196616 | tf_op jit(solution)/shard_map/ppermute | solution.py:221
  458.9 16.7 %collective-permute-start.43 = (bf16[64,512]{1,0:T(8,128)(2,1)S(1)}, bf16[64,512]{1,0:T(8,128)(2,1)S(1)}, u32[]{:S(2)}, u32[]{:S(2)}) collective-permute-start(bf16[64,512]{1,0:T(8,128)(2,1)S(1)} %get-tuple-element.504), channel_id=1, source_target_pairs={{256,328},{264,336},{272,344},{280,352},{288,360},{296,368},{304,3... | collective-permute-start | bytes 196616 | tf_op jit(solution)/shard_map/ppermute | solution.py:221
  475.7 16.7 %collective-permute-start.44 = (bf16[64,512]{1,0:T(8,128)(2,1)S(1)}, bf16[64,512]{1,0:T(8,128)(2,1)S(1)}, u32[]{:S(2)}, u32[]{:S(2)}) collective-permute-start(bf16[64,512]{1,0:T(8,128)(2,1)S(1)} %get-tuple-element.504), channel_id=1, source_target_pairs={{256,336},{264,344},{272,352},{280,360},{288,368},{296,376},{304,3... | collective-permute-start | bytes 196616 | tf_op jit(solution)/shard_map/ppermute | solution.py:221
  492.4 16.7 %collective-permute-start.45 = (bf16[64,512]{1,0:T(8,128)(2,1)S(1)}, bf16[64,512]{1,0:T(8,128)(2,1)S(1)}, u32[]{:S(2)}, u32[]{:S(2)}) collective-permute-start(bf16[64,512]{1,0:T(8,128)(2,1)S(1)} %get-tuple-element.504), channel_id=1, source_target_pairs={{256,344},{264,352},{272,360},{280,368},{288,376},{296,320},{304,3... | collective-permute-start | bytes 196616 | tf_op jit(solution)/shard_map/ppermute | solution.py:221
  509.2 16.7 %collective-permute-start.46 = (bf16[64,512]{1,0:T(8,128)(2,1)S(1)}, bf16[64,512]{1,0:T(8,128)(2,1)S(1)}, u32[]{:S(2)}, u32[]{:S(2)}) collective-permute-start(bf16[64,512]{1,0:T(8,128)(2,1)S(1)} %get-tuple-element.504), channel_id=1, source_target_pairs={{256,352},{264,360},{272,368},{280,376},{288,320},{296,328},{304,3... | collective-permute-start | bytes 196616 | tf_op jit(solution)/shard_map/ppermute | solution.py:221
  525.9 16.7 %collective-permute-start.47 = (bf16[64,512]{1,0:T(8,128)(2,1)S(1)}, bf16[64,512]{1,0:T(8,128)(2,1)S(1)}, u32[]{:S(2)}, u32[]{:S(2)}) collective-permute-start(bf16[64,512]{1,0:T(8,128)(2,1)S(1)} %get-tuple-element.504), channel_id=1, source_target_pairs={{256,360},{264,368},{272,376},{280,320},{288,328},{296,336},{304,3... | collective-permute-start | bytes 196616 | tf_op jit(solution)/shard_map/ppermute | solution.py:221
  542.7 16.7 %collective-permute-start.48 = (bf16[64,512]{1,0:T(8,128)(2,1)S(1)}, bf16[64,512]{1,0:T(8,128)(2,1)S(1)}, u32[]{:S(2)}, u32[]{:S(2)}) collective-permute-start(bf16[64,512]{1,0:T(8,128)(2,1)S(1)} %get-tuple-element.504), channel_id=1, source_target_pairs={{256,368},{264,376},{272,320},{280,328},{288,336},{296,344},{304,3... | collective-permute-start | bytes 196616 | tf_op jit(solution)/shard_map/ppermute | solution.py:221
  559.4 16.7 %collective-permute-start.49 = (bf16[64,512]{1,0:T(8,128)(2,1)S(1)}, bf16[64,512]{1,0:T(8,128)(2,1)S(1)}, u32[]{:S(2)}, u32[]{:S(2)}) collective-permute-start(bf16[64,512]{1,0:T(8,128)(2,1)S(1)} %get-tuple-element.504), channel_id=1, source_target_pairs={{256,376},{264,320},{272,328},{280,336},{288,344},{296,352},{304,3... | collective-permute-start | bytes 196616 | tf_op jit(solution)/shard_map/ppermute | solution.py:221
  576.2 51.7 %collective-permute-start.50 = (bf16[64,512]{1,0:T(8,128)(2,1)S(1)}, bf16[64,512]{1,0:T(8,128)(2,1)S(1)}, u32[]{:S(2)}, u32[]{:S(2)}) collective-permute-start(bf16[64,512]{1,0:T(8,128)(2,1)S(1)} %get-tuple-element.505), channel_id=1, source_target_pairs={{320,384},{328,392},{336,400},{344,408},{352,416},{360,424},{368,4... | collective-permute-start | bytes 196616 | tf_op jit(solution)/shard_map/ppermute | solution.py:221
  627.9 16.4 %collective-permute-start.51 = (bf16[64,512]{1,0:T(8,128)(2,1)S(1)}, bf16[64,512]{1,0:T(8,128)(2,1)S(1)}, u32[]{:S(2)}, u32[]{:S(2)}) collective-permute-start(bf16[64,512]{1,0:T(8,128)(2,1)S(1)} %get-tuple-element.505), channel_id=1, source_target_pairs={{320,392},{328,400},{336,408},{344,416},{352,424},{360,432},{368,4... | collective-permute-start | bytes 196616 | tf_op jit(solution)/shard_map/ppermute | solution.py:221
  644.3 16.4 %collective-permute-start.52 = (bf16[64,512]{1,0:T(8,128)(2,1)S(1)}, bf16[64,512]{1,0:T(8,128)(2,1)S(1)}, u32[]{:S(2)}, u32[]{:S(2)}) collective-permute-start(bf16[64,512]{1,0:T(8,128)(2,1)S(1)} %get-tuple-element.505), channel_id=1, source_target_pairs={{320,400},{328,408},{336,416},{344,424},{352,432},{360,440},{368,3... | collective-permute-start | bytes 196616 | tf_op jit(solution)/shard_map/ppermute | solution.py:221
  660.7 16.4 %collective-permute-start.53 = (bf16[64,512]{1,0:T(8,128)(2,1)S(1)}, bf16[64,512]{1,0:T(8,128)(2,1)S(1)}, u32[]{:S(2)}, u32[]{:S(2)}) collective-permute-start(bf16[64,512]{1,0:T(8,128)(2,1)S(1)} %get-tuple-element.505), channel_id=1, source_target_pairs={{320,408},{328,416},{336,424},{344,432},{352,440},{360,384},{368,3... | collective-permute-start | bytes 196616 | tf_op jit(solution)/shard_map/ppermute | solution.py:221
  677.1 16.4 %collective-permute-start.54 = (bf16[64,512]{1,0:T(8,128)(2,1)S(1)}, bf16[64,512]{1,0:T(8,128)(2,1)S(1)}, u32[]{:S(2)}, u32[]{:S(2)}) collective-permute-start(bf16[64,512]{1,0:T(8,128)(2,1)S(1)} %get-tuple-element.505), channel_id=1, source_target_pairs={{320,416},{328,424},{336,432},{344,440},{352,384},{360,392},{368,4... | collective-permute-start | bytes 196616 | tf_op jit(solution)/shard_map/ppermute | solution.py:221
  693.5 16.4 %collective-permute-start.55 = (bf16[64,512]{1,0:T(8,128)(2,1)S(1)}, bf16[64,512]{1,0:T(8,128)(2,1)S(1)}, u32[]{:S(2)}, u32[]{:S(2)}) collective-permute-start(bf16[64,512]{1,0:T(8,128)(2,1)S(1)} %get-tuple-element.505), channel_id=1, source_target_pairs={{320,424},{328,432},{336,440},{344,384},{352,392},{360,400},{368,4... | collective-permute-start | bytes 196616 | tf_op jit(solution)/shard_map/ppermute | solution.py:221
  709.9 16.4 %collective-permute-start.56 = (bf16[64,512]{1,0:T(8,128)(2,1)S(1)}, bf16[64,512]{1,0:T(8,128)(2,1)S(1)}, u32[]{:S(2)}, u32[]{:S(2)}) collective-permute-start(bf16[64,512]{1,0:T(8,128)(2,1)S(1)} %get-tuple-element.505), channel_id=1, source_target_pairs={{320,432},{328,440},{336,384},{344,392},{352,400},{360,408},{368,4... | collective-permute-start | bytes 196616 | tf_op jit(solution)/shard_map/ppermute | solution.py:221
  726.3 16.4 %collective-permute-start.57 = (bf16[64,512]{1,0:T(8,128)(2,1)S(1)}, bf16[64,512]{1,0:T(8,128)(2,1)S(1)}, u32[]{:S(2)}, u32[]{:S(2)}) collective-permute-start(bf16[64,512]{1,0:T(8,128)(2,1)S(1)} %get-tuple-element.505), channel_id=1, source_target_pairs={{320,440},{328,384},{336,392},{344,400},{352,408},{360,416},{368,4... | collective-permute-start | bytes 196616 | tf_op jit(solution)/shard_map/ppermute | solution.py:221
  742.7 51.4 %collective-permute-start.58 = (bf16[64,512]{1,0:T(8,128)(2,1)S(1)}, bf16[64,512]{1,0:T(8,128)(2,1)S(1)}, u32[]{:S(2)}, u32[]{:S(2)}) collective-permute-start(bf16[64,512]{1,0:T(8,128)(2,1)S(1)} %get-tuple-element.506), channel_id=1, source_target_pairs={{384,448},{392,456},{400,464},{408,472},{416,480},{424,488},{432,4... | collective-permute-start | bytes 196616 | tf_op jit(solution)/shard_map/ppermute | solution.py:221
  794.1 16.1 %collective-permute-start.59 = (bf16[64,512]{1,0:T(8,128)(2,1)S(1)}, bf16[64,512]{1,0:T(8,128)(2,1)S(1)}, u32[]{:S(2)}, u32[]{:S(2)}) collective-permute-start(bf16[64,512]{1,0:T(8,128)(2,1)S(1)} %get-tuple-element.506), channel_id=1, source_target_pairs={{384,456},{392,464},{400,472},{408,480},{416,488},{424,496},{432,5... | collective-permute-start | bytes 196616 | tf_op jit(solution)/shard_map/ppermute | solution.py:221
  810.2 16.1 %collective-permute-start.60 = (bf16[64,512]{1,0:T(8,128)(2,1)S(1)}, bf16[64,512]{1,0:T(8,128)(2,1)S(1)}, u32[]{:S(2)}, u32[]{:S(2)}) collective-permute-start(bf16[64,512]{1,0:T(8,128)(2,1)S(1)} %get-tuple-element.506), channel_id=1, source_target_pairs={{384,464},{392,472},{400,480},{408,488},{416,496},{424,504},{432,4... | collective-permute-start | bytes 196616 | tf_op jit(solution)/shard_map/ppermute | solution.py:221
  826.3 16.1 %collective-permute-start.61 = (bf16[64,512]{1,0:T(8,128)(2,1)S(1)}, bf16[64,512]{1,0:T(8,128)(2,1)S(1)}, u32[]{:S(2)}, u32[]{:S(2)}) collective-permute-start(bf16[64,512]{1,0:T(8,128)(2,1)S(1)} %get-tuple-element.506), channel_id=1, source_target_pairs={{384,472},{392,480},{400,488},{408,496},{416,504},{424,448},{432,4... | collective-permute-start | bytes 196616 | tf_op jit(solution)/shard_map/ppermute | solution.py:221
  842.4 16.3 %collective-permute-start.62 = (bf16[64,512]{1,0:T(8,128)(2,1)S(1)}, bf16[64,512]{1,0:T(8,128)(2,1)S(1)}, u32[]{:S(2)}, u32[]{:S(2)}) collective-permute-start(bf16[64,512]{1,0:T(8,128)(2,1)S(1)} %get-tuple-element.506), channel_id=1, source_target_pairs={{384,480},{392,488},{400,496},{408,504},{416,448},{424,456},{432,4... | collective-permute-start | bytes 196616 | tf_op jit(solution)/shard_map/ppermute | solution.py:221
  858.7 16.1 %collective-permute-start.63 = (bf16[64,512]{1,0:T(8,128)(2,1)S(1)}, bf16[64,512]{1,0:T(8,128)(2,1)S(1)}, u32[]{:S(2)}, u32[]{:S(2)}) collective-permute-start(bf16[64,512]{1,0:T(8,128)(2,1)S(1)} %get-tuple-element.506), channel_id=1, source_target_pairs={{384,488},{392,496},{400,504},{408,448},{416,456},{424,464},{432,4... | collective-permute-start | bytes 196616 | tf_op jit(solution)/shard_map/ppermute | solution.py:221
  874.8 16.1 %collective-permute-start.64 = (bf16[64,512]{1,0:T(8,128)(2,1)S(1)}, bf16[64,512]{1,0:T(8,128)(2,1)S(1)}, u32[]{:S(2)}, u32[]{:S(2)}) collective-permute-start(bf16[64,512]{1,0:T(8,128)(2,1)S(1)} %get-tuple-element.506), channel_id=1, source_target_pairs={{384,496},{392,504},{400,448},{408,456},{416,464},{424,472},{432,4... | collective-permute-start | bytes 196616 | tf_op jit(solution)/shard_map/ppermute | solution.py:221
  890.9 16.1 %collective-permute-start.65 = (bf16[64,512]{1,0:T(8,128)(2,1)S(1)}, bf16[64,512]{1,0:T(8,128)(2,1)S(1)}, u32[]{:S(2)}, u32[]{:S(2)}) collective-permute-start(bf16[64,512]{1,0:T(8,128)(2,1)S(1)} %get-tuple-element.506), channel_id=1, source_target_pairs={{384,504},{392,448},{400,456},{408,464},{416,472},{424,480},{432,4... | collective-permute-start | bytes 196616 | tf_op jit(solution)/shard_map/ppermute | solution.py:221
  909.1 56.6 %conditional.19 = (f32[16,512]{1,0:T(8,128)S(1)}) conditional(s32[]{:T(128)} %convert_element_type.107, (s32[]{:T(128)}, s32[]{:T(128)}, s32[1,16]{1,0:T(1,128)S(1)}, bf16[1,1,40]{2,1,0:T(2,128)(2,1)S(1)}, bf16[512,10]{0,1:T(8,128)(2,1)S(1)}, /*index=5*/f32[512]{0:T(512)S(1)}, f32[512]{0:T(512)S(1)}, f32[512]{0:T(512)S(1)}, ...), branch_computations={%region_34.45_spmd, %region_45.46_spmd} | conditional | flops 1064623 | bytes 458498 | solution.py:293
  915.0 3.6 psum.39
  918.6 17.0 %psum.40 = f32[16,512]{1,0:T(8,128)S(1)} all-reduce(f32[16,512]{1,0:T(8,128)S(1)} %psum.39), channel_id=1, replica_groups=mesh['section'=8,'y'=8,'core'=2,'dp'=4] {'dp'}, use_global_device_ids=true, to_apply=%region_43.43 | all-reduce | flops 8192 | bytes 65536 | tf_op jit(solution)/shard_map/cond/branch_0_fun/psum | solution.py:277
  935.7 30.1 %psum.41 = f32[16,512]{1,0:T(8,128)S(1)} all-reduce(f32[16,512]{1,0:T(8,128)S(1)} %psum.40), channel_id=1, replica_groups=mesh['section'=8,'y'=8,'core'=2,'dp'=4] {'y'}, use_global_device_ids=true, to_apply=%region_44.44 | all-reduce | flops 8192 | bytes 65536 | tf_op jit(solution)/shard_map/cond/branch_0_fun/psum | solution.py:277
  (201 shorter events, 50.4 us)
Async XLA Ops:
  0.7 46.5 %collective-permute-start = (bf16[512,256]{1,0:T(8,128)(2,1)}, bf16[512,256]{1,0:T(8,128)(2,1)S(1)}, u32[]{:S(2)}, u32[]{:S(2)}) collective-permute-start(bf16[512,256]{1,0:T(8,128)(2,1)} %param.48), channel_id=1, source_target_pairs={{0,4},{4,0},{1,5},{5,1},{2,6},{6,2},{3,7},{7,3},{8,12},{12,8},{9,1... | collective-permute-start | bytes 786440 | tf_op jit(solution)/shard_map/ppermute | solution.py:162
  7.9 45.2 %collective-permute-start.9 = (bf16[8,4,512,128]{3,2,1,0:T(8,128)(2,1)}, bf16[8,4,512,128]{3,2,1,0:T(8,128)(2,1)}, u32[]{:S(2)}, u32[]{:S(2)}) collective-permute-start(bf16[8,4,512,128]{3,2,1,0:T(8,128)(2,1)} %pad_maximum_fusion), channel_id=1, source_target_pairs={{0,4},{4,0},{1,5},{5,1},{2,6},{6,2},{3,7},{7,3},{8,12},{12,8},{9,1... | collective-permute-start | bytes 12582920 | tf_op jit(solution)/shard_map/ppermute | solution.py:162
  53.1 63.0 %collective-permute-start.10 = (bf16[64,512]{1,0:T(8,128)(2,1)S(1)}, bf16[64,512]{1,0:T(8,128)(2,1)S(1)}, u32[]{:S(2)}, u32[]{:S(2)}) collective-permute-start(bf16[64,512]{1,0:T(8,128)(2,1)S(1)} %get-tuple-element.500), channel_id=1, source_target_pairs={{0,64},{8,72},{16,80},{24,88},{32,96},{40,104},{48,112},{56,120},{... | collective-permute-start | bytes 196616 | tf_op jit(solution)/shard_map/ppermute | solution.py:221
  54.4 63.8 %collective-permute-start.11 = (bf16[64,512]{1,0:T(8,128)(2,1)S(1)}, bf16[64,512]{1,0:T(8,128)(2,1)S(1)}, u32[]{:S(2)}, u32[]{:S(2)}) collective-permute-start(bf16[64,512]{1,0:T(8,128)(2,1)S(1)} %get-tuple-element.500), channel_id=1, source_target_pairs={{0,72},{8,80},{16,88},{24,96},{32,104},{40,112},{48,120},{56,64},{... | collective-permute-start | bytes 196616 | tf_op jit(solution)/shard_map/ppermute | solution.py:221
  55.7 63.9 %collective-permute-start.12 = (bf16[64,512]{1,0:T(8,128)(2,1)S(1)}, bf16[64,512]{1,0:T(8,128)(2,1)S(1)}, u32[]{:S(2)}, u32[]{:S(2)}) collective-permute-start(bf16[64,512]{1,0:T(8,128)(2,1)S(1)} %get-tuple-element.500), channel_id=1, source_target_pairs={{0,80},{8,88},{16,96},{24,104},{32,112},{40,120},{48,64},{56,72},{... | collective-permute-start | bytes 196616 | tf_op jit(solution)/shard_map/ppermute | solution.py:221
  57.0 63.9 %collective-permute-start.13 = (bf16[64,512]{1,0:T(8,128)(2,1)S(1)}, bf16[64,512]{1,0:T(8,128)(2,1)S(1)}, u32[]{:S(2)}, u32[]{:S(2)}) collective-permute-start(bf16[64,512]{1,0:T(8,128)(2,1)S(1)} %get-tuple-element.500), channel_id=1, source_target_pairs={{0,88},{8,96},{16,104},{24,112},{32,120},{40,64},{48,72},{56,80},{... | collective-permute-start | bytes 196616 | tf_op jit(solution)/shard_map/ppermute | solution.py:221
  58.3 67.0 %collective-permute-start.14 = (bf16[64,512]{1,0:T(8,128)(2,1)S(1)}, bf16[64,512]{1,0:T(8,128)(2,1)S(1)}, u32[]{:S(2)}, u32[]{:S(2)}) collective-permute-start(bf16[64,512]{1,0:T(8,128)(2,1)S(1)} %get-tuple-element.500), channel_id=1, source_target_pairs={{0,96},{8,104},{16,112},{24,120},{32,64},{40,72},{48,80},{56,88},{... | collective-permute-start | bytes 196616 | tf_op jit(solution)/shard_map/ppermute | solution.py:221
  116.0 9.2 collective-permute-start.15
  118.1 9.4 collective-permute-start.16
  177.2 53.2 %collective-permute-start.28 = (bf16[64,512]{1,0:T(8,128)(2,1)S(1)}, bf16[64,512]{1,0:T(8,128)(2,1)S(1)}, u32[]{:S(2)}, u32[]{:S(2)}) collective-permute-start(bf16[64,512]{1,0:T(8,128)(2,1)S(1)} %get-tuple-element.502), channel_id=1, source_target_pairs={{128,208},{136,216},{144,224},{152,232},{160,240},{168,248},{176,1... | collective-permute-start | bytes 196616 | tf_op jit(solution)/shard_map/ppermute | solution.py:221
  177.9 68.6 %collective-permute-start.29 = (bf16[64,512]{1,0:T(8,128)(2,1)S(1)}, bf16[64,512]{1,0:T(8,128)(2,1)S(1)}, u32[]{:S(2)}, u32[]{:S(2)}) collective-permute-start(bf16[64,512]{1,0:T(8,128)(2,1)S(1)} %get-tuple-element.502), channel_id=1, source_target_pairs={{128,216},{136,224},{144,232},{152,240},{160,248},{168,192},{176,2... | collective-permute-start | bytes 196616 | tf_op jit(solution)/shard_map/ppermute | solution.py:221
  178.5 68.0 %collective-permute-start.30 = (bf16[64,512]{1,0:T(8,128)(2,1)S(1)}, bf16[64,512]{1,0:T(8,128)(2,1)S(1)}, u32[]{:S(2)}, u32[]{:S(2)}) collective-permute-start(bf16[64,512]{1,0:T(8,128)(2,1)S(1)} %get-tuple-element.502), channel_id=1, source_target_pairs={{128,224},{136,232},{144,240},{152,248},{160,192},{168,200},{176,2... | collective-permute-start | bytes 196616 | tf_op jit(solution)/shard_map/ppermute | solution.py:221
  179.2 67.3 %collective-permute-start.31 = (bf16[64,512]{1,0:T(8,128)(2,1)S(1)}, bf16[64,512]{1,0:T(8,128)(2,1)S(1)}, u32[]{:S(2)}, u32[]{:S(2)}) collective-permute-start(bf16[64,512]{1,0:T(8,128)(2,1)S(1)} %get-tuple-element.502), channel_id=1, source_target_pairs={{128,232},{136,240},{144,248},{152,192},{160,200},{168,208},{176,2... | collective-permute-start | bytes 196616 | tf_op jit(solution)/shard_map/ppermute | solution.py:221
  179.9 66.6 %collective-permute-start.32 = (bf16[64,512]{1,0:T(8,128)(2,1)S(1)}, bf16[64,512]{1,0:T(8,128)(2,1)S(1)}, u32[]{:S(2)}, u32[]{:S(2)}) collective-permute-start(bf16[64,512]{1,0:T(8,128)(2,1)S(1)} %get-tuple-element.502), channel_id=1, source_target_pairs={{128,240},{136,248},{144,192},{152,200},{160,208},{168,216},{176,2... | collective-permute-start | bytes 196616 | tf_op jit(solution)/shard_map/ppermute | solution.py:221
  230.4 16.1 %collective-permute-start.33 = (bf16[64,512]{1,0:T(8,128)(2,1)S(1)}, bf16[64,512]{1,0:T(8,128)(2,1)S(1)}, u32[]{:S(2)}, u32[]{:S(2)}) collective-permute-start(bf16[64,512]{1,0:T(8,128)(2,1)S(1)} %get-tuple-element.502), channel_id=1, source_target_pairs={{128,248},{136,192},{144,200},{152,208},{160,216},{168,224},{176,2... | collective-permute-start | bytes 196616 | tf_op jit(solution)/shard_map/ppermute | solution.py:221
  246.5 112.9 %collective-permute-start.34 = (bf16[64,512]{1,0:T(8,128)(2,1)S(1)}, bf16[64,512]{1,0:T(8,128)(2,1)S(1)}, u32[]{:S(2)}, u32[]{:S(2)}) collective-permute-start(bf16[64,512]{1,0:T(8,128)(2,1)S(1)} %get-tuple-element.503), channel_id=1, source_target_pairs={{192,256},{200,264},{208,272},{216,280},{224,288},{232,296},{240,3... | collective-permute-start | bytes 196616 | tf_op jit(solution)/shard_map/ppermute | solution.py:221
  295.1 80.4 %collective-permute-start.35 = (bf16[64,512]{1,0:T(8,128)(2,1)S(1)}, bf16[64,512]{1,0:T(8,128)(2,1)S(1)}, u32[]{:S(2)}, u32[]{:S(2)}) collective-permute-start(bf16[64,512]{1,0:T(8,128)(2,1)S(1)} %get-tuple-element.503), channel_id=1, source_target_pairs={{192,264},{200,272},{208,280},{216,288},{224,296},{232,304},{240,3... | collective-permute-start | bytes 196616 | tf_op jit(solution)/shard_map/ppermute | solution.py:221
  311.2 80.4 %collective-permute-start.36 = (bf16[64,512]{1,0:T(8,128)(2,1)S(1)}, bf16[64,512]{1,0:T(8,128)(2,1)S(1)}, u32[]{:S(2)}, u32[]{:S(2)}) collective-permute-start(bf16[64,512]{1,0:T(8,128)(2,1)S(1)} %get-tuple-element.503), channel_id=1, source_target_pairs={{192,272},{200,280},{208,288},{216,296},{224,304},{232,312},{240,2... | collective-permute-start | bytes 196616 | tf_op jit(solution)/shard_map/ppermute | solution.py:221
  327.2 80.4 %collective-permute-start.37 = (bf16[64,512]{1,0:T(8,128)(2,1)S(1)}, bf16[64,512]{1,0:T(8,128)(2,1)S(1)}, u32[]{:S(2)}, u32[]{:S(2)}) collective-permute-start(bf16[64,512]{1,0:T(8,128)(2,1)S(1)} %get-tuple-element.503), channel_id=1, source_target_pairs={{192,280},{200,288},{208,296},{216,304},{224,312},{232,256},{240,2... | collective-permute-start | bytes 196616 | tf_op jit(solution)/shard_map/ppermute | solution.py:221
  343.3 64.4 %collective-permute-start.38 = (bf16[64,512]{1,0:T(8,128)(2,1)S(1)}, bf16[64,512]{1,0:T(8,128)(2,1)S(1)}, u32[]{:S(2)}, u32[]{:S(2)}) collective-permute-start(bf16[64,512]{1,0:T(8,128)(2,1)S(1)} %get-tuple-element.503), channel_id=1, source_target_pairs={{192,288},{200,296},{208,304},{216,312},{224,256},{232,264},{240,2... | collective-permute-start | bytes 196616 | tf_op jit(solution)/shard_map/ppermute | solution.py:221
  359.4 48.3 %collective-permute-start.39 = (bf16[64,512]{1,0:T(8,128)(2,1)S(1)}, bf16[64,512]{1,0:T(8,128)(2,1)S(1)}, u32[]{:S(2)}, u32[]{:S(2)}) collective-permute-start(bf16[64,512]{1,0:T(8,128)(2,1)S(1)} %get-tuple-element.503), channel_id=1, source_target_pairs={{192,296},{200,304},{208,312},{216,256},{224,264},{232,272},{240,2... | collective-permute-start | bytes 196616 | tf_op jit(solution)/shard_map/ppermute | solution.py:221
  375.5 32.2 %collective-permute-start.40 = (bf16[64,512]{1,0:T(8,128)(2,1)S(1)}, bf16[64,512]{1,0:T(8,128)(2,1)S(1)}, u32[]{:S(2)}, u32[]{:S(2)}) collective-permute-start(bf16[64,512]{1,0:T(8,128)(2,1)S(1)} %get-tuple-element.503), channel_id=1, source_target_pairs={{192,304},{200,312},{208,256},{216,264},{224,272},{232,280},{240,2... | collective-permute-start | bytes 196616 | tf_op jit(solution)/shard_map/ppermute | solution.py:221
  391.6 16.1 %collective-permute-start.41 = (bf16[64,512]{1,0:T(8,128)(2,1)S(1)}, bf16[64,512]{1,0:T(8,128)(2,1)S(1)}, u32[]{:S(2)}, u32[]{:S(2)}) collective-permute-start(bf16[64,512]{1,0:T(8,128)(2,1)S(1)} %get-tuple-element.503), channel_id=1, source_target_pairs={{192,312},{200,256},{208,264},{216,272},{224,280},{232,288},{240,2... | collective-permute-start | bytes 196616 | tf_op jit(solution)/shard_map/ppermute | solution.py:221
  407.8 118.2 %collective-permute-start.42 = (bf16[64,512]{1,0:T(8,128)(2,1)S(1)}, bf16[64,512]{1,0:T(8,128)(2,1)S(1)}, u32[]{:S(2)}, u32[]{:S(2)}) collective-permute-start(bf16[64,512]{1,0:T(8,128)(2,1)S(1)} %get-tuple-element.504), channel_id=1, source_target_pairs={{256,320},{264,328},{272,336},{280,344},{288,352},{296,360},{304,3... | collective-permute-start | bytes 196616 | tf_op jit(solution)/shard_map/ppermute | solution.py:221
  458.9 83.7 %collective-permute-start.43 = (bf16[64,512]{1,0:T(8,128)(2,1)S(1)}, bf16[64,512]{1,0:T(8,128)(2,1)S(1)}, u32[]{:S(2)}, u32[]{:S(2)}) collective-permute-start(bf16[64,512]{1,0:T(8,128)(2,1)S(1)} %get-tuple-element.504), channel_id=1, source_target_pairs={{256,328},{264,336},{272,344},{280,352},{288,360},{296,368},{304,3... | collective-permute-start | bytes 196616 | tf_op jit(solution)/shard_map/ppermute | solution.py:221
  475.7 83.7 %collective-permute-start.44 = (bf16[64,512]{1,0:T(8,128)(2,1)S(1)}, bf16[64,512]{1,0:T(8,128)(2,1)S(1)}, u32[]{:S(2)}, u32[]{:S(2)}) collective-permute-start(bf16[64,512]{1,0:T(8,128)(2,1)S(1)} %get-tuple-element.504), channel_id=1, source_target_pairs={{256,336},{264,344},{272,352},{280,360},{288,368},{296,376},{304,3... | collective-permute-start | bytes 196616 | tf_op jit(solution)/shard_map/ppermute | solution.py:221
  492.4 83.8 %collective-permute-start.45 = (bf16[64,512]{1,0:T(8,128)(2,1)S(1)}, bf16[64,512]{1,0:T(8,128)(2,1)S(1)}, u32[]{:S(2)}, u32[]{:S(2)}) collective-permute-start(bf16[64,512]{1,0:T(8,128)(2,1)S(1)} %get-tuple-element.504), channel_id=1, source_target_pairs={{256,344},{264,352},{272,360},{280,368},{288,376},{296,320},{304,3... | collective-permute-start | bytes 196616 | tf_op jit(solution)/shard_map/ppermute | solution.py:221
  509.2 67.0 %collective-permute-start.46 = (bf16[64,512]{1,0:T(8,128)(2,1)S(1)}, bf16[64,512]{1,0:T(8,128)(2,1)S(1)}, u32[]{:S(2)}, u32[]{:S(2)}) collective-permute-start(bf16[64,512]{1,0:T(8,128)(2,1)S(1)} %get-tuple-element.504), channel_id=1, source_target_pairs={{256,352},{264,360},{272,368},{280,376},{288,320},{296,328},{304,3... | collective-permute-start | bytes 196616 | tf_op jit(solution)/shard_map/ppermute | solution.py:221
  525.9 50.3 %collective-permute-start.47 = (bf16[64,512]{1,0:T(8,128)(2,1)S(1)}, bf16[64,512]{1,0:T(8,128)(2,1)S(1)}, u32[]{:S(2)}, u32[]{:S(2)}) collective-permute-start(bf16[64,512]{1,0:T(8,128)(2,1)S(1)} %get-tuple-element.504), channel_id=1, source_target_pairs={{256,360},{264,368},{272,376},{280,320},{288,328},{296,336},{304,3... | collective-permute-start | bytes 196616 | tf_op jit(solution)/shard_map/ppermute | solution.py:221
  542.7 33.5 %collective-permute-start.48 = (bf16[64,512]{1,0:T(8,128)(2,1)S(1)}, bf16[64,512]{1,0:T(8,128)(2,1)S(1)}, u32[]{:S(2)}, u32[]{:S(2)}) collective-permute-start(bf16[64,512]{1,0:T(8,128)(2,1)S(1)} %get-tuple-element.504), channel_id=1, source_target_pairs={{256,368},{264,376},{272,320},{280,328},{288,336},{296,344},{304,3... | collective-permute-start | bytes 196616 | tf_op jit(solution)/shard_map/ppermute | solution.py:221
  559.4 16.8 %collective-permute-start.49 = (bf16[64,512]{1,0:T(8,128)(2,1)S(1)}, bf16[64,512]{1,0:T(8,128)(2,1)S(1)}, u32[]{:S(2)}, u32[]{:S(2)}) collective-permute-start(bf16[64,512]{1,0:T(8,128)(2,1)S(1)} %get-tuple-element.504), channel_id=1, source_target_pairs={{256,376},{264,320},{272,328},{280,336},{288,344},{296,352},{304,3... | collective-permute-start | bytes 196616 | tf_op jit(solution)/shard_map/ppermute | solution.py:221
  576.2 117.3 %collective-permute-start.50 = (bf16[64,512]{1,0:T(8,128)(2,1)S(1)}, bf16[64,512]{1,0:T(8,128)(2,1)S(1)}, u32[]{:S(2)}, u32[]{:S(2)}) collective-permute-start(bf16[64,512]{1,0:T(8,128)(2,1)S(1)} %get-tuple-element.505), channel_id=1, source_target_pairs={{320,384},{328,392},{336,400},{344,408},{352,416},{360,424},{368,4... | collective-permute-start | bytes 196616 | tf_op jit(solution)/shard_map/ppermute | solution.py:221
  627.9 81.9 %collective-permute-start.51 = (bf16[64,512]{1,0:T(8,128)(2,1)S(1)}, bf16[64,512]{1,0:T(8,128)(2,1)S(1)}, u32[]{:S(2)}, u32[]{:S(2)}) collective-permute-start(bf16[64,512]{1,0:T(8,128)(2,1)S(1)} %get-tuple-element.505), channel_id=1, source_target_pairs={{320,392},{328,400},{336,408},{344,416},{352,424},{360,432},{368,4... | collective-permute-start | bytes 196616 | tf_op jit(solution)/shard_map/ppermute | solution.py:221
  644.3 81.9 %collective-permute-start.52 = (bf16[64,512]{1,0:T(8,128)(2,1)S(1)}, bf16[64,512]{1,0:T(8,128)(2,1)S(1)}, u32[]{:S(2)}, u32[]{:S(2)}) collective-permute-start(bf16[64,512]{1,0:T(8,128)(2,1)S(1)} %get-tuple-element.505), channel_id=1, source_target_pairs={{320,400},{328,408},{336,416},{344,424},{352,432},{360,440},{368,3... | collective-permute-start | bytes 196616 | tf_op jit(solution)/shard_map/ppermute | solution.py:221
  660.7 82.0 %collective-permute-start.53 = (bf16[64,512]{1,0:T(8,128)(2,1)S(1)}, bf16[64,512]{1,0:T(8,128)(2,1)S(1)}, u32[]{:S(2)}, u32[]{:S(2)}) collective-permute-start(bf16[64,512]{1,0:T(8,128)(2,1)S(1)} %get-tuple-element.505), channel_id=1, source_target_pairs={{320,408},{328,416},{336,424},{344,432},{352,440},{360,384},{368,3... | collective-permute-start | bytes 196616 | tf_op jit(solution)/shard_map/ppermute | solution.py:221
  677.1 65.6 %collective-permute-start.54 = (bf16[64,512]{1,0:T(8,128)(2,1)S(1)}, bf16[64,512]{1,0:T(8,128)(2,1)S(1)}, u32[]{:S(2)}, u32[]{:S(2)}) collective-permute-start(bf16[64,512]{1,0:T(8,128)(2,1)S(1)} %get-tuple-element.505), channel_id=1, source_target_pairs={{320,416},{328,424},{336,432},{344,440},{352,384},{360,392},{368,4... | collective-permute-start | bytes 196616 | tf_op jit(solution)/shard_map/ppermute | solution.py:221
  693.5 49.2 %collective-permute-start.55 = (bf16[64,512]{1,0:T(8,128)(2,1)S(1)}, bf16[64,512]{1,0:T(8,128)(2,1)S(1)}, u32[]{:S(2)}, u32[]{:S(2)}) collective-permute-start(bf16[64,512]{1,0:T(8,128)(2,1)S(1)} %get-tuple-element.505), channel_id=1, source_target_pairs={{320,424},{328,432},{336,440},{344,384},{352,392},{360,400},{368,4... | collective-permute-start | bytes 196616 | tf_op jit(solution)/shard_map/ppermute | solution.py:221
  709.9 32.8 %collective-permute-start.56 = (bf16[64,512]{1,0:T(8,128)(2,1)S(1)}, bf16[64,512]{1,0:T(8,128)(2,1)S(1)}, u32[]{:S(2)}, u32[]{:S(2)}) collective-permute-start(bf16[64,512]{1,0:T(8,128)(2,1)S(1)} %get-tuple-element.505), channel_id=1, source_target_pairs={{320,432},{328,440},{336,384},{344,392},{352,400},{360,408},{368,4... | collective-permute-start | bytes 196616 | tf_op jit(solution)/shard_map/ppermute | solution.py:221
  726.3 16.4 %collective-permute-start.57 = (bf16[64,512]{1,0:T(8,128)(2,1)S(1)}, bf16[64,512]{1,0:T(8,128)(2,1)S(1)}, u32[]{:S(2)}, u32[]{:S(2)}) collective-permute-start(bf16[64,512]{1,0:T(8,128)(2,1)S(1)} %get-tuple-element.505), channel_id=1, source_target_pairs={{320,440},{328,384},{336,392},{344,400},{352,408},{360,416},{368,4... | collective-permute-start | bytes 196616 | tf_op jit(solution)/shard_map/ppermute | solution.py:221
  742.7 115.9 %collective-permute-start.58 = (bf16[64,512]{1,0:T(8,128)(2,1)S(1)}, bf16[64,512]{1,0:T(8,128)(2,1)S(1)}, u32[]{:S(2)}, u32[]{:S(2)}) collective-permute-start(bf16[64,512]{1,0:T(8,128)(2,1)S(1)} %get-tuple-element.506), channel_id=1, source_target_pairs={{384,448},{392,456},{400,464},{408,472},{416,480},{424,488},{432,4... | collective-permute-start | bytes 196616 | tf_op jit(solution)/shard_map/ppermute | solution.py:221
  794.1 80.7 %collective-permute-start.59 = (bf16[64,512]{1,0:T(8,128)(2,1)S(1)}, bf16[64,512]{1,0:T(8,128)(2,1)S(1)}, u32[]{:S(2)}, u32[]{:S(2)}) collective-permute-start(bf16[64,512]{1,0:T(8,128)(2,1)S(1)} %get-tuple-element.506), channel_id=1, source_target_pairs={{384,456},{392,464},{400,472},{408,480},{416,488},{424,496},{432,5... | collective-permute-start | bytes 196616 | tf_op jit(solution)/shard_map/ppermute | solution.py:221
  810.2 80.7 %collective-permute-start.60 = (bf16[64,512]{1,0:T(8,128)(2,1)S(1)}, bf16[64,512]{1,0:T(8,128)(2,1)S(1)}, u32[]{:S(2)}, u32[]{:S(2)}) collective-permute-start(bf16[64,512]{1,0:T(8,128)(2,1)S(1)} %get-tuple-element.506), channel_id=1, source_target_pairs={{384,464},{392,472},{400,480},{408,488},{416,496},{424,504},{432,4... | collective-permute-start | bytes 196616 | tf_op jit(solution)/shard_map/ppermute | solution.py:221
  826.3 80.7 %collective-permute-start.61 = (bf16[64,512]{1,0:T(8,128)(2,1)S(1)}, bf16[64,512]{1,0:T(8,128)(2,1)S(1)}, u32[]{:S(2)}, u32[]{:S(2)}) collective-permute-start(bf16[64,512]{1,0:T(8,128)(2,1)S(1)} %get-tuple-element.506), channel_id=1, source_target_pairs={{384,472},{392,480},{400,488},{408,496},{416,504},{424,448},{432,4... | collective-permute-start | bytes 196616 | tf_op jit(solution)/shard_map/ppermute | solution.py:221
  842.4 64.6 %collective-permute-start.62 = (bf16[64,512]{1,0:T(8,128)(2,1)S(1)}, bf16[64,512]{1,0:T(8,128)(2,1)S(1)}, u32[]{:S(2)}, u32[]{:S(2)}) collective-permute-start(bf16[64,512]{1,0:T(8,128)(2,1)S(1)} %get-tuple-element.506), channel_id=1, source_target_pairs={{384,480},{392,488},{400,496},{408,504},{416,448},{424,456},{432,4... | collective-permute-start | bytes 196616 | tf_op jit(solution)/shard_map/ppermute | solution.py:221
  858.7 48.3 %collective-permute-start.63 = (bf16[64,512]{1,0:T(8,128)(2,1)S(1)}, bf16[64,512]{1,0:T(8,128)(2,1)S(1)}, u32[]{:S(2)}, u32[]{:S(2)}) collective-permute-start(bf16[64,512]{1,0:T(8,128)(2,1)S(1)} %get-tuple-element.506), channel_id=1, source_target_pairs={{384,488},{392,496},{400,504},{408,448},{416,456},{424,464},{432,4... | collective-permute-start | bytes 196616 | tf_op jit(solution)/shard_map/ppermute | solution.py:221
  874.8 32.2 %collective-permute-start.64 = (bf16[64,512]{1,0:T(8,128)(2,1)S(1)}, bf16[64,512]{1,0:T(8,128)(2,1)S(1)}, u32[]{:S(2)}, u32[]{:S(2)}) collective-permute-start(bf16[64,512]{1,0:T(8,128)(2,1)S(1)} %get-tuple-element.506), channel_id=1, source_target_pairs={{384,496},{392,504},{400,448},{408,456},{416,464},{424,472},{432,4... | collective-permute-start | bytes 196616 | tf_op jit(solution)/shard_map/ppermute | solution.py:221
  890.9 16.1 %collective-permute-start.65 = (bf16[64,512]{1,0:T(8,128)(2,1)S(1)}, bf16[64,512]{1,0:T(8,128)(2,1)S(1)}, u32[]{:S(2)}, u32[]{:S(2)}) collective-permute-start(bf16[64,512]{1,0:T(8,128)(2,1)S(1)} %get-tuple-element.506), channel_id=1, source_target_pairs={{384,504},{392,448},{400,456},{408,464},{416,472},{424,480},{432,4... | collective-permute-start | bytes 196616 | tf_op jit(solution)/shard_map/ppermute | solution.py:221
  907.1 59.9 %collective-permute-start.66 = (bf16[64,256]{1,0:T(8,128)(2,1)S(1)}, bf16[64,256]{1,0:T(8,128)(2,1)S(1)}, u32[]{:S(2)}, u32[]{:S(2)}) collective-permute-start(bf16[64,256]{1,0:T(8,128)(2,1)S(1)} %get-tuple-element.489), channel_id=1, source_target_pairs={{0,4},{4,0},{1,5},{5,1},{2,6},{6,2},{3,7},{7,3},{8,12},{12,8},{9,1... | collective-permute-start | bytes 98312 | tf_op jit(solution)/shard_map/ppermute | solution.py:162
  (36 other events, 655.5 us)

commit v3 on v1

v3 whole, which is shorter than its diff:
```python
import jax
import jax.numpy as jnp
from jax import lax
from jax.experimental import pallas as pl
from jax.experimental.pallas import tpu as pltpu
from jax.sharding import Mesh, PartitionSpec as P

HEAD_DIM = 128
KERNEL = 10
STRIDE = 5
MICRO = 2
CORES = 2


def layer_norm(values, gain, shift):
    average = jnp.mean(values, axis=-1, keepdims=True)
    centered = values - average
    spread = jnp.mean(centered * centered, axis=-1, keepdims=True)
    return centered * lax.rsqrt(spread + 1e-05) * gain + shift


def frame_counts(lengths):
    return (lengths - KERNEL) // STRIDE + 1


def framed_of(wave, lengths):
    owners, samples = wave.shape
    positions = lax.broadcasted_iota(jnp.int32, wave.shape, 1)
    cleaned = jnp.where(positions < lengths[:, None], wave, jnp.zeros_like(wave))
    blocks = cleaned.reshape(owners, samples // STRIDE, STRIDE)
    after = jnp.concatenate([blocks[:, 1:], jnp.zeros_like(blocks[:, :1])], axis=1)
    return jnp.concatenate([blocks, after], axis=2)


def live_of(lengths, frame_total):
    counts = frame_counts(lengths)
    return lax.broadcasted_iota(jnp.int32, (lengths.shape[0], frame_total), 1) < counts[:, None]


def frontend(weight, bias, gain, shift, framed, live):
    convolved = (
        jnp.einsum("...fk,ck->...fc", framed, weight, precision=lax.Precision.HIGHEST) + bias
    )
    active = jax.nn.gelu(layer_norm(convolved, gain, shift), approximate=False)
    return jnp.where(live[..., None], active, jnp.zeros_like(active))


def product(left, right):
    return jnp.dot(left, right, preferred_element_type=jnp.float32)


def mixing_kernel(blocks, gain, shift, query, key, value, masking, out):
    parts, rows, width = blocks.shape
    total = jnp.zeros((rows, 1), jnp.float32)
    for i in range(parts):
        total += jnp.sum(blocks[i].astype(jnp.float32), axis=-1, keepdims=True)
    average = total / (parts * width)
    spread = jnp.zeros_like(average)
    for i in range(parts):
        centered = blocks[i].astype(jnp.float32) - average
        spread += jnp.sum(centered * centered, axis=-1, keepdims=True)
    scale = lax.rsqrt(spread / (parts * width) + 1e-05)
    both = jnp.zeros((rows, 2 * HEAD_DIM), jnp.float32)
    values = jnp.zeros((rows, HEAD_DIM), jnp.float32)
    for i in range(parts):
        centered = blocks[i].astype(jnp.float32) - average
        normed = (centered * scale * gain[i] + shift[i]).astype(jnp.bfloat16)
        both += product(normed, jnp.concatenate([query[i], key[i]], axis=1))
        values += product(normed, value[i])
    queries = (both[:, :HEAD_DIM] * HEAD_DIM ** (-0.5)).astype(jnp.bfloat16)
    key_rows = both[:, HEAD_DIM:].astype(jnp.bfloat16)
    scores = lax.dot_general(
        queries, key_rows, (((1,), (1,)), ((), ())), preferred_element_type=jnp.float32
    )
    scores = jnp.where(masking[...] > 0, scores, -jnp.inf)
    raised = jnp.exp(scores - jnp.max(scores, axis=-1, keepdims=True))
    attention = (raised / jnp.sum(raised, axis=-1, keepdims=True)).astype(jnp.bfloat16)
    out[...] = product(attention, values.astype(jnp.bfloat16)).astype(jnp.bfloat16)


def leaving_kernel(mixed, current, weights, bias, out):
    total = current[...].astype(jnp.float32) + bias[...]
    for i in range(0, mixed.shape[0], 2):
        pair = jnp.concatenate([mixed[i], mixed[i + 1]], axis=1)
        total += product(pair, weights[i // 2])
    out[...] = total.astype(jnp.bfloat16)


def on_device(
    wave,
    lengths,
    assign,
    conv_weight,
    conv_bias,
    conv_gain,
    conv_shift,
    feat_gain,
    feat_shift,
    proj_weight,
    proj_bias,
    norm_gain,
    norm_shift,
    query_weight,
    key_weight,
    value_weight,
    out_weight,
    out_bias,
    feat_grad,
):
    section, chip, core = (lax.axis_index(name) for name in ("section", "y", "core"))
    sections, chips = lax.axis_size("section"), lax.axis_size("y")
    group = chips * CORES
    samples = wave.shape[2]
    frame_total = samples // STRIDE
    batch_size = lengths.shape[1]
    utts = batch_size // MICRO
    rows = utts * frame_total
    columns = proj_weight.shape[1]

    waves = lax.all_gather(wave[0].astype(jnp.float32), ("y", "core"), axis=0, tiled=True)
    slots = lax.broadcasted_iota(jnp.int32, (batch_size, batch_size), 1)
    chosen = assign[0][:, None] == slots
    slot_lengths = jnp.sum(jnp.where(chosen, lengths[0][:, None], 0), axis=0)
    slot_waves = jnp.sum(jnp.where(chosen[:, :, None], waves[:, None], 0.0), axis=0)
    framed = framed_of(slot_waves.astype(jnp.bfloat16), slot_lengths)
    convolved = (
        jnp.einsum("ufk,ck->ufc", framed, conv_weight, preferred_element_type=jnp.float32)
        + conv_bias
    )
    active = jax.nn.gelu(layer_norm(convolved, conv_gain, conv_shift), approximate=False)
    live = live_of(slot_lengths, frame_total)
    frames = jnp.where(live[..., None], active, 0.0).astype(jnp.bfloat16)
    frames = frames.reshape(MICRO * rows, frames.shape[2])
    normed_frames = layer_norm(frames.astype(jnp.float32), feat_gain, feat_shift).astype(
        jnp.bfloat16
    )
    entering = (product(normed_frames, proj_weight) + proj_bias).astype(jnp.bfloat16)
    entering = entering.reshape(MICRO, rows, columns)

    owner = lax.broadcasted_iota(jnp.int32, (rows, rows), 0) // frame_total
    column = lax.broadcasted_iota(jnp.int32, (rows, rows), 1) // frame_total
    maskings = jnp.where((owner == column)[None] & live.reshape(MICRO, 1, rows), 1.0, 0.0)
    gain = norm_gain.reshape(group, 1, columns)
    shift = norm_shift.reshape(group, 1, columns)
    query, key, value = (
        weight.reshape(group, columns, HEAD_DIM)
        for weight in (query_weight, key_weight, value_weight)
    )
    out_part = out_weight.reshape(group // 2, 2 * HEAD_DIM, columns)

    vmem = pl.BlockSpec(memory_space=pltpu.VMEM)
    mixing = pl.pallas_call(
        mixing_kernel,
        out_shape=jax.ShapeDtypeStruct((rows, HEAD_DIM), jnp.bfloat16),
        in_specs=[vmem] * 7,
        out_specs=vmem,
        compiler_params=pltpu.CompilerParams(vmem_limit_bytes=24 * 2**20),
    )
    leaving = pl.pallas_call(
        leaving_kernel,
        out_shape=jax.ShapeDtypeStruct((rows, columns), jnp.bfloat16),
        in_specs=[vmem] * 4,
        out_specs=vmem,
        compiler_params=pltpu.CompilerParams(vmem_limit_bytes=24 * 2**20),
    )

    def to_all(block, axes, size):
        copies = jnp.broadcast_to(block[None], (size,) + block.shape)
        return lax.all_to_all(copies, axes, 0, 0, tiled=True)

    def attend(current, masking):
        chip_blocks = to_all(current, "y", chips)
        blocks = lax.all_gather(chip_blocks, "core", axis=1, tiled=False)
        blocks = blocks.reshape(group, rows, columns)
        mixture = mixing(blocks, gain, shift, query, key, value, masking)
        mixed = to_all(mixture, ("y", "core"), group)
        return leaving(mixed, current, out_part, out_bias)

    def partial_gradients():
        own_lengths = lax.dynamic_slice_in_dim(lengths[0], chip * CORES + core, 1, 0)
        own_framed = framed_of(wave[0], own_lengths).astype(jnp.float32)
        own_live = live_of(own_lengths, frame_total)

        def frontend_at(weight, bias, gain, shift):
            return frontend(weight, bias, gain, shift, own_framed, own_live)

        _, pullback = jax.vjp(
            frontend_at, conv_weight.astype(jnp.float32), conv_bias, conv_gain, conv_shift
        )
        partial = pullback(feat_grad[0].astype(jnp.float32))
        packed = jnp.concatenate(
            [partial[0].T, partial[1][None], partial[2][None], partial[3][None]], axis=0
        )
        packed = jnp.pad(packed, ((0, 16 - packed.shape[0]), (0, 0)))
        return lax.psum(lax.psum(packed, "core"), "dp")

    gradient_tick = jnp.where(section >= sections // 2, 1, sections - 2)
    ticks = sections + MICRO - 1

    def advance(tick, state):
        previous, outputs, packed = state
        arrived = lax.ppermute(previous, "section", [(s, s + 1) for s in range(sections - 1)])
        piece = tick - section
        slot = jnp.clip(piece, 0, MICRO - 1)
        fresh = lax.dynamic_index_in_dim(entering, slot, 0, keepdims=False)
        current = jnp.where(section == 0, fresh, arrived)
        masking = lax.dynamic_index_in_dim(maskings, slot, 0, keepdims=False)
        kind = jnp.clip(tick - gradient_tick, -1, 2)
        kind = jnp.where((kind == 0) | (kind == 1), kind + 1, 0)
        result, packed = lax.switch(
            kind,
            [
                lambda: (attend(current, masking), packed),
                lambda: (current, partial_gradients()),
                lambda: (current, lax.psum(packed, "y")),
            ],
        )
        kept = lax.dynamic_index_in_dim(outputs, slot, 0, keepdims=False)
        has_work = (piece >= 0) & (piece < MICRO)
        outputs = lax.dynamic_update_index_in_dim(
            outputs, jnp.where(has_work, result, kept), slot, 0
        )
        return (result, outputs, packed)

    start = (
        jnp.zeros((rows, columns), jnp.bfloat16),
        jnp.zeros((MICRO, rows, columns), jnp.bfloat16),
        jnp.zeros((16, conv_bias.shape[0]), jnp.float32),
    )
    _, outputs, packed = lax.fori_loop(0, ticks, advance, start)
    return (
        outputs[None, None],
        packed[:KERNEL].T,
        packed[KERNEL],
        packed[KERNEL + 1],
        packed[KERNEL + 2],
    )


def solution(mesh):
    sizes = dict(mesh.shape)
    split = Mesh(
        mesh.devices.reshape(
            sizes["section"], sizes["seq"] // CORES, CORES, sizes["dp"]
        ),
        ("section", "y", "core", "dp"),
    )
    seq = ("y", "core")
    return jax.shard_map(
        on_device,
        mesh=split,
        in_specs=(
            P("dp", seq, None),
            P("dp", None),
            P("dp", None),
            P(),
            P(),
            P(),
            P(),
            P(),
            P(),
            P(None, seq),
            P(seq),
            P("section", None),
            P("section", None),
            P("section", None, seq),
            P("section", None, seq),
            P("section", None, seq),
            P("section", None, seq),
            P("section", seq),
            P("dp", seq, None, None),
        ),
        out_specs=(P("section", "dp", None, None, seq), P(), P(), P(), P()),
        check_vma=False,
    )
```

time: 563 us -> 420 us (0.75)
  the two profiles are of different devices: /device:TPU:449 before, /device:TPU:195 now
where the time goes in v3:
time: 420 us; the launch traced here: 417 us
  blocking collectives  175 us (42%)
  starting transfers between devices  95.7 us (23%)
  waiting for transfers between devices  82.3 us (20%)
  local copies, waits for them, and re-layouts  30.5 us (7%)
  other arithmetic  16.2 us (4%)
  Pallas kernels  11.7 us (3%)
    all_to_all x7, blocking collectives, to_all(): return lax.all_to_all(copies, axes, 0, 0, tiled=True)  103 us
    all_to_all x7, waiting for transfers between devices, to_all(): return lax.all_to_all(copies, axes, 0, 0, tiled=True)  75.1 us
    ppermute x9, starting transfers between devices, advance(): lax.ppermute(previous, 'section', [(s, s + 1) for s in range(sections - 1)])  67.4 us
    all_to_all x7, starting transfers between devices, to_all(): return lax.all_to_all(copies, axes, 0, 0, tiled=True)  28.3 us
    all_gather x7, blocking collectives, attend(): blocks = lax.all_gather(chip_blocks, 'core', axis=1, tiled=False)  20.6 us
    psum x1, blocking collectives, advance(): lax.psum(packed, 'y')  20.1 us
    all_gather x1, blocking collectives, on_device(): lax.all_gather(wave[0].astype(jnp.float32), ('y', 'core'), axis=0, tiled=...  17.9 us
    psum x2, blocking collectives, partial_gradients(): return lax.psum(lax.psum(packed, 'core'), 'dp')  14.1 us
  transfers between devices with their start and end apart: 16, of which 16 were waited for; matrix products, arithmetic and copies ran while one was open for 4% of the time, Pallas kernels for 0%

profile of v3, /device:TPU:195, one launch (start us, length us, event | category | flops | bytes accessed | tf_op | source)
XLA Modules:
  0.0 416.7 jit_solution(14434450037332972162)
XLA Ops:
  2.1 17.9 %all-gather.1 = f32[16,1,40]{2,1,0:T(1,128)S(1)} all-gather(f32[1,1,40]{2,1,0:T(1,128)S(1)} %convert_element_type.62), channel_id=3, replica_groups=mesh['section'=8,'y'=8,'core'=2,'dp'=4] {'y','core'}, dimensions={0}, use_global_device_ids=true | all-gather | bytes 2720 | tf_op jit(solution)/shard_map/all_gather | solution.py:120
  25.5 390.1 %while.19 = (s32[]{:T(128)}, bf16[64,256]{1,0:T(8,128)(2,1)S(1)}, bf16[2,64,256]{2,1,0:T(8,128)(2,1)}, f32[16,512]{1,0:T(8,128)S(1)}, s32[]{:T(128)}, /*index=5*...) while((s32[]{:T(128)}, bf16[64,256]{1,0:T(8,128)(2,1)S(1)}, ...), condition=%wide.region_20.21_spmd.clone, body=%wide.region_6.20_spmd.clone.sunk | while | flops 1089216 | bytes 12199514 | solution.py:230
  25.5 5.2 %collective-permute-start = (bf16[64,256]{1,0:T(8,128)(2,1)S(1)}, bf16[64,256]{1,0:T(8,128)(2,1)S(1)}, u32[]{:S(2)}, u32[]{:S(2)}) collective-permute-start(bf16[64,256]{1,0:T(8,128)(2,1)S(1)} %get-tuple-element.907), channel_id=1, source_target_pairs={{0,64},{64,128},{128,192},{192,256},{256,320},{320,384},{384,448},... | collective-permute-start | bytes 98312 | tf_op jit(solution)/shard_map/while/body/eval_jaxpr/ppermute | solution.py:202
  31.7 37.0 %conditional.3 = (bf16[64,256]{1,0:T(8,128)(2,1)S(1)}, f32[16,512]{1,0:T(8,128)S(1)}) conditional(s32[]{:T(128)} %clamp.10, (bf16[64,256]{1,0:T(8,128)(2,1)S(1)}, pred[64,64]{1,0:T(8,128)(4,1)}, s32[]{:T(128)}, f32[16,1,256]{2,1,0:T(1,128)}, f32[16,1,256]{2,1,0:T(1,128)}, /*index=5*/bf16[16,256,128]{2,1,0:T(8,128)(2,1)S(1)}, ...), branch_computations={%region_7.7_spmd, %region_8.17_spmd, %region_18.19_spmd} | conditional | flops 1056431 | bytes 11280768 | solution.py:210
  32.5 4.0 all-to-all-start
  37.8 8.9 %all-to-all-done = bf16[8,64,256]{2,1,0:T(8,128)(2,1)} async-done(((bf16[8,64,256]{2,1,0:T(8,128)(2,1)}), bf16[8,64,256]{2,1,0:T(8,128)(2,1)}, u32[]{:S(2)}, u32[]{:S(2)}) %all-to-all-start) | async-done | bytes 262176 | tf_op jit(solution)/shard_map/while/body/eval_jaxpr/cond/branch_0_fun/all_to_all | solution.py:169
  46.7 4.9 %all-gather = bf16[8,128,256]{2,1,0:T(8,128)(2,1)S(1)} all-gather(bf16[8,64,256]{2,1,0:T(8,128)(2,1)} %all-to-all-done), channel_id=2, replica_groups=mesh['section'=8,'y'=8,'core'=2,'dp'=4] {'core'}, dimensions={1}, use_global_device_ids=true | all-gather | bytes 786432 | tf_op jit(solution)/shard_map/while/body/eval_jaxpr/cond/branch_0_fun/all_gather | solution.py:173
  53.0 14.6 %all_to_all.8.mixed = bf16[16,64,128]{2,1,0:T(8,128)(2,1)S(1)} all-to-all(bf16[16,64,128]{2,1,0:T(8,128)(2,1)S(1)} %broadcast_in_dim.77), channel_id=1, replica_groups=mesh['section'=8,'y'=8,'core'=2,'dp'=4] {'y','core'}, dimensions={0} | all-to-all | bytes 524288 | tf_op jit(solution)/shard_map/while/body/eval_jaxpr/cond/branch_0_fun/all_to_all | solution.py:169
  69.5 4.8 %collective-permute-start = (bf16[64,256]{1,0:T(8,128)(2,1)S(1)}, bf16[64,256]{1,0:T(8,128)(2,1)S(1)}, u32[]{:S(2)}, u32[]{:S(2)}) collective-permute-start(bf16[64,256]{1,0:T(8,128)(2,1)S(1)} %get-tuple-element.907), channel_id=1, source_target_pairs={{0,64},{64,128},{128,192},{192,256},{256,320},{320,384},{384,448},... | collective-permute-start | bytes 98312 | tf_op jit(solution)/shard_map/while/body/eval_jaxpr/ppermute | solution.py:202
  75.4 36.9 %conditional.3 = (bf16[64,256]{1,0:T(8,128)(2,1)S(1)}, f32[16,512]{1,0:T(8,128)S(1)}) conditional(s32[]{:T(128)} %clamp.10, (bf16[64,256]{1,0:T(8,128)(2,1)S(1)}, pred[64,64]{1,0:T(8,128)(4,1)}, s32[]{:T(128)}, f32[16,1,256]{2,1,0:T(1,128)}, f32[16,1,256]{2,1,0:T(1,128)}, /*index=5*/bf16[16,256,128]{2,1,0:T(8,128)(2,1)S(1)}, ...), branch_computations={%region_7.7_spmd, %region_8.17_spmd, %region_18.19_spmd} | conditional | flops 1056431 | bytes 11280768 | solution.py:210
  76.2 4.0 all-to-all-start
  81.5 11.0 %all-to-all-done = bf16[8,64,256]{2,1,0:T(8,128)(2,1)} async-done(((bf16[8,64,256]{2,1,0:T(8,128)(2,1)}), bf16[8,64,256]{2,1,0:T(8,128)(2,1)}, u32[]{:S(2)}, u32[]{:S(2)}) %all-to-all-start) | async-done | bytes 262176 | tf_op jit(solution)/shard_map/while/body/eval_jaxpr/cond/branch_0_fun/all_to_all | solution.py:169
  92.6 2.6 all-gather
  96.6 14.6 %all_to_all.8.mixed = bf16[16,64,128]{2,1,0:T(8,128)(2,1)S(1)} all-to-all(bf16[16,64,128]{2,1,0:T(8,128)(2,1)S(1)} %broadcast_in_dim.77), channel_id=1, replica_groups=mesh['section'=8,'y'=8,'core'=2,'dp'=4] {'y','core'}, dimensions={0} | all-to-all | bytes 524288 | tf_op jit(solution)/shard_map/while/body/eval_jaxpr/cond/branch_0_fun/all_to_all | solution.py:169
  118.1 36.9 %conditional.3 = (bf16[64,256]{1,0:T(8,128)(2,1)S(1)}, f32[16,512]{1,0:T(8,128)S(1)}) conditional(s32[]{:T(128)} %clamp.10, (bf16[64,256]{1,0:T(8,128)(2,1)S(1)}, pred[64,64]{1,0:T(8,128)(4,1)}, s32[]{:T(128)}, f32[16,1,256]{2,1,0:T(1,128)}, f32[16,1,256]{2,1,0:T(1,128)}, /*index=5*/bf16[16,256,128]{2,1,0:T(8,128)(2,1)S(1)}, ...), branch_computations={%region_7.7_spmd, %region_8.17_spmd, %region_18.19_spmd} | conditional | flops 1056431 | bytes 11280768 | solution.py:210
  118.8 4.0 all-to-all-start
  124.2 11.0 %all-to-all-done = bf16[8,64,256]{2,1,0:T(8,128)(2,1)} async-done(((bf16[8,64,256]{2,1,0:T(8,128)(2,1)}), bf16[8,64,256]{2,1,0:T(8,128)(2,1)}, u32[]{:S(2)}, u32[]{:S(2)}) %all-to-all-start) | async-done | bytes 262176 | tf_op jit(solution)/shard_map/while/body/eval_jaxpr/cond/branch_0_fun/all_to_all | solution.py:169
  135.2 2.6 all-gather
  139.3 14.6 %all_to_all.8.mixed = bf16[16,64,128]{2,1,0:T(8,128)(2,1)S(1)} all-to-all(bf16[16,64,128]{2,1,0:T(8,128)(2,1)S(1)} %broadcast_in_dim.77), channel_id=1, replica_groups=mesh['section'=8,'y'=8,'core'=2,'dp'=4] {'y','core'}, dimensions={0} | all-to-all | bytes 524288 | tf_op jit(solution)/shard_map/while/body/eval_jaxpr/cond/branch_0_fun/all_to_all | solution.py:169
  160.7 36.9 %conditional.3 = (bf16[64,256]{1,0:T(8,128)(2,1)S(1)}, f32[16,512]{1,0:T(8,128)S(1)}) conditional(s32[]{:T(128)} %clamp.10, (bf16[64,256]{1,0:T(8,128)(2,1)S(1)}, pred[64,64]{1,0:T(8,128)(4,1)}, s32[]{:T(128)}, f32[16,1,256]{2,1,0:T(1,128)}, f32[16,1,256]{2,1,0:T(1,128)}, /*index=5*/bf16[16,256,128]{2,1,0:T(8,128)(2,1)S(1)}, ...), branch_computations={%region_7.7_spmd, %region_8.17_spmd, %region_18.19_spmd} | conditional | flops 1056431 | bytes 11280768 | solution.py:210
  161.5 4.0 all-to-all-start
  166.9 11.0 %all-to-all-done = bf16[8,64,256]{2,1,0:T(8,128)(2,1)} async-done(((bf16[8,64,256]{2,1,0:T(8,128)(2,1)}), bf16[8,64,256]{2,1,0:T(8,128)(2,1)}, u32[]{:S(2)}, u32[]{:S(2)}) %all-to-all-start) | async-done | bytes 262176 | tf_op jit(solution)/shard_map/while/body/eval_jaxpr/cond/branch_0_fun/all_to_all | solution.py:169
  177.9 2.6 all-gather
  182.0 14.6 %all_to_all.8.mixed = bf16[16,64,128]{2,1,0:T(8,128)(2,1)S(1)} all-to-all(bf16[16,64,128]{2,1,0:T(8,128)(2,1)S(1)} %broadcast_in_dim.77), channel_id=1, replica_groups=mesh['section'=8,'y'=8,'core'=2,'dp'=4] {'y','core'}, dimensions={0} | all-to-all | bytes 524288 | tf_op jit(solution)/shard_map/while/body/eval_jaxpr/cond/branch_0_fun/all_to_all | solution.py:169
  198.5 2.8 collective-permute-start
  203.4 36.9 %conditional.3 = (bf16[64,256]{1,0:T(8,128)(2,1)S(1)}, f32[16,512]{1,0:T(8,128)S(1)}) conditional(s32[]{:T(128)} %clamp.10, (bf16[64,256]{1,0:T(8,128)(2,1)S(1)}, pred[64,64]{1,0:T(8,128)(4,1)}, s32[]{:T(128)}, f32[16,1,256]{2,1,0:T(1,128)}, f32[16,1,256]{2,1,0:T(1,128)}, /*index=5*/bf16[16,256,128]{2,1,0:T(8,128)(2,1)S(1)}, ...), branch_computations={%region_7.7_spmd, %region_8.17_spmd, %region_18.19_spmd} | conditional | flops 1056431 | bytes 11280768 | solution.py:210
  204.2 4.0 all-to-all-start
  209.5 11.0 %all-to-all-done = bf16[8,64,256]{2,1,0:T(8,128)(2,1)} async-done(((bf16[8,64,256]{2,1,0:T(8,128)(2,1)}), bf16[8,64,256]{2,1,0:T(8,128)(2,1)}, u32[]{:S(2)}, u32[]{:S(2)}) %all-to-all-start) | async-done | bytes 262176 | tf_op jit(solution)/shard_map/while/body/eval_jaxpr/cond/branch_0_fun/all_to_all | solution.py:169
  220.5 2.6 all-gather
  224.6 14.6 %all_to_all.8.mixed = bf16[16,64,128]{2,1,0:T(8,128)(2,1)S(1)} all-to-all(bf16[16,64,128]{2,1,0:T(8,128)(2,1)S(1)} %broadcast_in_dim.77), channel_id=1, replica_groups=mesh['section'=8,'y'=8,'core'=2,'dp'=4] {'y','core'}, dimensions={0} | all-to-all | bytes 524288 | tf_op jit(solution)/shard_map/while/body/eval_jaxpr/cond/branch_0_fun/all_to_all | solution.py:169
  241.1 4.0 collective-permute-start
  246.2 36.9 %conditional.3 = (bf16[64,256]{1,0:T(8,128)(2,1)S(1)}, f32[16,512]{1,0:T(8,128)S(1)}) conditional(s32[]{:T(128)} %clamp.10, (bf16[64,256]{1,0:T(8,128)(2,1)S(1)}, pred[64,64]{1,0:T(8,128)(4,1)}, s32[]{:T(128)}, f32[16,1,256]{2,1,0:T(1,128)}, f32[16,1,256]{2,1,0:T(1,128)}, /*index=5*/bf16[16,256,128]{2,1,0:T(8,128)(2,1)S(1)}, ...), branch_computations={%region_7.7_spmd, %region_8.17_spmd, %region_18.19_spmd} | conditional | flops 1056431 | bytes 11280768 | solution.py:210
  247.0 4.0 all-to-all-start
  252.3 11.0 %all-to-all-done = bf16[8,64,256]{2,1,0:T(8,128)(2,1)} async-done(((bf16[8,64,256]{2,1,0:T(8,128)(2,1)}), bf16[8,64,256]{2,1,0:T(8,128)(2,1)}, u32[]{:S(2)}, u32[]{:S(2)}) %all-to-all-start) | async-done | bytes 262176 | tf_op jit(solution)/shard_map/while/body/eval_jaxpr/cond/branch_0_fun/all_to_all | solution.py:169
  263.4 2.6 all-gather
  267.4 14.6 %all_to_all.8.mixed = bf16[16,64,128]{2,1,0:T(8,128)(2,1)S(1)} all-to-all(bf16[16,64,128]{2,1,0:T(8,128)(2,1)S(1)} %broadcast_in_dim.77), channel_id=1, replica_groups=mesh['section'=8,'y'=8,'core'=2,'dp'=4] {'y','core'}, dimensions={0} | all-to-all | bytes 524288 | tf_op jit(solution)/shard_map/while/body/eval_jaxpr/cond/branch_0_fun/all_to_all | solution.py:169
  283.9 5.1 %collective-permute-start = (bf16[64,256]{1,0:T(8,128)(2,1)S(1)}, bf16[64,256]{1,0:T(8,128)(2,1)S(1)}, u32[]{:S(2)}, u32[]{:S(2)}) collective-permute-start(bf16[64,256]{1,0:T(8,128)(2,1)S(1)} %get-tuple-element.907), channel_id=1, source_target_pairs={{0,64},{64,128},{128,192},{192,256},{256,320},{320,384},{384,448},... | collective-permute-start | bytes 98312 | tf_op jit(solution)/shard_map/while/body/eval_jaxpr/ppermute | solution.py:202
  290.1 22.3 %conditional.3 = (bf16[64,256]{1,0:T(8,128)(2,1)S(1)}, f32[16,512]{1,0:T(8,128)S(1)}) conditional(s32[]{:T(128)} %clamp.10, (bf16[64,256]{1,0:T(8,128)(2,1)S(1)}, pred[64,64]{1,0:T(8,128)(4,1)}, s32[]{:T(128)}, f32[16,1,256]{2,1,0:T(1,128)}, f32[16,1,256]{2,1,0:T(1,128)}, /*index=5*/bf16[16,256,128]{2,1,0:T(8,128)(2,1)S(1)}, ...), branch_computations={%region_7.7_spmd, %region_8.17_spmd, %region_18.19_spmd} | conditional | flops 1056431 | bytes 11280768 | solution.py:210
  298.3 3.4 psum.18
  301.7 10.7 %psum.19 = f32[16,512]{1,0:T(8,128)S(1)} all-reduce(f32[16,512]{1,0:T(8,128)S(1)} %psum.18), channel_id=1, replica_groups=mesh['section'=8,'y'=8,'core'=2,'dp'=4] {'dp'}, use_global_device_ids=true, to_apply=%region_17.16 | all-reduce | flops 8192 | bytes 65536 | tf_op jit(solution)/shard_map/while/body/eval_jaxpr/cond/branch_1_fun/psum | solution.py:195
  313.3 19.7 %collective-permute-start = (bf16[64,256]{1,0:T(8,128)(2,1)S(1)}, bf16[64,256]{1,0:T(8,128)(2,1)S(1)}, u32[]{:S(2)}, u32[]{:S(2)}) collective-permute-start(bf16[64,256]{1,0:T(8,128)(2,1)S(1)} %get-tuple-element.907), channel_id=1, source_target_pairs={{0,64},{64,128},{128,192},{192,256},{256,320},{320,384},{384,448},... | collective-permute-start | bytes 98312 | tf_op jit(solution)/shard_map/while/body/eval_jaxpr/ppermute | solution.py:202
  333.9 20.2 %conditional.3 = (bf16[64,256]{1,0:T(8,128)(2,1)S(1)}, f32[16,512]{1,0:T(8,128)S(1)}) conditional(s32[]{:T(128)} %clamp.10, (bf16[64,256]{1,0:T(8,128)(2,1)S(1)}, pred[64,64]{1,0:T(8,128)(4,1)}, s32[]{:T(128)}, f32[16,1,256]{2,1,0:T(1,128)}, f32[16,1,256]{2,1,0:T(1,128)}, /*index=5*/bf16[16,256,128]{2,1,0:T(8,128)(2,1)S(1)}, ...), branch_computations={%region_7.7_spmd, %region_8.17_spmd, %region_18.19_spmd} | conditional | flops 1056431 | bytes 11280768 | solution.py:210
  334.0 20.1 %psum.20 = f32[16,512]{1,0:T(8,128)S(1)} all-reduce(f32[16,512]{1,0:T(8,128)S(1)} %get-tuple-element.530), channel_id=1, replica_groups=mesh['section'=8,'y'=8,'core'=2,'dp'=4] {'y'}, use_global_device_ids=true, to_apply=%region_19.18 | all-reduce | flops 8192 | bytes 65536 | tf_op jit(solution)/shard_map/while/body/eval_jaxpr/cond/branch_2_fun/psum | solution.py:215
  355.0 21.8 %collective-permute-start = (bf16[64,256]{1,0:T(8,128)(2,1)S(1)}, bf16[64,256]{1,0:T(8,128)(2,1)S(1)}, u32[]{:S(2)}, u32[]{:S(2)}) collective-permute-start(bf16[64,256]{1,0:T(8,128)(2,1)S(1)} %get-tuple-element.907), channel_id=1, source_target_pairs={{0,64},{64,128},{128,192},{192,256},{256,320},{320,384},{384,448},... | collective-permute-start | bytes 98312 | tf_op jit(solution)/shard_map/while/body/eval_jaxpr/ppermute | solution.py:202
  377.8 36.9 %conditional.3 = (bf16[64,256]{1,0:T(8,128)(2,1)S(1)}, f32[16,512]{1,0:T(8,128)S(1)}) conditional(s32[]{:T(128)} %clamp.10, (bf16[64,256]{1,0:T(8,128)(2,1)S(1)}, pred[64,64]{1,0:T(8,128)(4,1)}, s32[]{:T(128)}, f32[16,1,256]{2,1,0:T(1,128)}, f32[16,1,256]{2,1,0:T(1,128)}, /*index=5*/bf16[16,256,128]{2,1,0:T(8,128)(2,1)S(1)}, ...), branch_computations={%region_7.7_spmd, %region_8.17_spmd, %region_18.19_spmd} | conditional | flops 1056431 | bytes 11280768 | solution.py:210
  378.6 4.0 all-to-all-start
  383.9 11.0 %all-to-all-done = bf16[8,64,256]{2,1,0:T(8,128)(2,1)} async-done(((bf16[8,64,256]{2,1,0:T(8,128)(2,1)}), bf16[8,64,256]{2,1,0:T(8,128)(2,1)}, u32[]{:S(2)}, u32[]{:S(2)}) %all-to-all-start) | async-done | bytes 262176 | tf_op jit(solution)/shard_map/while/body/eval_jaxpr/cond/branch_0_fun/all_to_all | solution.py:169
  399.0 14.6 %all_to_all.8.mixed = bf16[16,64,128]{2,1,0:T(8,128)(2,1)S(1)} all-to-all(bf16[16,64,128]{2,1,0:T(8,128)(2,1)S(1)} %broadcast_in_dim.77), channel_id=1, replica_groups=mesh['section'=8,'y'=8,'core'=2,'dp'=4] {'y','core'}, dimensions={0} | all-to-all | bytes 524288 | tf_op jit(solution)/shard_map/while/body/eval_jaxpr/cond/branch_0_fun/all_to_all | solution.py:169
  (287 shorter events, 73.1 us)
Async XLA Ops:
  0.6 22.2 %copy-start = (bf16[512,256]{1,0:T(8,128)(2,1)S(1)}, bf16[512,256]{1,0:T(8,128)(2,1)}, u32[]{:S(2)}) copy-start(bf16[512,256]{1,0:T(8,128)(2,1)} %param.33) | copy-start | bytes 786436
  21.1 4.4 %copy-start.1 = (bf16[1,4096,128]{2,1,0:T(8,128)(2,1)S(1)}, bf16[1,4096,128]{2,1,0:T(8,128)(2,1)}, u32[]{:S(2)}) copy-start(bf16[1,4096,128]{2,1,0:T(8,128)(2,1)} %param.37) | copy-start | bytes 3145732
  21.1 4.4 %copy-start.2 = (bf16[1,4096,128]{2,1,0:T(8,128)(2,1)S(1)}, bf16[1,4096,128]{2,1,0:T(8,128)(2,1)}, u32[]{:S(2)}) copy-start(bf16[1,4096,128]{2,1,0:T(8,128)(2,1)} %param.38) | copy-start | bytes 3145732
  25.5 6.2 %copy-start.8 = (bf16[2,64,256]{2,1,0:T(8,128)(2,1)}, bf16[2,64,256]{2,1,0:T(8,128)(2,1)S(1)}, u32[]{:S(2)}) copy-start(bf16[2,64,256]{2,1,0:T(8,128)(2,1)S(1)} %get-tuple-element.943) | copy-start | bytes 196612 | tf_op jit(solution)/shard_map/while
  25.5 6.2 %collective-permute-start = (bf16[64,256]{1,0:T(8,128)(2,1)S(1)}, bf16[64,256]{1,0:T(8,128)(2,1)S(1)}, u32[]{:S(2)}, u32[]{:S(2)}) collective-permute-start(bf16[64,256]{1,0:T(8,128)(2,1)S(1)} %get-tuple-element.907), channel_id=1, source_target_pairs={{0,64},{64,128},{128,192},{192,256},{256,320},{320,384},{384,448},... | collective-permute-start | bytes 98312 | tf_op jit(solution)/shard_map/while/body/eval_jaxpr/ppermute | solution.py:202
  31.7 19.9 %copy-start.3 = (bf16[16,256,128]{2,1,0:T(8,128)(2,1)S(1)}, bf16[16,256,128]{2,1,0:T(8,128)(2,1)}, u32[]{:S(2)}) copy-start(bf16[16,256,128]{2,1,0:T(8,128)(2,1)} %get-tuple-element.513.value) | copy-start | bytes 3145732 | tf_op jit(solution)/shard_map/while/body/eval_jaxpr/cond
  32.5 14.2 %all-to-all-start = ((bf16[8,64,256]{2,1,0:T(8,128)(2,1)}), bf16[8,64,256]{2,1,0:T(8,128)(2,1)}, u32[]{:S(2)}, u32[]{:S(2)}) async-start(bf16[8,64,256]{2,1,0:T(8,128)(2,1)} %broadcast_in_dim.76), calls=%async_computation | async-start | bytes 524288 | tf_op jit(solution)/shard_map/while/body/eval_jaxpr/cond/branch_0_fun/all_to_all | solution.py:169
  46.7 4.9 %copy-start.6 = (f32[16,1,256]{2,1,0:T(1,128)S(1)}, f32[16,1,256]{2,1,0:T(1,128)}, u32[]{:S(2)}) copy-start(f32[16,1,256]{2,1,0:T(1,128)} %get-tuple-element.509.gain) | copy-start | bytes 49156 | tf_op jit(solution)/shard_map/while/body/eval_jaxpr/cond
  46.7 4.9 %copy-start.7 = (f32[16,1,256]{2,1,0:T(1,128)S(1)}, f32[16,1,256]{2,1,0:T(1,128)}, u32[]{:S(2)}) copy-start(f32[16,1,256]{2,1,0:T(1,128)} %get-tuple-element.510.shift) | copy-start | bytes 49156 | tf_op jit(solution)/shard_map/while/body/eval_jaxpr/cond
  51.6 16.1 %copy-start.4 = (bf16[8,256,256]{2,1,0:T(8,128)(2,1)S(1)}, bf16[8,256,256]{2,1,0:T(8,128)(2,1)}, u32[]{:S(2)}) copy-start(bf16[8,256,256]{2,1,0:T(8,128)(2,1)} %get-tuple-element.516.weights) | copy-start | bytes 3145732 | tf_op jit(solution)/shard_map/while/body/eval_jaxpr/cond
  69.5 5.9 %copy-start.8 = (bf16[2,64,256]{2,1,0:T(8,128)(2,1)}, bf16[2,64,256]{2,1,0:T(8,128)(2,1)S(1)}, u32[]{:S(2)}) copy-start(bf16[2,64,256]{2,1,0:T(8,128)(2,1)S(1)} %get-tuple-element.943) | copy-start | bytes 196612 | tf_op jit(solution)/shard_map/while
  69.5 5.9 %collective-permute-start = (bf16[64,256]{1,0:T(8,128)(2,1)S(1)}, bf16[64,256]{1,0:T(8,128)(2,1)S(1)}, u32[]{:S(2)}, u32[]{:S(2)}) collective-permute-start(bf16[64,256]{1,0:T(8,128)(2,1)S(1)} %get-tuple-element.907), channel_id=1, source_target_pairs={{0,64},{64,128},{128,192},{192,256},{256,320},{320,384},{384,448},... | collective-permute-start | bytes 98312 | tf_op jit(solution)/shard_map/while/body/eval_jaxpr/ppermute | solution.py:202
  75.4 19.8 %copy-start.3 = (bf16[16,256,128]{2,1,0:T(8,128)(2,1)S(1)}, bf16[16,256,128]{2,1,0:T(8,128)(2,1)}, u32[]{:S(2)}) copy-start(bf16[16,256,128]{2,1,0:T(8,128)(2,1)} %get-tuple-element.513.value) | copy-start | bytes 3145732 | tf_op jit(solution)/shard_map/while/body/eval_jaxpr/cond
  76.2 16.4 %all-to-all-start = ((bf16[8,64,256]{2,1,0:T(8,128)(2,1)}), bf16[8,64,256]{2,1,0:T(8,128)(2,1)}, u32[]{:S(2)}, u32[]{:S(2)}) async-start(bf16[8,64,256]{2,1,0:T(8,128)(2,1)} %broadcast_in_dim.76), calls=%async_computation | async-start | bytes 524288 | tf_op jit(solution)/shard_map/while/body/eval_jaxpr/cond/branch_0_fun/all_to_all | solution.py:169
  95.2 16.1 %copy-start.4 = (bf16[8,256,256]{2,1,0:T(8,128)(2,1)S(1)}, bf16[8,256,256]{2,1,0:T(8,128)(2,1)}, u32[]{:S(2)}) copy-start(bf16[8,256,256]{2,1,0:T(8,128)(2,1)} %get-tuple-element.516.weights) | copy-start | bytes 3145732 | tf_op jit(solution)/shard_map/while/body/eval_jaxpr/cond
  113.1 4.9 %copy-start.8 = (bf16[2,64,256]{2,1,0:T(8,128)(2,1)}, bf16[2,64,256]{2,1,0:T(8,128)(2,1)S(1)}, u32[]{:S(2)}) copy-start(bf16[2,64,256]{2,1,0:T(8,128)(2,1)S(1)} %get-tuple-element.943) | copy-start | bytes 196612 | tf_op jit(solution)/shard_map/while
  113.1 4.9 %collective-permute-start = (bf16[64,256]{1,0:T(8,128)(2,1)S(1)}, bf16[64,256]{1,0:T(8,128)(2,1)S(1)}, u32[]{:S(2)}, u32[]{:S(2)}) collective-permute-start(bf16[64,256]{1,0:T(8,128)(2,1)S(1)} %get-tuple-element.907), channel_id=1, source_target_pairs={{0,64},{64,128},{128,192},{192,256},{256,320},{320,384},{384,448},... | collective-permute-start | bytes 98312 | tf_op jit(solution)/shard_map/while/body/eval_jaxpr/ppermute | solution.py:202
  118.1 19.8 %copy-start.3 = (bf16[16,256,128]{2,1,0:T(8,128)(2,1)S(1)}, bf16[16,256,128]{2,1,0:T(8,128)(2,1)}, u32[]{:S(2)}) copy-start(bf16[16,256,128]{2,1,0:T(8,128)(2,1)} %get-tuple-element.513.value) | copy-start | bytes 3145732 | tf_op jit(solution)/shard_map/while/body/eval_jaxpr/cond
  118.8 16.4 %all-to-all-start = ((bf16[8,64,256]{2,1,0:T(8,128)(2,1)}), bf16[8,64,256]{2,1,0:T(8,128)(2,1)}, u32[]{:S(2)}, u32[]{:S(2)}) async-start(bf16[8,64,256]{2,1,0:T(8,128)(2,1)} %broadcast_in_dim.76), calls=%async_computation | async-start | bytes 524288 | tf_op jit(solution)/shard_map/while/body/eval_jaxpr/cond/branch_0_fun/all_to_all | solution.py:169
  135.2 2.6 copy-start.7
  137.9 16.1 %copy-start.4 = (bf16[8,256,256]{2,1,0:T(8,128)(2,1)S(1)}, bf16[8,256,256]{2,1,0:T(8,128)(2,1)}, u32[]{:S(2)}) copy-start(bf16[8,256,256]{2,1,0:T(8,128)(2,1)} %get-tuple-element.516.weights) | copy-start | bytes 3145732 | tf_op jit(solution)/shard_map/while/body/eval_jaxpr/cond
  155.8 4.9 %copy-start.8 = (bf16[2,64,256]{2,1,0:T(8,128)(2,1)}, bf16[2,64,256]{2,1,0:T(8,128)(2,1)S(1)}, u32[]{:S(2)}) copy-start(bf16[2,64,256]{2,1,0:T(8,128)(2,1)S(1)} %get-tuple-element.943) | copy-start | bytes 196612 | tf_op jit(solution)/shard_map/while
  155.8 4.9 %collective-permute-start = (bf16[64,256]{1,0:T(8,128)(2,1)S(1)}, bf16[64,256]{1,0:T(8,128)(2,1)S(1)}, u32[]{:S(2)}, u32[]{:S(2)}) collective-permute-start(bf16[64,256]{1,0:T(8,128)(2,1)S(1)} %get-tuple-element.907), channel_id=1, source_target_pairs={{0,64},{64,128},{128,192},{192,256},{256,320},{320,384},{384,448},... | collective-permute-start | bytes 98312 | tf_op jit(solution)/shard_map/while/body/eval_jaxpr/ppermute | solution.py:202
  160.8 19.8 %copy-start.3 = (bf16[16,256,128]{2,1,0:T(8,128)(2,1)S(1)}, bf16[16,256,128]{2,1,0:T(8,128)(2,1)}, u32[]{:S(2)}) copy-start(bf16[16,256,128]{2,1,0:T(8,128)(2,1)} %get-tuple-element.513.value) | copy-start | bytes 3145732 | tf_op jit(solution)/shard_map/while/body/eval_jaxpr/cond
  161.5 16.4 %all-to-all-start = ((bf16[8,64,256]{2,1,0:T(8,128)(2,1)}), bf16[8,64,256]{2,1,0:T(8,128)(2,1)}, u32[]{:S(2)}, u32[]{:S(2)}) async-start(bf16[8,64,256]{2,1,0:T(8,128)(2,1)} %broadcast_in_dim.76), calls=%async_computation | async-start | bytes 524288 | tf_op jit(solution)/shard_map/while/body/eval_jaxpr/cond/branch_0_fun/all_to_all | solution.py:169
  177.9 2.6 copy-start.6
  177.9 2.6 copy-start.7
  180.5 16.1 %copy-start.4 = (bf16[8,256,256]{2,1,0:T(8,128)(2,1)S(1)}, bf16[8,256,256]{2,1,0:T(8,128)(2,1)}, u32[]{:S(2)}) copy-start(bf16[8,256,256]{2,1,0:T(8,128)(2,1)} %get-tuple-element.516.weights) | copy-start | bytes 3145732 | tf_op jit(solution)/shard_map/while/body/eval_jaxpr/cond
  198.5 4.9 %copy-start.8 = (bf16[2,64,256]{2,1,0:T(8,128)(2,1)}, bf16[2,64,256]{2,1,0:T(8,128)(2,1)S(1)}, u32[]{:S(2)}) copy-start(bf16[2,64,256]{2,1,0:T(8,128)(2,1)S(1)} %get-tuple-element.943) | copy-start | bytes 196612 | tf_op jit(solution)/shard_map/while
  198.5 4.9 %collective-permute-start = (bf16[64,256]{1,0:T(8,128)(2,1)S(1)}, bf16[64,256]{1,0:T(8,128)(2,1)S(1)}, u32[]{:S(2)}, u32[]{:S(2)}) collective-permute-start(bf16[64,256]{1,0:T(8,128)(2,1)S(1)} %get-tuple-element.907), channel_id=1, source_target_pairs={{0,64},{64,128},{128,192},{192,256},{256,320},{320,384},{384,448},... | collective-permute-start | bytes 98312 | tf_op jit(solution)/shard_map/while/body/eval_jaxpr/ppermute | solution.py:202
  203.4 19.8 %copy-start.3 = (bf16[16,256,128]{2,1,0:T(8,128)(2,1)S(1)}, bf16[16,256,128]{2,1,0:T(8,128)(2,1)}, u32[]{:S(2)}) copy-start(bf16[16,256,128]{2,1,0:T(8,128)(2,1)} %get-tuple-element.513.value) | copy-start | bytes 3145732 | tf_op jit(solution)/shard_map/while/body/eval_jaxpr/cond
  204.2 16.4 %all-to-all-start = ((bf16[8,64,256]{2,1,0:T(8,128)(2,1)}), bf16[8,64,256]{2,1,0:T(8,128)(2,1)}, u32[]{:S(2)}, u32[]{:S(2)}) async-start(bf16[8,64,256]{2,1,0:T(8,128)(2,1)} %broadcast_in_dim.76), calls=%async_computation | async-start | bytes 524288 | tf_op jit(solution)/shard_map/while/body/eval_jaxpr/cond/branch_0_fun/all_to_all | solution.py:169
  220.5 2.6 copy-start.7
  223.2 16.1 %copy-start.4 = (bf16[8,256,256]{2,1,0:T(8,128)(2,1)S(1)}, bf16[8,256,256]{2,1,0:T(8,128)(2,1)}, u32[]{:S(2)}) copy-start(bf16[8,256,256]{2,1,0:T(8,128)(2,1)} %get-tuple-element.516.weights) | copy-start | bytes 3145732 | tf_op jit(solution)/shard_map/while/body/eval_jaxpr/cond
  241.1 5.1 %copy-start.8 = (bf16[2,64,256]{2,1,0:T(8,128)(2,1)}, bf16[2,64,256]{2,1,0:T(8,128)(2,1)S(1)}, u32[]{:S(2)}) copy-start(bf16[2,64,256]{2,1,0:T(8,128)(2,1)S(1)} %get-tuple-element.943) | copy-start | bytes 196612 | tf_op jit(solution)/shard_map/while
  241.1 5.1 %collective-permute-start = (bf16[64,256]{1,0:T(8,128)(2,1)S(1)}, bf16[64,256]{1,0:T(8,128)(2,1)S(1)}, u32[]{:S(2)}, u32[]{:S(2)}) collective-permute-start(bf16[64,256]{1,0:T(8,128)(2,1)S(1)} %get-tuple-element.907), channel_id=1, source_target_pairs={{0,64},{64,128},{128,192},{192,256},{256,320},{320,384},{384,448},... | collective-permute-start | bytes 98312 | tf_op jit(solution)/shard_map/while/body/eval_jaxpr/ppermute | solution.py:202
  246.2 19.8 %copy-start.3 = (bf16[16,256,128]{2,1,0:T(8,128)(2,1)S(1)}, bf16[16,256,128]{2,1,0:T(8,128)(2,1)}, u32[]{:S(2)}) copy-start(bf16[16,256,128]{2,1,0:T(8,128)(2,1)} %get-tuple-element.513.value) | copy-start | bytes 3145732 | tf_op jit(solution)/shard_map/while/body/eval_jaxpr/cond
  247.0 16.4 %all-to-all-start = ((bf16[8,64,256]{2,1,0:T(8,128)(2,1)}), bf16[8,64,256]{2,1,0:T(8,128)(2,1)}, u32[]{:S(2)}, u32[]{:S(2)}) async-start(bf16[8,64,256]{2,1,0:T(8,128)(2,1)} %broadcast_in_dim.76), calls=%async_computation | async-start | bytes 524288 | tf_op jit(solution)/shard_map/while/body/eval_jaxpr/cond/branch_0_fun/all_to_all | solution.py:169
  266.0 16.1 %copy-start.4 = (bf16[8,256,256]{2,1,0:T(8,128)(2,1)S(1)}, bf16[8,256,256]{2,1,0:T(8,128)(2,1)}, u32[]{:S(2)}) copy-start(bf16[8,256,256]{2,1,0:T(8,128)(2,1)} %get-tuple-element.516.weights) | copy-start | bytes 3145732 | tf_op jit(solution)/shard_map/while/body/eval_jaxpr/cond
  283.9 6.2 %copy-start.8 = (bf16[2,64,256]{2,1,0:T(8,128)(2,1)}, bf16[2,64,256]{2,1,0:T(8,128)(2,1)S(1)}, u32[]{:S(2)}) copy-start(bf16[2,64,256]{2,1,0:T(8,128)(2,1)S(1)} %get-tuple-element.943) | copy-start | bytes 196612 | tf_op jit(solution)/shard_map/while
  283.9 6.1 %collective-permute-start = (bf16[64,256]{1,0:T(8,128)(2,1)S(1)}, bf16[64,256]{1,0:T(8,128)(2,1)S(1)}, u32[]{:S(2)}, u32[]{:S(2)}) collective-permute-start(bf16[64,256]{1,0:T(8,128)(2,1)S(1)} %get-tuple-element.907), channel_id=1, source_target_pairs={{0,64},{64,128},{128,192},{192,256},{256,320},{320,384},{384,448},... | collective-permute-start | bytes 98312 | tf_op jit(solution)/shard_map/while/body/eval_jaxpr/ppermute | solution.py:202
  313.3 20.7 %copy-start.8 = (bf16[2,64,256]{2,1,0:T(8,128)(2,1)}, bf16[2,64,256]{2,1,0:T(8,128)(2,1)S(1)}, u32[]{:S(2)}) copy-start(bf16[2,64,256]{2,1,0:T(8,128)(2,1)S(1)} %get-tuple-element.943) | copy-start | bytes 196612 | tf_op jit(solution)/shard_map/while
  313.3 20.7 %collective-permute-start = (bf16[64,256]{1,0:T(8,128)(2,1)S(1)}, bf16[64,256]{1,0:T(8,128)(2,1)S(1)}, u32[]{:S(2)}, u32[]{:S(2)}) collective-permute-start(bf16[64,256]{1,0:T(8,128)(2,1)S(1)} %get-tuple-element.907), channel_id=1, source_target_pairs={{0,64},{64,128},{128,192},{192,256},{256,320},{320,384},{384,448},... | collective-permute-start | bytes 98312 | tf_op jit(solution)/shard_map/while/body/eval_jaxpr/ppermute | solution.py:202
  355.0 22.9 %copy-start.8 = (bf16[2,64,256]{2,1,0:T(8,128)(2,1)}, bf16[2,64,256]{2,1,0:T(8,128)(2,1)S(1)}, u32[]{:S(2)}) copy-start(bf16[2,64,256]{2,1,0:T(8,128)(2,1)S(1)} %get-tuple-element.943) | copy-start | bytes 196612 | tf_op jit(solution)/shard_map/while
  355.0 22.9 %collective-permute-start = (bf16[64,256]{1,0:T(8,128)(2,1)S(1)}, bf16[64,256]{1,0:T(8,128)(2,1)S(1)}, u32[]{:S(2)}, u32[]{:S(2)}) collective-permute-start(bf16[64,256]{1,0:T(8,128)(2,1)S(1)} %get-tuple-element.907), channel_id=1, source_target_pairs={{0,64},{64,128},{128,192},{192,256},{256,320},{320,384},{384,448},... | collective-permute-start | bytes 98312 | tf_op jit(solution)/shard_map/while/body/eval_jaxpr/ppermute | solution.py:202
  377.8 19.8 %copy-start.3 = (bf16[16,256,128]{2,1,0:T(8,128)(2,1)S(1)}, bf16[16,256,128]{2,1,0:T(8,128)(2,1)}, u32[]{:S(2)}) copy-start(bf16[16,256,128]{2,1,0:T(8,128)(2,1)} %get-tuple-element.513.value) | copy-start | bytes 3145732 | tf_op jit(solution)/shard_map/while/body/eval_jaxpr/cond
  378.6 16.4 %all-to-all-start = ((bf16[8,64,256]{2,1,0:T(8,128)(2,1)}), bf16[8,64,256]{2,1,0:T(8,128)(2,1)}, u32[]{:S(2)}, u32[]{:S(2)}) async-start(bf16[8,64,256]{2,1,0:T(8,128)(2,1)} %broadcast_in_dim.76), calls=%async_computation | async-start | bytes 524288 | tf_op jit(solution)/shard_map/while/body/eval_jaxpr/cond/branch_0_fun/all_to_all | solution.py:169
  397.6 16.1 %copy-start.4 = (bf16[8,256,256]{2,1,0:T(8,128)(2,1)S(1)}, bf16[8,256,256]{2,1,0:T(8,128)(2,1)}, u32[]{:S(2)}) copy-start(bf16[8,256,256]{2,1,0:T(8,128)(2,1)} %get-tuple-element.516.weights) | copy-start | bytes 3145732 | tf_op jit(solution)/shard_map/while/body/eval_jaxpr/cond
  (40 other events, 50.9 us)

commit v4 on v3

--- a/solution.py
+++ b/solution.py
@@ -176,7 +176,7 @@
         mixed = to_all(mixture, ("y", "core"), group)
         return leaving(mixed, current, out_part, out_bias)
 
-    def partial_gradients():
+    def gradients_of():
         own_lengths = lax.dynamic_slice_in_dim(lengths[0], chip * CORES + core, 1, 0)
         own_framed = framed_of(wave[0], own_lengths).astype(jnp.float32)
         own_live = live_of(own_lengths, frame_total)
@@ -192,42 +192,38 @@
             [partial[0].T, partial[1][None], partial[2][None], partial[3][None]], axis=0
         )
         packed = jnp.pad(packed, ((0, 16 - packed.shape[0]), (0, 0)))
-        return lax.psum(lax.psum(packed, "core"), "dp")
-
-    gradient_tick = jnp.where(section >= sections // 2, 1, sections - 2)
-    ticks = sections + MICRO - 1
+        return lax.psum(lax.psum(lax.psum(packed, "core"), "dp"), "y")
+
+    late = section >= sections // 2
+    packed = lax.cond(
+        late, gradients_of, lambda: jnp.zeros((16, conv_bias.shape[0]), jnp.float32)
+    )
+    entering, packed = lax.optimization_barrier((entering, packed))
 
     def advance(tick, state):
-        previous, outputs, packed = state
+        previous, outputs = state
         arrived = lax.ppermute(previous, "section", [(s, s + 1) for s in range(sections - 1)])
         piece = tick - section
         slot = jnp.clip(piece, 0, MICRO - 1)
-        fresh = lax.dynamic_index_in_dim(entering, slot, 0, keepdims=False)
-        current = jnp.where(section == 0, fresh, arrived)
-        masking = lax.dynamic_index_in_dim(maskings, slot, 0, keepdims=False)
-        kind = jnp.clip(tick - gradient_tick, -1, 2)
-        kind = jnp.where((kind == 0) | (kind == 1), kind + 1, 0)
-        result, packed = lax.switch(
-            kind,
-            [
-                lambda: (attend(current, masking), packed),
-                lambda: (current, partial_gradients()),
-                lambda: (current, lax.psum(packed, "y")),
-            ],
+
+        def work():
+            fresh = lax.dynamic_index_in_dim(entering, slot, 0, keepdims=False)
+            current = jnp.where(section == 0, fresh, arrived)
+            masking = lax.dynamic_index_in_dim(maskings, slot, 0, keepdims=False)
+            result = attend(current, masking)
+            return (result, lax.dynamic_update_index_in_dim(outputs, result, slot, 0))
+
+        return lax.cond(
+            (piece >= 0) & (piece < MICRO), work, lambda: (previous, outputs)
         )
-        kept = lax.dynamic_index_in_dim(outputs, slot, 0, keepdims=False)
-        has_work = (piece >= 0) & (piece < MICRO)
-        outputs = lax.dynamic_update_index_in_dim(
-            outputs, jnp.where(has_work, result, kept), slot, 0
-        )
-        return (result, outputs, packed)
 
     start = (
         jnp.zeros((rows, columns), jnp.bfloat16),
         jnp.zeros((MICRO, rows, columns), jnp.bfloat16),
-        jnp.zeros((16, conv_bias.shape[0]), jnp.float32),
-    )
-    _, outputs, packed = lax.fori_loop(0, ticks, advance, start)
+    )
+    _, outputs = lax.fori_loop(0, sections + MICRO - 1, advance, start)
+    outputs, packed = lax.optimization_barrier((outputs, packed))
+    packed = lax.cond(late, lambda: packed, gradients_of)
     return (
         outputs[None, None],
         packed[:KERNEL].T,

time: 420 us -> 412 us (0.981)
  the two profiles are of different devices: /device:TPU:195 before, /device:TPU:449 now
where the time goes in v4:
time: 412 us; the launch traced here: 411 us
  waiting for transfers between devices  273 us (66%)
  blocking collectives  89.8 us (22%)
  starting transfers between devices  19.6 us (5%)
  local copies, waits for them, and re-layouts  12.1 us (3%)
  other arithmetic  6.66 us (2%)
  Pallas kernels  4.61 us (1%)
    ppermute x9, waiting for transfers between devices, advance(): lax.ppermute(previous, 'section', [(s, s + 1) for s in range(sections - 1)])  250 us
    psum x3, blocking collectives, gradients_of(): return lax.psum(lax.psum(lax.psum(packed, 'core'), 'dp'), 'y')  37.6 us
    all_to_all x2, blocking collectives, to_all(): return lax.all_to_all(copies, axes, 0, 0, tiled=True)  29.3 us
    all_to_all x2, waiting for transfers between devices, to_all(): return lax.all_to_all(copies, axes, 0, 0, tiled=True)  23.4 us
    all_gather x1, blocking collectives, on_device(): lax.all_gather(wave[0].astype(jnp.float32), ('y', 'core'), axis=0, tiled=...  17.9 us
    ppermute x9, starting transfers between devices, advance(): lax.ppermute(previous, 'section', [(s, s + 1) for s in range(sections - 1)])  11.5 us
  transfers between devices with their start and end apart: 11, of which 11 were waited for; matrix products, arithmetic and copies ran while one was open for 0% of the time, Pallas kernels for 0%

profile of v4, /device:TPU:449, one launch (start us, length us, event | category | flops | bytes accessed | tf_op | source)
XLA Modules:
  0.0 411.0 jit_solution(16777644368925560611)
XLA Ops:
  0.7 0.7 copy-done.17
  2.1 17.9 %all-gather.1 = f32[16,1,40]{2,1,0:T(1,128)S(1)} all-gather(f32[1,1,40]{2,1,0:T(1,128)S(1)} %convert_element_type.85), channel_id=3, replica_groups=mesh['section'=8,'y'=8,'core'=2,'dp'=4] {'y','core'}, dimensions={0}, use_global_device_ids=true | all-gather | bytes 2720 | tf_op jit(solution)/shard_map/all_gather | solution.py:120
  20.4 0.7 copy-done.7
  22.4 0.8 convert_reduce_fusion
  23.6 0.9 fusion.54
  24.4 43.5 %conditional.3 = (f32[16,512]{1,0:T(8,128)S(1)}) conditional(s32[]{:T(128)} %convert_element_type.82, () %tuple.43, (s32[]{:T(128)}, s32[]{:T(128)}, s32[1,16]{1,0:T(1,128)S(1)}, bf16[1,1,40]{2,1,0:T(2,128)(2,1)S(1)}, bf16[512,10]{0,1:T(8,128)(2,1)S(1)}, /*index=5*/f32[512]{0:T(512)S(1)}, f32[512]{0:T(512)S(1)}, f32[512]{0:T(512)S(1)}, ...), branch_computations={%region_6.7_spmd, %region_7.18_spmd} | conditional | flops 1064623 | bytes 458498 | solution.py:198
  30.3 3.4 psum.36
  33.8 13.3 %psum.37 = f32[16,512]{1,0:T(8,128)S(1)} all-reduce(f32[16,512]{1,0:T(8,128)S(1)} %psum.36), channel_id=1, replica_groups=mesh['section'=8,'y'=8,'core'=2,'dp'=4] {'dp'}, use_global_device_ids=true, to_apply=%region_16.16 | all-reduce | flops 8192 | bytes 65536 | tf_op jit(solution)/shard_map/cond/branch_1_fun/psum | solution.py:195
  47.1 20.8 %psum.38 = f32[16,512]{1,0:T(8,128)S(1)} all-reduce(f32[16,512]{1,0:T(8,128)S(1)} %psum.37), channel_id=1, replica_groups=mesh['section'=8,'y'=8,'core'=2,'dp'=4] {'y'}, use_global_device_ids=true, to_apply=%region_17.17 | all-reduce | flops 8192 | bytes 65536 | tf_op jit(solution)/shard_map/cond/branch_1_fun/psum | solution.py:195
  70.4 339.4 %while.16 = (s32[]{:T(128)}, bf16[64,256]{1,0:T(8,128)(2,1)}, bf16[2,64,256]{2,1,0:T(8,128)(2,1)}, s32[]{:T(128)}, bf16[2,64,256]{2,1,0:T(8,128)(2,1)}, /*index=...) while((s32[]{:T(128)}, bf16[64,256]{1,0:T(8,128)(2,1)}, ...), condition=%wide.region_21.22_spmd.clone, body=%wide.region_18.21_spmd.clone.sunk | while | flops 24586 | bytes 11375321 | solution.py:224
  70.4 1.3 collective-permute-start
  71.7 3.6 collective-permute-done
  75.2 1.3 collective-permute-start
  76.5 3.6 collective-permute-done
  80.1 1.3 collective-permute-start
  81.4 3.6 collective-permute-done
  84.9 1.3 collective-permute-start
  86.2 3.6 collective-permute-done
  89.8 1.3 collective-permute-start
  91.1 3.6 collective-permute-done
  94.7 1.3 collective-permute-start
  96.0 3.6 collective-permute-done
  99.6 1.3 collective-permute-start
  100.9 4.8 %collective-permute-done = bf16[64,256]{1,0:T(8,128)(2,1)S(1)} collective-permute-done((bf16[64,256]{1,0:T(8,128)(2,1)}, bf16[64,256]{1,0:T(8,128)(2,1)S(1)}, u32[]{:S(2)}, u32[]{:S(2)}) %collective-permute-start) | collective-permute-done | bytes 32800 | tf_op jit(solution)/shard_map/while/body/eval_jaxpr/ppermute | solution.py:205
  105.7 1.3 collective-permute-start
  107.0 218.8 %collective-permute-done = bf16[64,256]{1,0:T(8,128)(2,1)S(1)} collective-permute-done((bf16[64,256]{1,0:T(8,128)(2,1)}, bf16[64,256]{1,0:T(8,128)(2,1)S(1)}, u32[]{:S(2)}, u32[]{:S(2)}) %collective-permute-start) | collective-permute-done | bytes 32800 | tf_op jit(solution)/shard_map/while/body/eval_jaxpr/ppermute | solution.py:205
  325.8 38.8 %conditional.7 = ((bf16[64,256]{1,0:T(8,128)(2,1)}, bf16[2,64,256]{2,1,0:T(8,128)(2,1)})) conditional(s32[]{:T(128)} %convert_element_type.112, (bf16[64,256]{1,0:T(8,128)(2,1)}, bf16[2,64,256]{2,1,0:T(8,128)(2,1)}) %tuple.88, (s32[]{:T(128)}, s32[]{:T(128)}, bf16[2,64,256]{2,1,0:T(8,128)(2,1)}, bf16[64,256]{1,0:T(8,128)(2,1)S(1)}, ...), branch_computations={%region_19.19_spmd, %region_20.20_spmd} | conditional | flops 24579 | bytes 11243870 | solution.py:216
  325.8 0.9 bitcast_select_fusion.current
  326.6 0.7 broadcast_in_dim.99
  327.3 4.0 all-to-all-start
  332.1 11.7 %all-to-all-done = bf16[8,64,256]{2,1,0:T(8,128)(2,1)} async-done(((bf16[8,64,256]{2,1,0:T(8,128)(2,1)}), bf16[8,64,256]{2,1,0:T(8,128)(2,1)}, u32[]{:S(2)}, u32[]{:S(2)}) %all-to-all-start) | async-done | bytes 262176 | tf_op jit(solution)/shard_map/while/body/eval_jaxpr/cond/branch_1_fun/all_to_all | solution.py:169
  343.7 2.5 all-gather
  346.2 1.4 branch_1_fun.2
  347.7 14.6 %all_to_all.8.mixed = bf16[16,64,128]{2,1,0:T(8,128)(2,1)S(1)} all-to-all(bf16[16,64,128]{2,1,0:T(8,128)(2,1)S(1)} %broadcast_in_dim.100), channel_id=1, replica_groups=mesh['section'=8,'y'=8,'core'=2,'dp'=4] {'y','core'}, dimensions={0} | all-to-all | bytes 524288 | tf_op jit(solution)/shard_map/while/body/eval_jaxpr/cond/branch_1_fun/all_to_all | solution.py:169
  362.3 0.9 branch_1_fun.3
  363.2 1.4 bitcast_dynamic-update-slice_fusion
  364.6 1.3 collective-permute-start
  365.9 5.1 %collective-permute-done = bf16[64,256]{1,0:T(8,128)(2,1)S(1)} collective-permute-done((bf16[64,256]{1,0:T(8,128)(2,1)}, bf16[64,256]{1,0:T(8,128)(2,1)S(1)}, u32[]{:S(2)}, u32[]{:S(2)}) %collective-permute-start) | collective-permute-done | bytes 32800 | tf_op jit(solution)/shard_map/while/body/eval_jaxpr/ppermute | solution.py:205
  371.0 38.8 %conditional.7 = ((bf16[64,256]{1,0:T(8,128)(2,1)}, bf16[2,64,256]{2,1,0:T(8,128)(2,1)})) conditional(s32[]{:T(128)} %convert_element_type.112, (bf16[64,256]{1,0:T(8,128)(2,1)}, bf16[2,64,256]{2,1,0:T(8,128)(2,1)}) %tuple.88, (s32[]{:T(128)}, s32[]{:T(128)}, bf16[2,64,256]{2,1,0:T(8,128)(2,1)}, bf16[64,256]{1,0:T(8,128)(2,1)S(1)}, ...), branch_computations={%region_19.19_spmd, %region_20.20_spmd} | conditional | flops 24579 | bytes 11243870 | solution.py:216
  371.0 0.9 bitcast_select_fusion.current
  371.8 0.7 broadcast_in_dim.99
  372.5 4.0 all-to-all-start
  377.3 11.7 %all-to-all-done = bf16[8,64,256]{2,1,0:T(8,128)(2,1)} async-done(((bf16[8,64,256]{2,1,0:T(8,128)(2,1)}), bf16[8,64,256]{2,1,0:T(8,128)(2,1)}, u32[]{:S(2)}, u32[]{:S(2)}) %all-to-all-start) | async-done | bytes 262176 | tf_op jit(solution)/shard_map/while/body/eval_jaxpr/cond/branch_1_fun/all_to_all | solution.py:169
  388.9 2.5 all-gather
  391.4 1.4 branch_1_fun.2
  392.9 14.6 %all_to_all.8.mixed = bf16[16,64,128]{2,1,0:T(8,128)(2,1)S(1)} all-to-all(bf16[16,64,128]{2,1,0:T(8,128)(2,1)S(1)} %broadcast_in_dim.100), channel_id=1, replica_groups=mesh['section'=8,'y'=8,'core'=2,'dp'=4] {'y','core'}, dimensions={0} | all-to-all | bytes 524288 | tf_op jit(solution)/shard_map/while/body/eval_jaxpr/cond/branch_1_fun/all_to_all | solution.py:169
  407.5 0.9 branch_1_fun.3
  408.4 1.4 bitcast_dynamic-update-slice_fusion
  (106 shorter events, 11.6 us)
Async XLA Ops:
  0.6 22.9 %copy-start = (bf16[512,256]{1,0:T(8,128)(2,1)S(1)}, bf16[512,256]{1,0:T(8,128)(2,1)}, u32[]{:S(2)}) copy-start(bf16[512,256]{1,0:T(8,128)(2,1)} %param.36) | copy-start | bytes 786436
  0.6 0.7 copy-start.17
  0.7 0.7 copy-start.19
  1.5 0.7 copy-start.23
  20.3 0.7 copy-start.7
  20.4 0.7 copy-start.15
  21.6 2.0 copy-start.20
  21.6 2.0 copy-start.21
  21.6 2.0 copy-start.22
  21.6 2.8 copy-start.10
  21.6 0.7 copy-start.9
  21.7 0.7 copy-start.13
  22.3 47.9 %copy-start.1 = (bf16[1,4096,128]{2,1,0:T(8,128)(2,1)S(1)}, bf16[1,4096,128]{2,1,0:T(8,128)(2,1)}, u32[]{:S(2)}) copy-start(bf16[1,4096,128]{2,1,0:T(8,128)(2,1)} %param.40) | copy-start | bytes 3145732
  22.3 47.9 %copy-start.2 = (bf16[1,4096,128]{2,1,0:T(8,128)(2,1)S(1)}, bf16[1,4096,128]{2,1,0:T(8,128)(2,1)}, u32[]{:S(2)}) copy-start(bf16[1,4096,128]{2,1,0:T(8,128)(2,1)} %param.41) | copy-start | bytes 3145732
  69.0 1.3 copy-start.12
  69.6 0.7 copy-start.5
  69.6 0.7 copy-start.6
  70.4 4.9 %collective-permute-start = (bf16[64,256]{1,0:T(8,128)(2,1)}, bf16[64,256]{1,0:T(8,128)(2,1)S(1)}, u32[]{:S(2)}, u32[]{:S(2)}) collective-permute-start(bf16[64,256]{1,0:T(8,128)(2,1)} %get-tuple-element.556), channel_id=1, source_target_pairs={{0,64},{64,128},{128,192},{192,256},{256,320},{320,384},{384,448},... | collective-permute-start | bytes 98312 | tf_op jit(solution)/shard_map/while/body/eval_jaxpr/ppermute | solution.py:205
  75.2 4.9 %collective-permute-start = (bf16[64,256]{1,0:T(8,128)(2,1)}, bf16[64,256]{1,0:T(8,128)(2,1)S(1)}, u32[]{:S(2)}, u32[]{:S(2)}) collective-permute-start(bf16[64,256]{1,0:T(8,128)(2,1)} %get-tuple-element.556), channel_id=1, source_target_pairs={{0,64},{64,128},{128,192},{192,256},{256,320},{320,384},{384,448},... | collective-permute-start | bytes 98312 | tf_op jit(solution)/shard_map/while/body/eval_jaxpr/ppermute | solution.py:205
  80.1 4.9 %collective-permute-start = (bf16[64,256]{1,0:T(8,128)(2,1)}, bf16[64,256]{1,0:T(8,128)(2,1)S(1)}, u32[]{:S(2)}, u32[]{:S(2)}) collective-permute-start(bf16[64,256]{1,0:T(8,128)(2,1)} %get-tuple-element.556), channel_id=1, source_target_pairs={{0,64},{64,128},{128,192},{192,256},{256,320},{320,384},{384,448},... | collective-permute-start | bytes 98312 | tf_op jit(solution)/shard_map/while/body/eval_jaxpr/ppermute | solution.py:205
  84.9 4.9 %collective-permute-start = (bf16[64,256]{1,0:T(8,128)(2,1)}, bf16[64,256]{1,0:T(8,128)(2,1)S(1)}, u32[]{:S(2)}, u32[]{:S(2)}) collective-permute-start(bf16[64,256]{1,0:T(8,128)(2,1)} %get-tuple-element.556), channel_id=1, source_target_pairs={{0,64},{64,128},{128,192},{192,256},{256,320},{320,384},{384,448},... | collective-permute-start | bytes 98312 | tf_op jit(solution)/shard_map/while/body/eval_jaxpr/ppermute | solution.py:205
  89.8 4.9 %collective-permute-start = (bf16[64,256]{1,0:T(8,128)(2,1)}, bf16[64,256]{1,0:T(8,128)(2,1)S(1)}, u32[]{:S(2)}, u32[]{:S(2)}) collective-permute-start(bf16[64,256]{1,0:T(8,128)(2,1)} %get-tuple-element.556), channel_id=1, source_target_pairs={{0,64},{64,128},{128,192},{192,256},{256,320},{320,384},{384,448},... | collective-permute-start | bytes 98312 | tf_op jit(solution)/shard_map/while/body/eval_jaxpr/ppermute | solution.py:205
  94.7 4.9 %collective-permute-start = (bf16[64,256]{1,0:T(8,128)(2,1)}, bf16[64,256]{1,0:T(8,128)(2,1)S(1)}, u32[]{:S(2)}, u32[]{:S(2)}) collective-permute-start(bf16[64,256]{1,0:T(8,128)(2,1)} %get-tuple-element.556), channel_id=1, source_target_pairs={{0,64},{64,128},{128,192},{192,256},{256,320},{320,384},{384,448},... | collective-permute-start | bytes 98312 | tf_op jit(solution)/shard_map/while/body/eval_jaxpr/ppermute | solution.py:205
  99.6 6.1 %collective-permute-start = (bf16[64,256]{1,0:T(8,128)(2,1)}, bf16[64,256]{1,0:T(8,128)(2,1)S(1)}, u32[]{:S(2)}, u32[]{:S(2)}) collective-permute-start(bf16[64,256]{1,0:T(8,128)(2,1)} %get-tuple-element.556), channel_id=1, source_target_pairs={{0,64},{64,128},{128,192},{192,256},{256,320},{320,384},{384,448},... | collective-permute-start | bytes 98312 | tf_op jit(solution)/shard_map/while/body/eval_jaxpr/ppermute | solution.py:205
  105.7 220.1 %collective-permute-start = (bf16[64,256]{1,0:T(8,128)(2,1)}, bf16[64,256]{1,0:T(8,128)(2,1)S(1)}, u32[]{:S(2)}, u32[]{:S(2)}) collective-permute-start(bf16[64,256]{1,0:T(8,128)(2,1)} %get-tuple-element.556), channel_id=1, source_target_pairs={{0,64},{64,128},{128,192},{192,256},{256,320},{320,384},{384,448},... | collective-permute-start | bytes 98312 | tf_op jit(solution)/shard_map/while/body/eval_jaxpr/ppermute | solution.py:205
  325.8 20.5 %copy-start.3 = (bf16[16,256,128]{2,1,0:T(8,128)(2,1)S(1)}, bf16[16,256,128]{2,1,0:T(8,128)(2,1)}, u32[]{:S(2)}) copy-start(bf16[16,256,128]{2,1,0:T(8,128)(2,1)} %get-tuple-element.297.value) | copy-start | bytes 3145732 | tf_op jit(solution)/shard_map/while/body/eval_jaxpr/cond
  327.3 16.4 %all-to-all-start = ((bf16[8,64,256]{2,1,0:T(8,128)(2,1)}), bf16[8,64,256]{2,1,0:T(8,128)(2,1)}, u32[]{:S(2)}, u32[]{:S(2)}) async-start(bf16[8,64,256]{2,1,0:T(8,128)(2,1)} %broadcast_in_dim.99), calls=%async_computation | async-start | bytes 524288 | tf_op jit(solution)/shard_map/while/body/eval_jaxpr/cond/branch_1_fun/all_to_all | solution.py:169
  346.2 16.1 %copy-start.4 = (bf16[8,256,256]{2,1,0:T(8,128)(2,1)S(1)}, bf16[8,256,256]{2,1,0:T(8,128)(2,1)}, u32[]{:S(2)}) copy-start(bf16[8,256,256]{2,1,0:T(8,128)(2,1)} %get-tuple-element.299.weights) | copy-start | bytes 3145732 | tf_op jit(solution)/shard_map/while/body/eval_jaxpr/cond
  364.6 6.4 %collective-permute-start = (bf16[64,256]{1,0:T(8,128)(2,1)}, bf16[64,256]{1,0:T(8,128)(2,1)S(1)}, u32[]{:S(2)}, u32[]{:S(2)}) collective-permute-start(bf16[64,256]{1,0:T(8,128)(2,1)} %get-tuple-element.556), channel_id=1, source_target_pairs={{0,64},{64,128},{128,192},{192,256},{256,320},{320,384},{384,448},... | collective-permute-start | bytes 98312 | tf_op jit(solution)/shard_map/while/body/eval_jaxpr/ppermute | solution.py:205
  371.0 20.5 %copy-start.3 = (bf16[16,256,128]{2,1,0:T(8,128)(2,1)S(1)}, bf16[16,256,128]{2,1,0:T(8,128)(2,1)}, u32[]{:S(2)}) copy-start(bf16[16,256,128]{2,1,0:T(8,128)(2,1)} %get-tuple-element.297.value) | copy-start | bytes 3145732 | tf_op jit(solution)/shard_map/while/body/eval_jaxpr/cond
  372.5 16.4 %all-to-all-start = ((bf16[8,64,256]{2,1,0:T(8,128)(2,1)}), bf16[8,64,256]{2,1,0:T(8,128)(2,1)}, u32[]{:S(2)}, u32[]{:S(2)}) async-start(bf16[8,64,256]{2,1,0:T(8,128)(2,1)} %broadcast_in_dim.99), calls=%async_computation | async-start | bytes 524288 | tf_op jit(solution)/shard_map/while/body/eval_jaxpr/cond/branch_1_fun/all_to_all | solution.py:169
  391.4 16.1 %copy-start.4 = (bf16[8,256,256]{2,1,0:T(8,128)(2,1)S(1)}, bf16[8,256,256]{2,1,0:T(8,128)(2,1)}, u32[]{:S(2)}) copy-start(bf16[8,256,256]{2,1,0:T(8,128)(2,1)} %get-tuple-element.299.weights) | copy-start | bytes 3145732 | tf_op jit(solution)/shard_map/while/body/eval_jaxpr/cond

commit v5 on v4

--- a/solution.py
+++ b/solution.py
@@ -49,41 +49,46 @@
     return jnp.dot(left, right, preferred_element_type=jnp.float32)
 
 
-def mixing_kernel(blocks, gain, shift, query, key, value, masking, out):
-    parts, rows, width = blocks.shape
+def mixing_kernel(place, rows_ref, gain, shift, query, key, value, masking, out):
+    rows, model = rows_ref.shape
+    width = 2 * HEAD_DIM
+    spans = [slice(at, at + width) for at in range(0, model, width)]
     total = jnp.zeros((rows, 1), jnp.float32)
-    for i in range(parts):
-        total += jnp.sum(blocks[i].astype(jnp.float32), axis=-1, keepdims=True)
-    average = total / (parts * width)
+    for span in spans:
+        total += jnp.sum(rows_ref[:, span].astype(jnp.float32), axis=-1, keepdims=True)
+    average = total / model
     spread = jnp.zeros_like(average)
-    for i in range(parts):
-        centered = blocks[i].astype(jnp.float32) - average
+    for span in spans:
+        centered = rows_ref[:, span].astype(jnp.float32) - average
         spread += jnp.sum(centered * centered, axis=-1, keepdims=True)
-    scale = lax.rsqrt(spread / (parts * width) + 1e-05)
+    scale = lax.rsqrt(spread / model + 1e-05)
     both = jnp.zeros((rows, 2 * HEAD_DIM), jnp.float32)
     values = jnp.zeros((rows, HEAD_DIM), jnp.float32)
-    for i in range(parts):
-        centered = blocks[i].astype(jnp.float32) - average
-        normed = (centered * scale * gain[i] + shift[i]).astype(jnp.bfloat16)
-        both += product(normed, jnp.concatenate([query[i], key[i]], axis=1))
-        values += product(normed, value[i])
+    for span in spans:
+        centered = rows_ref[:, span].astype(jnp.float32) - average
+        normed = (centered * scale * gain[:, span] + shift[:, span]).astype(jnp.bfloat16)
+        both += product(normed, jnp.concatenate([query[span], key[span]], axis=1))
+        values += product(normed, value[span])
     queries = (both[:, :HEAD_DIM] * HEAD_DIM ** (-0.5)).astype(jnp.bfloat16)
     key_rows = both[:, HEAD_DIM:].astype(jnp.bfloat16)
     scores = lax.dot_general(
         queries, key_rows, (((1,), (1,)), ((), ())), preferred_element_type=jnp.float32
     )
-    scores = jnp.where(masking[...] > 0, scores, -jnp.inf)
+    scores = jnp.where(masking[place[0]] > 0, scores, -jnp.inf)
     raised = jnp.exp(scores - jnp.max(scores, axis=-1, keepdims=True))
     attention = (raised / jnp.sum(raised, axis=-1, keepdims=True)).astype(jnp.bfloat16)
-    out[...] = product(attention, values.astype(jnp.bfloat16)).astype(jnp.bfloat16)
-
-
-def leaving_kernel(mixed, current, weights, bias, out):
+    mixture = product(attention, values.astype(jnp.bfloat16)).astype(jnp.bfloat16)
+    out[...] = jnp.broadcast_to(mixture[None], out.shape)
+
+
+def leaving_kernel(place, mixed, current, weights, bias, _, out, outputs):
     total = current[...].astype(jnp.float32) + bias[...]
     for i in range(0, mixed.shape[0], 2):
         pair = jnp.concatenate([mixed[i], mixed[i + 1]], axis=1)
         total += product(pair, weights[i // 2])
-    out[...] = total.astype(jnp.bfloat16)
+    result = total.astype(jnp.bfloat16)
+    out[...] = result
+    outputs[place[0]] = result
 
 
 def on_device(
@@ -140,41 +145,44 @@
     owner = lax.broadcasted_iota(jnp.int32, (rows, rows), 0) // frame_total
     column = lax.broadcasted_iota(jnp.int32, (rows, rows), 1) // frame_total
     maskings = jnp.where((owner == column)[None] & live.reshape(MICRO, 1, rows), 1.0, 0.0)
-    gain = norm_gain.reshape(group, 1, columns)
-    shift = norm_shift.reshape(group, 1, columns)
-    query, key, value = (
-        weight.reshape(group, columns, HEAD_DIM)
-        for weight in (query_weight, key_weight, value_weight)
-    )
     out_part = out_weight.reshape(group // 2, 2 * HEAD_DIM, columns)
 
     vmem = pl.BlockSpec(memory_space=pltpu.VMEM)
+    smem = pl.BlockSpec(memory_space=pltpu.SMEM)
     mixing = pl.pallas_call(
         mixing_kernel,
-        out_shape=jax.ShapeDtypeStruct((rows, HEAD_DIM), jnp.bfloat16),
-        in_specs=[vmem] * 7,
+        out_shape=jax.ShapeDtypeStruct((group, rows, HEAD_DIM), jnp.bfloat16),
+        in_specs=[smem] + [vmem] * 7,
         out_specs=vmem,
         compiler_params=pltpu.CompilerParams(vmem_limit_bytes=24 * 2**20),
     )
     leaving = pl.pallas_call(
         leaving_kernel,
-        out_shape=jax.ShapeDtypeStruct((rows, columns), jnp.bfloat16),
-        in_specs=[vmem] * 4,
-        out_specs=vmem,
+        out_shape=(
+            jax.ShapeDtypeStruct((rows, columns), jnp.bfloat16),
+            jax.ShapeDtypeStruct((MICRO, rows, columns), jnp.bfloat16),
+        ),
+        in_specs=[smem] + [vmem] * 5,
+        out_specs=(vmem, vmem),
+        input_output_aliases={5: 1},
         compiler_params=pltpu.CompilerParams(vmem_limit_bytes=24 * 2**20),
     )
 
-    def to_all(block, axes, size):
-        copies = jnp.broadcast_to(block[None], (size,) + block.shape)
-        return lax.all_to_all(copies, axes, 0, 0, tiled=True)
-
-    def attend(current, masking):
-        chip_blocks = to_all(current, "y", chips)
-        blocks = lax.all_gather(chip_blocks, "core", axis=1, tiled=False)
-        blocks = blocks.reshape(group, rows, columns)
-        mixture = mixing(blocks, gain, shift, query, key, value, masking)
-        mixed = to_all(mixture, ("y", "core"), group)
-        return leaving(mixed, current, out_part, out_bias)
+    def attend(current, slot, outputs):
+        place = slot.reshape(1)
+        whole = lax.all_gather(current, ("y", "core"), axis=1, tiled=True)
+        copies = mixing(
+            place,
+            whole,
+            norm_gain,
+            norm_shift,
+            query_weight[0],
+            key_weight[0],
+            value_weight[0],
+            maskings,
+        )
+        mixed = lax.all_to_all(copies, ("y", "core"), 0, 0, tiled=True)
+        return leaving(place, mixed, current, out_part, out_bias, outputs)
 
     def gradients_of():
         own_lengths = lax.dynamic_slice_in_dim(lengths[0], chip * CORES + core, 1, 0)
@@ -209,9 +217,7 @@
         def work():
             fresh = lax.dynamic_index_in_dim(entering, slot, 0, keepdims=False)
             current = jnp.where(section == 0, fresh, arrived)
-            masking = lax.dynamic_index_in_dim(maskings, slot, 0, keepdims=False)
-            result = attend(current, masking)
-            return (result, lax.dynamic_update_index_in_dim(outputs, result, slot, 0))
+            return tuple(attend(current, slot, outputs))
 
         return lax.cond(
             (piece >= 0) & (piece < MICRO), work, lambda: (previous, outputs)

time: 412 us -> 389 us (0.944)
  waiting for transfers between devices: 273 us -> 234 us
  blocking collectives: 89.8 us -> 122 us
  starting transfers between devices: 19.6 us -> 11.5 us
  local copies, waits for them, and re-layouts: 12.1 us -> 5.72 us
    all_gather x2, blocking collectives: 4.94 us -> 32.2 us  [attend(): whole = lax.all_gather(current, ('y', 'core'), axis=1, tiled=True)]
    all_to_all x2 -> x0, waiting for transfers between devices: 23.4 us -> none  [to_all(): return lax.all_to_all(copies, axes, 0, 0, tiled=True)]
    ppermute x9, waiting for transfers between devices: 250 us -> 234 us  [advance(): lax.ppermute(previous, 'section', [(s, s + 1) for s in range(sections - 1)])]
    all_to_all x2 -> x0, starting transfers between devices: 8.08 us -> none  [to_all(): return lax.all_to_all(copies, axes, 0, 0, tiled=True)]
    all_to_all x2, blocking collectives: 29.3 us -> 34.3 us  [attend(): mixed = lax.all_to_all(copies, ('y', 'core'), 0, 0, tiled=True)]
  transfers between devices with their start and end apart: 11 -> 9, of which waited for: 11 -> 9; matrix products, arithmetic and copies ran while one was open for 0% -> 0% of each run, Pallas kernels for 0% -> 0%
where the time goes in v5:
time: 389 us; the launch traced here: 388 us
  waiting for transfers between devices  234 us (60%)
  blocking collectives  122 us (31%)
  starting transfers between devices  11.5 us (3%)
  Pallas kernels  6.48 us (2%)
  local copies, waits for them, and re-layouts  5.72 us (1%)
  other arithmetic  4.37 us (1%)
    ppermute x9, waiting for transfers between devices, advance(): lax.ppermute(previous, 'section', [(s, s + 1) for s in range(sections - 1)])  234 us
    psum x3, blocking collectives, gradients_of(): return lax.psum(lax.psum(lax.psum(packed, 'core'), 'dp'), 'y')  37.6 us
    all_to_all x2, blocking collectives, attend(): mixed = lax.all_to_all(copies, ('y', 'core'), 0, 0, tiled=True)  34.3 us
    all_gather x2, blocking collectives, attend(): whole = lax.all_gather(current, ('y', 'core'), axis=1, tiled=True)  32.2 us
    all_gather x1, blocking collectives, on_device(): lax.all_gather(wave[0].astype(jnp.float32), ('y', 'core'), axis=0, tiled=...  17.9 us
    ppermute x9, starting transfers between devices, advance(): lax.ppermute(previous, 'section', [(s, s + 1) for s in range(sections - 1)])  11.5 us
  transfers between devices with their start and end apart: 9, of which 9 were waited for; matrix products, arithmetic and copies ran while one was open for 0% of the time, Pallas kernels for 0%

profile of v5, /device:TPU:449, one launch (start us, length us, event | category | flops | bytes accessed | tf_op | source)
XLA Modules:
  0.0 388.2 jit_solution(4336762526402095411)
XLA Ops:
  0.7 0.7 copy-done.12
  1.5 0.6 copy-done.17
  2.8 17.9 %all-gather = f32[16,1,40]{2,1,0:T(1,128)S(1)} all-gather(f32[1,1,40]{2,1,0:T(1,128)S(1)} %convert_element_type.85), channel_id=2, replica_groups=mesh['section'=8,'y'=8,'core'=2,'dp'=4] {'y','core'}, dimensions={0}, use_global_device_ids=true | all-gather | bytes 2720 | tf_op jit(solution)/shard_map/all_gather | solution.py:125
  21.1 0.6 copy-done.6
  21.7 43.4 %conditional.3 = (f32[16,512]{1,0:T(8,128)S(1)}) conditional(s32[]{:T(128)} %convert_element_type.82, () %tuple.42, (s32[]{:T(128)}, s32[]{:T(128)}, s32[1,16]{1,0:T(1,128)S(1)}, bf16[1,1,40]{2,1,0:T(2,128)(2,1)S(1)}, bf16[512,10]{0,1:T(8,128)(2,1)S(1)}, /*index=5*/f32[512]{0:T(512)S(1)}, f32[512]{0:T(512)S(1)}, f32[512]{0:T(512)S(1)}, ...), branch_computations={%region_6.7_spmd, %region_7.18_spmd} | conditional | flops 1064623 | bytes 458498 | solution.py:206
  21.7 0.5 broadcast.920
  22.3 0.7 reduce.36
  22.9 0.6 fusion.97
  25.6 0.6 fusion.21
  26.2 0.3 fusion.96
  27.5 3.4 psum.36
  31.0 13.3 %psum.37 = f32[16,512]{1,0:T(8,128)S(1)} all-reduce(f32[16,512]{1,0:T(8,128)S(1)} %psum.36), channel_id=1, replica_groups=mesh['section'=8,'y'=8,'core'=2,'dp'=4] {'dp'}, use_global_device_ids=true, to_apply=%region_16.16 | all-reduce | flops 8192 | bytes 65536 | tf_op jit(solution)/shard_map/cond/branch_1_fun/psum | solution.py:203
  44.3 20.8 %psum.38 = f32[16,512]{1,0:T(8,128)S(1)} all-reduce(f32[16,512]{1,0:T(8,128)S(1)} %psum.37), channel_id=1, replica_groups=mesh['section'=8,'y'=8,'core'=2,'dp'=4] {'y'}, use_global_device_ids=true, to_apply=%region_17.17 | all-reduce | flops 8192 | bytes 65536 | tf_op jit(solution)/shard_map/cond/branch_1_fun/psum | solution.py:203
  65.1 0.3 fusion.101
  65.6 0.8 convert_reduce_fusion
  67.2 0.6 copy-done.4
  67.9 318.5 %while.16 = (s32[]{:T(128)}, bf16[64,256]{1,0:T(8,128)(2,1)S(1)}, bf16[2,64,256]{2,1,0:T(8,128)(2,1)S(1)}, s32[]{:T(128)}, bf16[2,64,256]{2,1,0:T(8,128)(2,1)S(1...) while((s32[]{:T(128)}, bf16[64,256]{1,0:T(8,128)(2,1)S(1)}, ...), condition=%wide.region_21.22_spmd.clone, body=%wide.region_18.21_spmd.clone.sunk | while | flops 32778 | bytes 1348145 | solution.py:230
  67.9 1.3 collective-permute-start
  69.2 3.3 collective-permute-done
  72.5 1.3 collective-permute-start
  73.8 3.3 collective-permute-done
  77.2 1.3 collective-permute-start
  78.5 3.3 collective-permute-done
  81.8 1.3 collective-permute-start
  83.1 3.3 collective-permute-done
  86.5 1.3 collective-permute-start
  87.8 3.3 collective-permute-done
  91.1 1.3 collective-permute-start
  92.4 3.5 collective-permute-done
  95.9 1.3 collective-permute-start
  97.2 4.6 %collective-permute-done = bf16[64,256]{1,0:T(8,128)(2,1)S(1)} collective-permute-done((bf16[64,256]{1,0:T(8,128)(2,1)S(1)}, bf16[64,256]{1,0:T(8,128)(2,1)S(1)}, u32[]{:S(2)}, u32[]{:S(2)}) %collective-permute-start) | collective-permute-done | bytes 32800 | tf_op jit(solution)/shard_map/while/body/eval_jaxpr/ppermute | solution.py:213
  101.7 1.3 collective-permute-start
  103.0 203.9 %collective-permute-done = bf16[64,256]{1,0:T(8,128)(2,1)S(1)} collective-permute-done((bf16[64,256]{1,0:T(8,128)(2,1)S(1)}, bf16[64,256]{1,0:T(8,128)(2,1)S(1)}, u32[]{:S(2)}, u32[]{:S(2)}) %collective-permute-start) | collective-permute-done | bytes 32800 | tf_op jit(solution)/shard_map/while/body/eval_jaxpr/ppermute | solution.py:213
  307.0 36.5 %conditional.7 = ((bf16[64,256]{1,0:T(8,128)(2,1)S(1)}, bf16[2,64,256]{2,1,0:T(8,128)(2,1)S(1)})) conditional(s32[]{:T(128)} %convert_element_type.112, (bf16[64,256]{1,0:T(8,128)(2,1)S(1)}, bf16[2,64,256]{2,1,0:T(8,128)(2,1)S(1)}) %tuple.87, (s32[]{:T(128)}, s32[]{:T(128)}, bf16[2,64,256]{2,1,0:T(8,128)(2,1)S(1)}, bf16[64,256]{1,0:T(8,128)(2,1)S(1)}, ...), branch_computations={%region_19.19_spmd, %region_20.20_spmd} | conditional | flops 32771 | bytes 1216686 | solution.py:222
  307.0 16.1 %all_gather.4.rows_ref = bf16[64,4096]{1,0:T(8,128)(2,1)S(1)} all-gather(bf16[64,256]{1,0:T(8,128)(2,1)S(1)} %bitcast_select_fusion.current), channel_id=1, replica_groups=mesh['section'=8,'y'=8,'core'=2,'dp'=4] {'y','core'}, dimensions={1}, use_global_device_ids=true | all-gather | bytes 557056 | tf_op jit(solution)/shard_map/while/body/eval_jaxpr/cond/branch_1_fun/all_gather | solution.py:173
  323.1 2.9 branch_1_fun.2
  326.0 17.2 %all_to_all.4.mixed = bf16[16,64,128]{2,1,0:T(8,128)(2,1)S(1)} all-to-all(bf16[16,64,128]{2,1,0:T(8,128)(2,1)S(1)} %branch_1_fun.2), channel_id=1, replica_groups=mesh['section'=8,'y'=8,'core'=2,'dp'=4] {'y','core'}, dimensions={0} | all-to-all | bytes 524288 | tf_op jit(solution)/shard_map/while/body/eval_jaxpr/cond/branch_1_fun/all_to_all | solution.py:184
  343.2 0.3 branch_1_fun.3
  343.5 1.3 collective-permute-start
  344.8 5.0 %collective-permute-done = bf16[64,256]{1,0:T(8,128)(2,1)S(1)} collective-permute-done((bf16[64,256]{1,0:T(8,128)(2,1)S(1)}, bf16[64,256]{1,0:T(8,128)(2,1)S(1)}, u32[]{:S(2)}, u32[]{:S(2)}) %collective-permute-start) | collective-permute-done | bytes 32800 | tf_op jit(solution)/shard_map/while/body/eval_jaxpr/ppermute | solution.py:213
  349.8 36.5 %conditional.7 = ((bf16[64,256]{1,0:T(8,128)(2,1)S(1)}, bf16[2,64,256]{2,1,0:T(8,128)(2,1)S(1)})) conditional(s32[]{:T(128)} %convert_element_type.112, (bf16[64,256]{1,0:T(8,128)(2,1)S(1)}, bf16[2,64,256]{2,1,0:T(8,128)(2,1)S(1)}) %tuple.87, (s32[]{:T(128)}, s32[]{:T(128)}, bf16[2,64,256]{2,1,0:T(8,128)(2,1)S(1)}, bf16[64,256]{1,0:T(8,128)(2,1)S(1)}, ...), branch_computations={%region_19.19_spmd, %region_20.20_spmd} | conditional | flops 32771 | bytes 1216686 | solution.py:222
  349.8 16.1 %all_gather.4.rows_ref = bf16[64,4096]{1,0:T(8,128)(2,1)S(1)} all-gather(bf16[64,256]{1,0:T(8,128)(2,1)S(1)} %bitcast_select_fusion.current), channel_id=1, replica_groups=mesh['section'=8,'y'=8,'core'=2,'dp'=4] {'y','core'}, dimensions={1}, use_global_device_ids=true | all-gather | bytes 557056 | tf_op jit(solution)/shard_map/while/body/eval_jaxpr/cond/branch_1_fun/all_gather | solution.py:173
  365.9 2.9 branch_1_fun.2
  368.9 17.2 %all_to_all.4.mixed = bf16[16,64,128]{2,1,0:T(8,128)(2,1)S(1)} all-to-all(bf16[16,64,128]{2,1,0:T(8,128)(2,1)S(1)} %branch_1_fun.2), channel_id=1, replica_groups=mesh['section'=8,'y'=8,'core'=2,'dp'=4] {'y','core'}, dimensions={0} | all-to-all | bytes 524288 | tf_op jit(solution)/shard_map/while/body/eval_jaxpr/cond/branch_1_fun/all_to_all | solution.py:184
  386.0 0.3 branch_1_fun.3
  386.4 0.6 copy-done.3
  387.0 0.6 fusion.100
  387.6 0.6 slice_bitcast_fusion
  (88 shorter events, 3.2 us)
Async XLA Ops:
  0.6 66.2 %copy-start = (bf16[512,256]{1,0:T(8,128)(2,1)S(1)}, bf16[512,256]{1,0:T(8,128)(2,1)}, u32[]{:S(2)}) copy-start(bf16[512,256]{1,0:T(8,128)(2,1)} %param.36) | copy-start | bytes 786436
  0.7 0.7 copy-start.12
  0.7 0.7 copy-start.13
  1.4 0.7 copy-start.17
  20.9 0.7 copy-start.6
  20.9 0.7 copy-start.7
  20.9 0.7 copy-start.8
  20.9 0.7 copy-start.10
  20.9 0.7 copy-start.11
  21.7 45.2 %copy-start.14 = (f32[512]{0:T(512)S(1)}, f32[512]{0:T(512)}, u32[]{:S(2)}) copy-start(f32[512]{0:T(512)} %param.35) | copy-start | bytes 6148
  21.7 45.2 %copy-start.15 = (f32[512]{0:T(512)S(1)}, f32[512]{0:T(512)}, u32[]{:S(2)}) copy-start(f32[512]{0:T(512)} %param.34) | copy-start | bytes 6148
  21.7 45.2 %copy-start.16 = (f32[256]{0:T(256)S(1)}, f32[256]{0:T(256)}, u32[]{:S(2)}) copy-start(f32[256]{0:T(256)} %param.37) | copy-start | bytes 3076
  21.7 45.5 %copy-start.2 = (bf16[1,4096,128]{2,1,0:T(8,128)(2,1)S(1)}, bf16[1,4096,128]{2,1,0:T(8,128)(2,1)}, u32[]{:S(2)}) copy-start(bf16[1,4096,128]{2,1,0:T(8,128)(2,1)} %param.40) | copy-start | bytes 3145732
  65.1 2.1 copy-start.1
  67.1 0.7 copy-start.4
  67.1 0.7 copy-start.5
  67.2 0.7 copy-start.9
  67.9 4.6 %collective-permute-start = (bf16[64,256]{1,0:T(8,128)(2,1)S(1)}, bf16[64,256]{1,0:T(8,128)(2,1)S(1)}, u32[]{:S(2)}, u32[]{:S(2)}) collective-permute-start(bf16[64,256]{1,0:T(8,128)(2,1)S(1)} %get-tuple-element.556), channel_id=1, source_target_pairs={{0,64},{64,128},{128,192},{192,256},{256,320},{320,384},{384,448},... | collective-permute-start | bytes 98312 | tf_op jit(solution)/shard_map/while/body/eval_jaxpr/ppermute | solution.py:213
  72.5 4.6 %collective-permute-start = (bf16[64,256]{1,0:T(8,128)(2,1)S(1)}, bf16[64,256]{1,0:T(8,128)(2,1)S(1)}, u32[]{:S(2)}, u32[]{:S(2)}) collective-permute-start(bf16[64,256]{1,0:T(8,128)(2,1)S(1)} %get-tuple-element.556), channel_id=1, source_target_pairs={{0,64},{64,128},{128,192},{192,256},{256,320},{320,384},{384,448},... | collective-permute-start | bytes 98312 | tf_op jit(solution)/shard_map/while/body/eval_jaxpr/ppermute | solution.py:213
  77.2 4.6 %collective-permute-start = (bf16[64,256]{1,0:T(8,128)(2,1)S(1)}, bf16[64,256]{1,0:T(8,128)(2,1)S(1)}, u32[]{:S(2)}, u32[]{:S(2)}) collective-permute-start(bf16[64,256]{1,0:T(8,128)(2,1)S(1)} %get-tuple-element.556), channel_id=1, source_target_pairs={{0,64},{64,128},{128,192},{192,256},{256,320},{320,384},{384,448},... | collective-permute-start | bytes 98312 | tf_op jit(solution)/shard_map/while/body/eval_jaxpr/ppermute | solution.py:213
  81.8 4.6 %collective-permute-start = (bf16[64,256]{1,0:T(8,128)(2,1)S(1)}, bf16[64,256]{1,0:T(8,128)(2,1)S(1)}, u32[]{:S(2)}, u32[]{:S(2)}) collective-permute-start(bf16[64,256]{1,0:T(8,128)(2,1)S(1)} %get-tuple-element.556), channel_id=1, source_target_pairs={{0,64},{64,128},{128,192},{192,256},{256,320},{320,384},{384,448},... | collective-permute-start | bytes 98312 | tf_op jit(solution)/shard_map/while/body/eval_jaxpr/ppermute | solution.py:213
  86.5 4.6 %collective-permute-start = (bf16[64,256]{1,0:T(8,128)(2,1)S(1)}, bf16[64,256]{1,0:T(8,128)(2,1)S(1)}, u32[]{:S(2)}, u32[]{:S(2)}) collective-permute-start(bf16[64,256]{1,0:T(8,128)(2,1)S(1)} %get-tuple-element.556), channel_id=1, source_target_pairs={{0,64},{64,128},{128,192},{192,256},{256,320},{320,384},{384,448},... | collective-permute-start | bytes 98312 | tf_op jit(solution)/shard_map/while/body/eval_jaxpr/ppermute | solution.py:213
  91.1 4.8 %collective-permute-start = (bf16[64,256]{1,0:T(8,128)(2,1)S(1)}, bf16[64,256]{1,0:T(8,128)(2,1)S(1)}, u32[]{:S(2)}, u32[]{:S(2)}) collective-permute-start(bf16[64,256]{1,0:T(8,128)(2,1)S(1)} %get-tuple-element.556), channel_id=1, source_target_pairs={{0,64},{64,128},{128,192},{192,256},{256,320},{320,384},{384,448},... | collective-permute-start | bytes 98312 | tf_op jit(solution)/shard_map/while/body/eval_jaxpr/ppermute | solution.py:213
  95.9 5.9 %collective-permute-start = (bf16[64,256]{1,0:T(8,128)(2,1)S(1)}, bf16[64,256]{1,0:T(8,128)(2,1)S(1)}, u32[]{:S(2)}, u32[]{:S(2)}) collective-permute-start(bf16[64,256]{1,0:T(8,128)(2,1)S(1)} %get-tuple-element.556), channel_id=1, source_target_pairs={{0,64},{64,128},{128,192},{192,256},{256,320},{320,384},{384,448},... | collective-permute-start | bytes 98312 | tf_op jit(solution)/shard_map/while/body/eval_jaxpr/ppermute | solution.py:213
  101.7 205.2 %collective-permute-start = (bf16[64,256]{1,0:T(8,128)(2,1)S(1)}, bf16[64,256]{1,0:T(8,128)(2,1)S(1)}, u32[]{:S(2)}, u32[]{:S(2)}) collective-permute-start(bf16[64,256]{1,0:T(8,128)(2,1)S(1)} %get-tuple-element.556), channel_id=1, source_target_pairs={{0,64},{64,128},{128,192},{192,256},{256,320},{320,384},{384,448},... | collective-permute-start | bytes 98312 | tf_op jit(solution)/shard_map/while/body/eval_jaxpr/ppermute | solution.py:213
  343.5 6.3 %collective-permute-start = (bf16[64,256]{1,0:T(8,128)(2,1)S(1)}, bf16[64,256]{1,0:T(8,128)(2,1)S(1)}, u32[]{:S(2)}, u32[]{:S(2)}) collective-permute-start(bf16[64,256]{1,0:T(8,128)(2,1)S(1)} %get-tuple-element.556), channel_id=1, source_target_pairs={{0,64},{64,128},{128,192},{192,256},{256,320},{320,384},{384,448},... | collective-permute-start | bytes 98312 | tf_op jit(solution)/shard_map/while/body/eval_jaxpr/ppermute | solution.py:213
  386.4 0.6 copy-start.3

commit v6 on v5

--- a/solution.py
+++ b/solution.py
@@ -1,3 +1,5 @@
+import functools
+
 import jax
 import jax.numpy as jnp
 from jax import lax
@@ -49,18 +51,19 @@
     return jnp.dot(left, right, preferred_element_type=jnp.float32)
 
 
-def mixing_kernel(place, rows_ref, gain, shift, query, key, value, masking, out):
+def mixing_kernel(frame_total, place, rows_ref, gain, shift, query, key, value, live, out):
     rows, model = rows_ref.shape
     width = 2 * HEAD_DIM
     spans = [slice(at, at + width) for at in range(0, model, width)]
-    total = jnp.zeros((rows, 1), jnp.float32)
+    total = jnp.zeros((rows, width), jnp.float32)
     for span in spans:
-        total += jnp.sum(rows_ref[:, span].astype(jnp.float32), axis=-1, keepdims=True)
-    average = total / model
-    spread = jnp.zeros_like(average)
+        total += rows_ref[:, span].astype(jnp.float32)
+    average = jnp.sum(total, axis=-1, keepdims=True) / model
+    total = jnp.zeros((rows, width), jnp.float32)
     for span in spans:
         centered = rows_ref[:, span].astype(jnp.float32) - average
-        spread += jnp.sum(centered * centered, axis=-1, keepdims=True)
+        total += centered * centered
+    spread = jnp.sum(total, axis=-1, keepdims=True)
     scale = lax.rsqrt(spread / model + 1e-05)
     both = jnp.zeros((rows, 2 * HEAD_DIM), jnp.float32)
     values = jnp.zeros((rows, HEAD_DIM), jnp.float32)
@@ -74,7 +77,9 @@
     scores = lax.dot_general(
         queries, key_rows, (((1,), (1,)), ((), ())), preferred_element_type=jnp.float32
     )
-    scores = jnp.where(masking[place[0]] > 0, scores, -jnp.inf)
+    owner = lax.broadcasted_iota(jnp.int32, (rows, rows), 0) // frame_total
+    column = lax.broadcasted_iota(jnp.int32, (rows, rows), 1) // frame_total
+    scores = jnp.where((owner == column) & (live[place[0]] > 0), scores, -jnp.inf)
     raised = jnp.exp(scores - jnp.max(scores, axis=-1, keepdims=True))
     attention = (raised / jnp.sum(raised, axis=-1, keepdims=True)).astype(jnp.bfloat16)
     mixture = product(attention, values.astype(jnp.bfloat16)).astype(jnp.bfloat16)
@@ -83,9 +88,9 @@
 
 def leaving_kernel(place, mixed, current, weights, bias, _, out, outputs):
     total = current[...].astype(jnp.float32) + bias[...]
-    for i in range(0, mixed.shape[0], 2):
-        pair = jnp.concatenate([mixed[i], mixed[i + 1]], axis=1)
-        total += product(pair, weights[i // 2])
+    for i in range(mixed.shape[1]):
+        pair = jnp.concatenate([mixed[0, i], mixed[1, i]], axis=1)
+        total += product(pair, weights[i])
     result = total.astype(jnp.bfloat16)
     out[...] = result
     outputs[place[0]] = result
@@ -142,16 +147,14 @@
     entering = (product(normed_frames, proj_weight) + proj_bias).astype(jnp.bfloat16)
     entering = entering.reshape(MICRO, rows, columns)
 
-    owner = lax.broadcasted_iota(jnp.int32, (rows, rows), 0) // frame_total
-    column = lax.broadcasted_iota(jnp.int32, (rows, rows), 1) // frame_total
-    maskings = jnp.where((owner == column)[None] & live.reshape(MICRO, 1, rows), 1.0, 0.0)
+    live_keys = live.reshape(MICRO, 1, rows).astype(jnp.float32)
     out_part = out_weight.reshape(group // 2, 2 * HEAD_DIM, columns)
 
     vmem = pl.BlockSpec(memory_space=pltpu.VMEM)
     smem = pl.BlockSpec(memory_space=pltpu.SMEM)
     mixing = pl.pallas_call(
-        mixing_kernel,
-        out_shape=jax.ShapeDtypeStruct((group, rows, HEAD_DIM), jnp.bfloat16),
+        functools.partial(mixing_kernel, frame_total),
+        out_shape=jax.ShapeDtypeStruct((chips, rows, HEAD_DIM), jnp.bfloat16),
         in_specs=[smem] + [vmem] * 7,
         out_specs=vmem,
         compiler_params=pltpu.CompilerParams(vmem_limit_bytes=24 * 2**20),
@@ -179,9 +182,10 @@
             query_weight[0],
             key_weight[0],
             value_weight[0],
-            maskings,
-        )
-        mixed = lax.all_to_all(copies, ("y", "core"), 0, 0, tiled=True)
+            live_keys,
+        )
+        chip_mixed = lax.all_to_all(copies, "y", 0, 0, tiled=True)
+        mixed = lax.all_gather(chip_mixed, "core", axis=0, tiled=False)
         return leaving(place, mixed, current, out_part, out_bias, outputs)
 
     def gradients_of():

time: 389 us -> 396 us (1.018)
  local copies, waits for them, and re-layouts: 5.72 us -> 11 us
    all_to_all x2, blocking collectives: 34.3 us -> 23.3 us  [attend(): chip_mixed = lax.all_to_all(copies, 'y', 0, 0, tiled=True)]
    all_gather x0 -> x2, blocking collectives: none -> 6.56 us  [attend(): mixed = lax.all_gather(chip_mixed, 'core', axis=0, tiled=False)]
where the time goes in v6:
time: 396 us; the launch traced here: 395 us
  waiting for transfers between devices  235 us (59%)
  blocking collectives  120 us (30%)
  starting transfers between devices  11.5 us (3%)
  local copies, waits for them, and re-layouts  11 us (3%)
  other arithmetic  5.88 us (1%)
  Pallas kernels  5.81 us (1%)
    ppermute x9, waiting for transfers between devices, advance(): lax.ppermute(previous, 'section', [(s, s + 1) for s in range(sections - 1)])  235 us
    psum x3, blocking collectives, gradients_of(): return lax.psum(lax.psum(lax.psum(packed, 'core'), 'dp'), 'y')  38.2 us
    all_gather x2, blocking collectives, attend(): whole = lax.all_gather(current, ('y', 'core'), axis=1, tiled=True)  34.3 us
    all_to_all x2, blocking collectives, attend(): chip_mixed = lax.all_to_all(copies, 'y', 0, 0, tiled=True)  23.3 us
    all_gather x1, blocking collectives, on_device(): lax.all_gather(wave[0].astype(jnp.float32), ('y', 'core'), axis=0, tiled=...  17.9 us
    ppermute x9, starting transfers between devices, advance(): lax.ppermute(previous, 'section', [(s, s + 1) for s in range(sections - 1)])  11.5 us
  transfers between devices with their start and end apart: 9, of which 9 were waited for; matrix products, arithmetic and copies ran while one was open for 0% of the time, Pallas kernels for 0%

profile of v6, /device:TPU:449, one launch (start us, length us, event | category | flops | bytes accessed | tf_op | source)
XLA Modules:
  0.0 394.7 jit_solution(1480419898486122154)
XLA Ops:
  0.7 0.7 copy-done.15
  2.5 17.9 %all-gather.1 = f32[16,1,40]{2,1,0:T(1,128)S(1)} all-gather(f32[1,1,40]{2,1,0:T(1,128)S(1)} %convert_element_type.97), channel_id=3, replica_groups=mesh['section'=8,'y'=8,'core'=2,'dp'=4] {'y','core'}, dimensions={0}, use_global_device_ids=true | all-gather | bytes 2720 | tf_op jit(solution)/shard_map/all_gather | solution.py:130
  21.4 44.1 %conditional.3 = (f32[16,512]{1,0:T(8,128)}) conditional(s32[]{:T(128)} %convert_element_type.93, () %tuple.42, (s32[]{:T(128)}, s32[]{:T(128)}, s32[1,16]{1,0:T(1,128)S(1)}, bf16[1,1,40]{2,1,0:T(2,128)(2,1)S(1)}, bf16[512,10]{0,1:T(8,128)(2,1)S(1)}, /*index=5*/f32[512]{0:T(512)S(1)}, f32[512]{0:T(512)S(1)}, f32[512]{0:T(512)S(1)}, ...), branch_computations={%region_6.7_spmd, %region_7.18_spmd} | conditional | flops 1064623 | bytes 458498 | solution.py:210
  22.0 0.7 reduce.36
  22.6 0.6 fusion.97
  25.3 0.7 fusion.21
  27.3 3.4 psum.36
  30.8 13.3 %psum.37 = f32[16,512]{1,0:T(8,128)S(1)} all-reduce(f32[16,512]{1,0:T(8,128)S(1)} %psum.36), channel_id=1, replica_groups=mesh['section'=8,'y'=8,'core'=2,'dp'=4] {'dp'}, use_global_device_ids=true, to_apply=%region_16.16 | all-reduce | flops 8192 | bytes 65536 | tf_op jit(solution)/shard_map/cond/branch_1_fun/psum | solution.py:207
  44.1 21.4 %psum.38 = f32[16,512]{1,0:T(8,128)} all-reduce(f32[16,512]{1,0:T(8,128)S(1)} %psum.37), channel_id=1, replica_groups=mesh['section'=8,'y'=8,'core'=2,'dp'=4] {'y'}, use_global_device_ids=true, to_apply=%region_17.17 | all-reduce | flops 8192 | bytes 65536 | tf_op jit(solution)/shard_map/cond/branch_1_fun/psum | solution.py:207
  66.0 0.8 convert_reduce_fusion
  67.2 0.9 fusion.54
  68.2 0.7 copy-done.5
  68.9 322.4 %while.16 = (s32[]{:T(128)}, bf16[64,256]{1,0:T(8,128)(2,1)S(1)}, bf16[2,64,256]{2,1,0:T(8,128)(2,1)S(1)}, s32[]{:T(128)}, bf16[2,64,256]{2,1,0:T(8,128)(2,1)}, ...) while((s32[]{:T(128)}, bf16[64,256]{1,0:T(8,128)(2,1)S(1)}, ...), condition=%wide.region_21.22_spmd.clone, body=%wide.region_18.21_spmd.clone.sunk | while | flops 16650 | bytes 5643565 | solution.py:234
  68.9 1.3 collective-permute-start
  70.3 3.2 collective-permute-done
  73.5 1.3 collective-permute-start
  75.0 3.2 collective-permute-done
  78.2 1.3 collective-permute-start
  79.6 3.2 collective-permute-done
  82.8 1.3 collective-permute-start
  84.3 3.2 collective-permute-done
  87.5 1.3 collective-permute-start
  88.9 3.2 collective-permute-done
  92.1 1.3 collective-permute-start
  93.6 3.3 collective-permute-done
  96.9 1.3 collective-permute-start
  98.3 4.4 %collective-permute-done = bf16[64,256]{1,0:T(8,128)(2,1)S(1)} collective-permute-done((bf16[64,256]{1,0:T(8,128)(2,1)S(1)}, bf16[64,256]{1,0:T(8,128)(2,1)S(1)}, u32[]{:S(2)}, u32[]{:S(2)}) %collective-permute-start) | collective-permute-done | bytes 32800 | tf_op jit(solution)/shard_map/while/body/eval_jaxpr/ppermute | solution.py:217
  102.7 1.3 collective-permute-start
  104.2 206.8 %collective-permute-done = bf16[64,256]{1,0:T(8,128)(2,1)S(1)} collective-permute-done((bf16[64,256]{1,0:T(8,128)(2,1)S(1)}, bf16[64,256]{1,0:T(8,128)(2,1)S(1)}, u32[]{:S(2)}, u32[]{:S(2)}) %collective-permute-start) | collective-permute-done | bytes 32800 | tf_op jit(solution)/shard_map/while/body/eval_jaxpr/ppermute | solution.py:217
  311.0 37.0 %conditional.7 = ((bf16[64,256]{1,0:T(8,128)(2,1)S(1)}, bf16[2,64,256]{2,1,0:T(8,128)(2,1)S(1)})) conditional(s32[]{:T(128)} %convert_element_type.131, (bf16[64,256]{1,0:T(8,128)(2,1)S(1)}, bf16[2,64,256]{2,1,0:T(8,128)(2,1)S(1)}) %tuple.85, (s32[]{:T(128)}, s32[]{:T(128)}, bf16[2,64,256]{2,1,0:T(8,128)(2,1)}, bf16[64,256]{1,0:T(8,128)(2,1)S(1)}, ...), branch_computations={%region_19.19_spmd, %region_20.20_spmd} | conditional | flops 16387 | bytes 5509250 | solution.py:226
  311.6 0.8 bitcast_select_fusion.current
  312.4 17.2 %all_gather.8.rows_ref = bf16[64,4096]{1,0:T(8,128)(2,1)S(1)} all-gather(bf16[64,256]{1,0:T(8,128)(2,1)S(1)} %bitcast_select_fusion.current), channel_id=1, replica_groups=mesh['section'=8,'y'=8,'core'=2,'dp'=4] {'y','core'}, dimensions={1}, use_global_device_ids=true | all-gather | bytes 557056 | tf_op jit(solution)/shard_map/while/body/eval_jaxpr/cond/branch_1_fun/all_gather | solution.py:176
  329.5 0.7 copy-done.9
  330.2 2.6 branch_1_fun.2
  332.8 11.7 %all_to_all.4 = bf16[8,64,128]{2,1,0:T(8,128)(2,1)S(1)} all-to-all(bf16[8,64,128]{2,1,0:T(8,128)(2,1)S(1)} %branch_1_fun.2), channel_id=1, replica_groups=mesh['section'=8,'y'=8,'core'=2,'dp'=4] {'y'}, dimensions={0} | all-to-all | bytes 262144 | tf_op jit(solution)/shard_map/while/body/eval_jaxpr/cond/branch_1_fun/all_to_all | solution.py:187
  344.5 3.3 all-gather
  348.1 1.3 collective-permute-start
  349.5 4.7 %collective-permute-done = bf16[64,256]{1,0:T(8,128)(2,1)S(1)} collective-permute-done((bf16[64,256]{1,0:T(8,128)(2,1)S(1)}, bf16[64,256]{1,0:T(8,128)(2,1)S(1)}, u32[]{:S(2)}, u32[]{:S(2)}) %collective-permute-start) | collective-permute-done | bytes 32800 | tf_op jit(solution)/shard_map/while/body/eval_jaxpr/ppermute | solution.py:217
  354.2 37.0 %conditional.7 = ((bf16[64,256]{1,0:T(8,128)(2,1)S(1)}, bf16[2,64,256]{2,1,0:T(8,128)(2,1)S(1)})) conditional(s32[]{:T(128)} %convert_element_type.131, (bf16[64,256]{1,0:T(8,128)(2,1)S(1)}, bf16[2,64,256]{2,1,0:T(8,128)(2,1)S(1)}) %tuple.85, (s32[]{:T(128)}, s32[]{:T(128)}, bf16[2,64,256]{2,1,0:T(8,128)(2,1)}, bf16[64,256]{1,0:T(8,128)(2,1)S(1)}, ...), branch_computations={%region_19.19_spmd, %region_20.20_spmd} | conditional | flops 16387 | bytes 5509250 | solution.py:226
  354.8 0.8 bitcast_select_fusion.current
  355.6 17.2 %all_gather.8.rows_ref = bf16[64,4096]{1,0:T(8,128)(2,1)S(1)} all-gather(bf16[64,256]{1,0:T(8,128)(2,1)S(1)} %bitcast_select_fusion.current), channel_id=1, replica_groups=mesh['section'=8,'y'=8,'core'=2,'dp'=4] {'y','core'}, dimensions={1}, use_global_device_ids=true | all-gather | bytes 557056 | tf_op jit(solution)/shard_map/while/body/eval_jaxpr/cond/branch_1_fun/all_gather | solution.py:176
  372.7 0.7 copy-done.9
  373.4 2.6 branch_1_fun.2
  376.0 11.7 %all_to_all.4 = bf16[8,64,128]{2,1,0:T(8,128)(2,1)S(1)} all-to-all(bf16[8,64,128]{2,1,0:T(8,128)(2,1)S(1)} %branch_1_fun.2), channel_id=1, replica_groups=mesh['section'=8,'y'=8,'core'=2,'dp'=4] {'y'}, dimensions={0} | all-to-all | bytes 262144 | tf_op jit(solution)/shard_map/while/body/eval_jaxpr/cond/branch_1_fun/all_to_all | solution.py:187
  387.7 3.3 all-gather
  391.3 0.6 copy-done.4
  391.9 1.4 fusion.100
  393.3 1.4 slice_bitcast_fusion
  (121 shorter events, 8.0 us)
Async XLA Ops:
  0.6 66.6 %copy-start = (bf16[512,256]{1,0:T(8,128)(2,1)S(1)}, bf16[512,256]{1,0:T(8,128)(2,1)}, u32[]{:S(2)}) copy-start(bf16[512,256]{1,0:T(8,128)(2,1)} %param.36) | copy-start | bytes 786436
  0.7 0.7 copy-start.15
  0.7 0.7 copy-start.16
  1.4 0.7 copy-start.20
  20.6 0.7 copy-start.7
  20.6 0.7 copy-start.10
  20.6 0.7 copy-start.11
  20.6 0.7 copy-start.13
  20.6 0.7 copy-start.14
  21.4 45.8 %copy-start.17 = (f32[512]{0:T(512)S(1)}, f32[512]{0:T(512)}, u32[]{:S(2)}) copy-start(f32[512]{0:T(512)} %param.35) | copy-start | bytes 6148
  21.4 45.8 %copy-start.18 = (f32[512]{0:T(512)S(1)}, f32[512]{0:T(512)}, u32[]{:S(2)}) copy-start(f32[512]{0:T(512)} %param.34) | copy-start | bytes 6148
  21.4 45.8 %copy-start.19 = (f32[256]{0:T(256)S(1)}, f32[256]{0:T(256)}, u32[]{:S(2)}) copy-start(f32[256]{0:T(256)} %param.37) | copy-start | bytes 3076
  21.4 46.8 %copy-start.2 = (bf16[1,4096,128]{2,1,0:T(8,128)(2,1)S(1)}, bf16[1,4096,128]{2,1,0:T(8,128)(2,1)}, u32[]{:S(2)}) copy-start(bf16[1,4096,128]{2,1,0:T(8,128)(2,1)} %param.41) | copy-start | bytes 3145732
  65.5 2.7 copy-start.1
  68.1 0.7 copy-start.5
  68.1 0.7 copy-start.6
  68.1 0.7 copy-start.12
  68.9 4.6 %collective-permute-start = (bf16[64,256]{1,0:T(8,128)(2,1)S(1)}, bf16[64,256]{1,0:T(8,128)(2,1)S(1)}, u32[]{:S(2)}, u32[]{:S(2)}) collective-permute-start(bf16[64,256]{1,0:T(8,128)(2,1)S(1)} %get-tuple-element.597), channel_id=1, source_target_pairs={{0,64},{64,128},{128,192},{192,256},{256,320},{320,384},{384,448},... | collective-permute-start | bytes 98312 | tf_op jit(solution)/shard_map/while/body/eval_jaxpr/ppermute | solution.py:217
  73.5 4.6 %collective-permute-start = (bf16[64,256]{1,0:T(8,128)(2,1)S(1)}, bf16[64,256]{1,0:T(8,128)(2,1)S(1)}, u32[]{:S(2)}, u32[]{:S(2)}) collective-permute-start(bf16[64,256]{1,0:T(8,128)(2,1)S(1)} %get-tuple-element.597), channel_id=1, source_target_pairs={{0,64},{64,128},{128,192},{192,256},{256,320},{320,384},{384,448},... | collective-permute-start | bytes 98312 | tf_op jit(solution)/shard_map/while/body/eval_jaxpr/ppermute | solution.py:217
  78.2 4.6 %collective-permute-start = (bf16[64,256]{1,0:T(8,128)(2,1)S(1)}, bf16[64,256]{1,0:T(8,128)(2,1)S(1)}, u32[]{:S(2)}, u32[]{:S(2)}) collective-permute-start(bf16[64,256]{1,0:T(8,128)(2,1)S(1)} %get-tuple-element.597), channel_id=1, source_target_pairs={{0,64},{64,128},{128,192},{192,256},{256,320},{320,384},{384,448},... | collective-permute-start | bytes 98312 | tf_op jit(solution)/shard_map/while/body/eval_jaxpr/ppermute | solution.py:217
  82.8 4.6 %collective-permute-start = (bf16[64,256]{1,0:T(8,128)(2,1)S(1)}, bf16[64,256]{1,0:T(8,128)(2,1)S(1)}, u32[]{:S(2)}, u32[]{:S(2)}) collective-permute-start(bf16[64,256]{1,0:T(8,128)(2,1)S(1)} %get-tuple-element.597), channel_id=1, source_target_pairs={{0,64},{64,128},{128,192},{192,256},{256,320},{320,384},{384,448},... | collective-permute-start | bytes 98312 | tf_op jit(solution)/shard_map/while/body/eval_jaxpr/ppermute | solution.py:217
  87.5 4.6 %collective-permute-start = (bf16[64,256]{1,0:T(8,128)(2,1)S(1)}, bf16[64,256]{1,0:T(8,128)(2,1)S(1)}, u32[]{:S(2)}, u32[]{:S(2)}) collective-permute-start(bf16[64,256]{1,0:T(8,128)(2,1)S(1)} %get-tuple-element.597), channel_id=1, source_target_pairs={{0,64},{64,128},{128,192},{192,256},{256,320},{320,384},{384,448},... | collective-permute-start | bytes 98312 | tf_op jit(solution)/shard_map/while/body/eval_jaxpr/ppermute | solution.py:217
  92.1 4.8 %collective-permute-start = (bf16[64,256]{1,0:T(8,128)(2,1)S(1)}, bf16[64,256]{1,0:T(8,128)(2,1)S(1)}, u32[]{:S(2)}, u32[]{:S(2)}) collective-permute-start(bf16[64,256]{1,0:T(8,128)(2,1)S(1)} %get-tuple-element.597), channel_id=1, source_target_pairs={{0,64},{64,128},{128,192},{192,256},{256,320},{320,384},{384,448},... | collective-permute-start | bytes 98312 | tf_op jit(solution)/shard_map/while/body/eval_jaxpr/ppermute | solution.py:217
  96.9 5.9 %collective-permute-start = (bf16[64,256]{1,0:T(8,128)(2,1)S(1)}, bf16[64,256]{1,0:T(8,128)(2,1)S(1)}, u32[]{:S(2)}, u32[]{:S(2)}) collective-permute-start(bf16[64,256]{1,0:T(8,128)(2,1)S(1)} %get-tuple-element.597), channel_id=1, source_target_pairs={{0,64},{64,128},{128,192},{192,256},{256,320},{320,384},{384,448},... | collective-permute-start | bytes 98312 | tf_op jit(solution)/shard_map/while/body/eval_jaxpr/ppermute | solution.py:217
  102.7 208.3 %collective-permute-start = (bf16[64,256]{1,0:T(8,128)(2,1)S(1)}, bf16[64,256]{1,0:T(8,128)(2,1)S(1)}, u32[]{:S(2)}, u32[]{:S(2)}) collective-permute-start(bf16[64,256]{1,0:T(8,128)(2,1)S(1)} %get-tuple-element.597), channel_id=1, source_target_pairs={{0,64},{64,128},{128,192},{192,256},{256,320},{320,384},{384,448},... | collective-permute-start | bytes 98312 | tf_op jit(solution)/shard_map/while/body/eval_jaxpr/ppermute | solution.py:217
  311.0 0.6 copy-start.8
  329.5 0.7 copy-start.9
  330.2 17.6 %copy-start.3 = (bf16[8,256,256]{2,1,0:T(8,128)(2,1)S(1)}, bf16[8,256,256]{2,1,0:T(8,128)(2,1)}, u32[]{:S(2)}) copy-start(bf16[8,256,256]{2,1,0:T(8,128)(2,1)} %get-tuple-element.299.weights) | copy-start | bytes 3145732 | tf_op jit(solution)/shard_map/while/body/eval_jaxpr/cond
  348.1 6.1 %collective-permute-start = (bf16[64,256]{1,0:T(8,128)(2,1)S(1)}, bf16[64,256]{1,0:T(8,128)(2,1)S(1)}, u32[]{:S(2)}, u32[]{:S(2)}) collective-permute-start(bf16[64,256]{1,0:T(8,128)(2,1)S(1)} %get-tuple-element.597), channel_id=1, source_target_pairs={{0,64},{64,128},{128,192},{192,256},{256,320},{320,384},{384,448},... | collective-permute-start | bytes 98312 | tf_op jit(solution)/shard_map/while/body/eval_jaxpr/ppermute | solution.py:217
  354.2 0.6 copy-start.8
  372.7 0.7 copy-start.9
  373.4 17.6 %copy-start.3 = (bf16[8,256,256]{2,1,0:T(8,128)(2,1)S(1)}, bf16[8,256,256]{2,1,0:T(8,128)(2,1)}, u32[]{:S(2)}) copy-start(bf16[8,256,256]{2,1,0:T(8,128)(2,1)} %get-tuple-element.299.weights) | copy-start | bytes 3145732 | tf_op jit(solution)/shard_map/while/body/eval_jaxpr/cond
  391.3 0.6 copy-start.4

commit v7 on v5

--- a/solution.py
+++ b/solution.py
@@ -49,36 +49,35 @@
     return jnp.dot(left, right, preferred_element_type=jnp.float32)
 
 
-def mixing_kernel(place, rows_ref, gain, shift, query, key, value, masking, out):
+def mixing_kernel(rows_ref, gain, shift, query, key, value, masking, out):
     rows, model = rows_ref.shape
-    width = 2 * HEAD_DIM
-    spans = [slice(at, at + width) for at in range(0, model, width)]
-    total = jnp.zeros((rows, 1), jnp.float32)
+    parts, width = query.shape[0], query.shape[1]
+    spans = [slice(i * width, (i + 1) * width) for i in range(parts)]
+    total = jnp.zeros((rows, width), jnp.float32)
     for span in spans:
-        total += jnp.sum(rows_ref[:, span].astype(jnp.float32), axis=-1, keepdims=True)
-    average = total / model
-    spread = jnp.zeros_like(average)
+        total += rows_ref[:, span].astype(jnp.float32)
+    average = jnp.sum(total, axis=-1, keepdims=True) / model
+    total = jnp.zeros((rows, width), jnp.float32)
     for span in spans:
         centered = rows_ref[:, span].astype(jnp.float32) - average
-        spread += jnp.sum(centered * centered, axis=-1, keepdims=True)
-    scale = lax.rsqrt(spread / model + 1e-05)
+        total += centered * centered
+    scale = lax.rsqrt(jnp.sum(total, axis=-1, keepdims=True) / model + 1e-05)
     both = jnp.zeros((rows, 2 * HEAD_DIM), jnp.float32)
     values = jnp.zeros((rows, HEAD_DIM), jnp.float32)
-    for span in spans:
+    for i, span in enumerate(spans):
         centered = rows_ref[:, span].astype(jnp.float32) - average
-        normed = (centered * scale * gain[:, span] + shift[:, span]).astype(jnp.bfloat16)
-        both += product(normed, jnp.concatenate([query[span], key[span]], axis=1))
-        values += product(normed, value[span])
+        normed = (centered * scale * gain[i] + shift[i]).astype(jnp.bfloat16)
+        both += product(normed, jnp.concatenate([query[i], key[i]], axis=1))
+        values += product(normed, value[i])
     queries = (both[:, :HEAD_DIM] * HEAD_DIM ** (-0.5)).astype(jnp.bfloat16)
     key_rows = both[:, HEAD_DIM:].astype(jnp.bfloat16)
     scores = lax.dot_general(
         queries, key_rows, (((1,), (1,)), ((), ())), preferred_element_type=jnp.float32
     )
-    scores = jnp.where(masking[place[0]] > 0, scores, -jnp.inf)
+    scores = jnp.where(masking[...] > 0, scores, -jnp.inf)
     raised = jnp.exp(scores - jnp.max(scores, axis=-1, keepdims=True))
     attention = (raised / jnp.sum(raised, axis=-1, keepdims=True)).astype(jnp.bfloat16)
-    mixture = product(attention, values.astype(jnp.bfloat16)).astype(jnp.bfloat16)
-    out[...] = jnp.broadcast_to(mixture[None], out.shape)
+    out[...] = product(attention, values.astype(jnp.bfloat16)).astype(jnp.bfloat16)
 
 
 def leaving_kernel(place, mixed, current, weights, bias, _, out, outputs):
@@ -145,14 +144,20 @@
     owner = lax.broadcasted_iota(jnp.int32, (rows, rows), 0) // frame_total
     column = lax.broadcasted_iota(jnp.int32, (rows, rows), 1) // frame_total
     maskings = jnp.where((owner == column)[None] & live.reshape(MICRO, 1, rows), 1.0, 0.0)
+    gain = norm_gain.reshape(group, 1, columns)
+    shift = norm_shift.reshape(group, 1, columns)
+    query, key, value = (
+        weight.reshape(group, columns, HEAD_DIM)
+        for weight in (query_weight, key_weight, value_weight)
+    )
     out_part = out_weight.reshape(group // 2, 2 * HEAD_DIM, columns)
 
     vmem = pl.BlockSpec(memory_space=pltpu.VMEM)
     smem = pl.BlockSpec(memory_space=pltpu.SMEM)
     mixing = pl.pallas_call(
         mixing_kernel,
-        out_shape=jax.ShapeDtypeStruct((group, rows, HEAD_DIM), jnp.bfloat16),
-        in_specs=[smem] + [vmem] * 7,
+        out_shape=jax.ShapeDtypeStruct((rows, HEAD_DIM), jnp.bfloat16),
+        in_specs=[vmem] * 7,
         out_specs=vmem,
         compiler_params=pltpu.CompilerParams(vmem_limit_bytes=24 * 2**20),
     )
@@ -171,16 +176,9 @@
     def attend(current, slot, outputs):
         place = slot.reshape(1)
         whole = lax.all_gather(current, ("y", "core"), axis=1, tiled=True)
-        copies = mixing(
-            place,
-            whole,
-            norm_gain,
-            norm_shift,
-            query_weight[0],
-            key_weight[0],
-            value_weight[0],
-            maskings,
-        )
+        masking = lax.dynamic_index_in_dim(maskings, slot, 0, keepdims=False)
+        mixture = mixing(whole, gain, shift, query, key, value, masking)
+        copies = jnp.broadcast_to(mixture[None], (group,) + mixture.shape)
         mixed = lax.all_to_all(copies, ("y", "core"), 0, 0, tiled=True)
         return leaving(place, mixed, current, out_part, out_bias, outputs)
 

time: 389 us -> 396 us (1.018)
  no operation moved by 1% of the time
where the time goes in v7:
time: 396 us; the launch traced here: 395 us
  waiting for transfers between devices  237 us (60%)
  blocking collectives  123 us (31%)
  starting transfers between devices  11.5 us (3%)
  local copies, waits for them, and re-layouts  7.45 us (2%)
  other arithmetic  6.09 us (2%)
  Pallas kernels  5.84 us (1%)
    ppermute x9, waiting for transfers between devices, advance(): lax.ppermute(previous, 'section', [(s, s + 1) for s in range(sections - 1)])  237 us
    psum x3, blocking collectives, gradients_of(): return lax.psum(lax.psum(lax.psum(packed, 'core'), 'dp'), 'y')  38.2 us
    all_to_all x2, blocking collectives, attend(): mixed = lax.all_to_all(copies, ('y', 'core'), 0, 0, tiled=True)  34.3 us
    all_gather x2, blocking collectives, attend(): whole = lax.all_gather(current, ('y', 'core'), axis=1, tiled=True)  32.1 us
    all_gather x1, blocking collectives, on_device(): lax.all_gather(wave[0].astype(jnp.float32), ('y', 'core'), axis=0, tiled=...  17.9 us
    ppermute x9, starting transfers between devices, advance(): lax.ppermute(previous, 'section', [(s, s + 1) for s in range(sections - 1)])  11.5 us
  transfers between devices with their start and end apart: 9, of which 9 were waited for; matrix products, arithmetic and copies ran while one was open for 0% of the time, Pallas kernels for 0%

profile of v7, /device:TPU:449, one launch (start us, length us, event | category | flops | bytes accessed | tf_op | source)
XLA Modules:
  0.0 395.3 jit_solution(16488966293682716152)
XLA Ops:
  0.7 0.7 copy-done.13
  1.5 0.6 copy-done.18
  2.8 17.9 %all-gather = f32[16,1,40]{2,1,0:T(1,128)S(1)} all-gather(f32[1,1,40]{2,1,0:T(1,128)S(1)} %convert_element_type.85), channel_id=2, replica_groups=mesh['section'=8,'y'=8,'core'=2,'dp'=4] {'y','core'}, dimensions={0}, use_global_device_ids=true | all-gather | bytes 2720 | tf_op jit(solution)/shard_map/all_gather | solution.py:124
  21.1 0.6 copy-done.7
  21.7 44.2 %conditional.3 = (f32[16,512]{1,0:T(8,128)}) conditional(s32[]{:T(128)} %convert_element_type.82, () %tuple.42, (s32[]{:T(128)}, s32[]{:T(128)}, s32[1,16]{1,0:T(1,128)S(1)}, bf16[1,1,40]{2,1,0:T(2,128)(2,1)S(1)}, bf16[512,10]{0,1:T(8,128)(2,1)S(1)}, /*index=5*/f32[512]{0:T(512)S(1)}, f32[512]{0:T(512)S(1)}, f32[512]{0:T(512)S(1)}, ...), branch_computations={%region_6.7_spmd, %region_7.18_spmd} | conditional | flops 1064623 | bytes 458498 | solution.py:204
  21.7 0.5 broadcast.921
  22.3 0.7 reduce.36
  22.9 0.7 fusion.97
  25.6 0.7 fusion.21
  27.7 3.4 psum.36
  31.2 13.3 %psum.37 = f32[16,512]{1,0:T(8,128)S(1)} all-reduce(f32[16,512]{1,0:T(8,128)S(1)} %psum.36), channel_id=1, replica_groups=mesh['section'=8,'y'=8,'core'=2,'dp'=4] {'dp'}, use_global_device_ids=true, to_apply=%region_16.16 | all-reduce | flops 8192 | bytes 65536 | tf_op jit(solution)/shard_map/cond/branch_1_fun/psum | solution.py:201
  44.5 21.4 %psum.38 = f32[16,512]{1,0:T(8,128)} all-reduce(f32[16,512]{1,0:T(8,128)S(1)} %psum.37), channel_id=1, replica_groups=mesh['section'=8,'y'=8,'core'=2,'dp'=4] {'y'}, use_global_device_ids=true, to_apply=%region_17.17 | all-reduce | flops 8192 | bytes 65536 | tf_op jit(solution)/shard_map/cond/branch_1_fun/psum | solution.py:201
  65.9 0.3 fusion.101
  66.4 0.8 convert_reduce_fusion
  67.7 0.9 fusion.54
  68.6 0.7 copy-done.5
  69.3 322.6 %while.16 = (s32[]{:T(128)}, bf16[64,256]{1,0:T(8,128)(2,1)S(1)}, bf16[2,64,256]{2,1,0:T(8,128)(2,1)S(1)}, s32[]{:T(128)}, bf16[2,64,256]{2,1,0:T(8,128)(2,1)}, ...) while((s32[]{:T(128)}, bf16[64,256]{1,0:T(8,128)(2,1)S(1)}, ...), condition=%wide.region_21.22_spmd.clone, body=%wide.region_18.21_spmd.clone.sunk | while | flops 24586 | bytes 5804689 | solution.py:228
  69.3 1.3 collective-permute-start
  70.6 3.3 collective-permute-done
  73.9 1.3 collective-permute-start
  75.2 3.3 collective-permute-done
  78.6 1.3 collective-permute-start
  79.9 3.3 collective-permute-done
  83.2 1.3 collective-permute-start
  84.5 3.3 collective-permute-done
  87.9 1.3 collective-permute-start
  89.2 3.3 collective-permute-done
  92.5 1.3 collective-permute-start
  93.8 3.5 collective-permute-done
  97.3 1.3 collective-permute-start
  98.6 4.6 %collective-permute-done = bf16[64,256]{1,0:T(8,128)(2,1)S(1)} collective-permute-done((bf16[64,256]{1,0:T(8,128)(2,1)S(1)}, bf16[64,256]{1,0:T(8,128)(2,1)S(1)}, u32[]{:S(2)}, u32[]{:S(2)}) %collective-permute-start) | collective-permute-done | bytes 32800 | tf_op jit(solution)/shard_map/while/body/eval_jaxpr/ppermute | solution.py:211
  103.2 1.3 collective-permute-start
  104.5 207.1 %collective-permute-done = bf16[64,256]{1,0:T(8,128)(2,1)S(1)} collective-permute-done((bf16[64,256]{1,0:T(8,128)(2,1)S(1)}, bf16[64,256]{1,0:T(8,128)(2,1)S(1)}, u32[]{:S(2)}, u32[]{:S(2)}) %collective-permute-start) | collective-permute-done | bytes 32800 | tf_op jit(solution)/shard_map/while/body/eval_jaxpr/ppermute | solution.py:211
  311.5 37.0 %conditional.7 = ((bf16[64,256]{1,0:T(8,128)(2,1)S(1)}, bf16[2,64,256]{2,1,0:T(8,128)(2,1)S(1)})) conditional(s32[]{:T(128)} %convert_element_type.112, (bf16[64,256]{1,0:T(8,128)(2,1)S(1)}, bf16[2,64,256]{2,1,0:T(8,128)(2,1)S(1)}) %tuple.87, (s32[]{:T(128)}, s32[]{:T(128)}, bf16[2,64,256]{2,1,0:T(8,128)(2,1)}, bf16[64,256]{1,0:T(8,128)(2,1)S(1)}, ...), branch_computations={%region_19.19_spmd, %region_20.20_spmd} | conditional | flops 24579 | bytes 5673230 | solution.py:220
  311.6 0.8 bitcast_select_fusion.current
  312.3 16.1 %all_gather.4.rows_ref = bf16[64,4096]{1,0:T(8,128)(2,1)S(1)} all-gather(bf16[64,256]{1,0:T(8,128)(2,1)S(1)} %bitcast_select_fusion.current), channel_id=1, replica_groups=mesh['section'=8,'y'=8,'core'=2,'dp'=4] {'y','core'}, dimensions={1}, use_global_device_ids=true | all-gather | bytes 557056 | tf_op jit(solution)/shard_map/while/body/eval_jaxpr/cond/branch_1_fun/all_gather | solution.py:178
  328.4 2.6 branch_1_fun.2
  331.1 17.2 %all_to_all.4.mixed = bf16[16,64,128]{2,1,0:T(8,128)(2,1)S(1)} all-to-all(bf16[16,64,128]{2,1,0:T(8,128)(2,1)S(1)} %broadcast_in_dim.100), channel_id=1, replica_groups=mesh['section'=8,'y'=8,'core'=2,'dp'=4] {'y','core'}, dimensions={0} | all-to-all | bytes 524288 | tf_op jit(solution)/shard_map/while/body/eval_jaxpr/cond/branch_1_fun/all_to_all | solution.py:182
  348.6 1.3 collective-permute-start
  349.9 5.0 %collective-permute-done = bf16[64,256]{1,0:T(8,128)(2,1)S(1)} collective-permute-done((bf16[64,256]{1,0:T(8,128)(2,1)S(1)}, bf16[64,256]{1,0:T(8,128)(2,1)S(1)}, u32[]{:S(2)}, u32[]{:S(2)}) %collective-permute-start) | collective-permute-done | bytes 32800 | tf_op jit(solution)/shard_map/while/body/eval_jaxpr/ppermute | solution.py:211
  354.9 37.0 %conditional.7 = ((bf16[64,256]{1,0:T(8,128)(2,1)S(1)}, bf16[2,64,256]{2,1,0:T(8,128)(2,1)S(1)})) conditional(s32[]{:T(128)} %convert_element_type.112, (bf16[64,256]{1,0:T(8,128)(2,1)S(1)}, bf16[2,64,256]{2,1,0:T(8,128)(2,1)S(1)}) %tuple.87, (s32[]{:T(128)}, s32[]{:T(128)}, bf16[2,64,256]{2,1,0:T(8,128)(2,1)}, bf16[64,256]{1,0:T(8,128)(2,1)S(1)}, ...), branch_computations={%region_19.19_spmd, %region_20.20_spmd} | conditional | flops 24579 | bytes 5673230 | solution.py:220
  354.9 0.8 bitcast_select_fusion.current
  355.6 16.1 %all_gather.4.rows_ref = bf16[64,4096]{1,0:T(8,128)(2,1)S(1)} all-gather(bf16[64,256]{1,0:T(8,128)(2,1)S(1)} %bitcast_select_fusion.current), channel_id=1, replica_groups=mesh['section'=8,'y'=8,'core'=2,'dp'=4] {'y','core'}, dimensions={1}, use_global_device_ids=true | all-gather | bytes 557056 | tf_op jit(solution)/shard_map/while/body/eval_jaxpr/cond/branch_1_fun/all_gather | solution.py:178
  371.7 2.6 branch_1_fun.2
  374.4 17.2 %all_to_all.4.mixed = bf16[16,64,128]{2,1,0:T(8,128)(2,1)S(1)} all-to-all(bf16[16,64,128]{2,1,0:T(8,128)(2,1)S(1)} %broadcast_in_dim.100), channel_id=1, replica_groups=mesh['section'=8,'y'=8,'core'=2,'dp'=4] {'y','core'}, dimensions={0} | all-to-all | bytes 524288 | tf_op jit(solution)/shard_map/while/body/eval_jaxpr/cond/branch_1_fun/all_to_all | solution.py:182
  391.9 0.6 copy-done.4
  392.5 1.4 fusion.100
  393.9 1.4 slice_bitcast_fusion
  (96 shorter events, 3.9 us)
Async XLA Ops:
  0.6 67.0 %copy-start = (bf16[512,256]{1,0:T(8,128)(2,1)S(1)}, bf16[512,256]{1,0:T(8,128)(2,1)}, u32[]{:S(2)}) copy-start(bf16[512,256]{1,0:T(8,128)(2,1)} %param.36) | copy-start | bytes 786436
  0.7 0.7 copy-start.13
  0.7 0.7 copy-start.14
  1.4 0.7 copy-start.18
  20.9 0.7 copy-start.7
  20.9 0.7 copy-start.8
  20.9 0.7 copy-start.9
  20.9 0.7 copy-start.11
  20.9 0.7 copy-start.12
  21.7 46.0 %copy-start.15 = (f32[512]{0:T(512)S(1)}, f32[512]{0:T(512)}, u32[]{:S(2)}) copy-start(f32[512]{0:T(512)} %param.35) | copy-start | bytes 6148
  21.7 46.0 %copy-start.16 = (f32[512]{0:T(512)S(1)}, f32[512]{0:T(512)}, u32[]{:S(2)}) copy-start(f32[512]{0:T(512)} %param.34) | copy-start | bytes 6148
  21.7 46.0 %copy-start.17 = (f32[256]{0:T(256)S(1)}, f32[256]{0:T(256)}, u32[]{:S(2)}) copy-start(f32[256]{0:T(256)} %param.37) | copy-start | bytes 3076
  21.7 46.9 %copy-start.2 = (bf16[1,4096,128]{2,1,0:T(8,128)(2,1)S(1)}, bf16[1,4096,128]{2,1,0:T(8,128)(2,1)}, u32[]{:S(2)}) copy-start(bf16[1,4096,128]{2,1,0:T(8,128)(2,1)} %param.41) | copy-start | bytes 3145732
  65.9 2.7 copy-start.1
  68.6 0.7 copy-start.5
  68.6 0.7 copy-start.6
  68.6 0.7 copy-start.10
  69.3 4.6 %collective-permute-start = (bf16[64,256]{1,0:T(8,128)(2,1)S(1)}, bf16[64,256]{1,0:T(8,128)(2,1)S(1)}, u32[]{:S(2)}, u32[]{:S(2)}) collective-permute-start(bf16[64,256]{1,0:T(8,128)(2,1)S(1)} %get-tuple-element.556), channel_id=1, source_target_pairs={{0,64},{64,128},{128,192},{192,256},{256,320},{320,384},{384,448},... | collective-permute-start | bytes 98312 | tf_op jit(solution)/shard_map/while/body/eval_jaxpr/ppermute | solution.py:211
  73.9 4.6 %collective-permute-start = (bf16[64,256]{1,0:T(8,128)(2,1)S(1)}, bf16[64,256]{1,0:T(8,128)(2,1)S(1)}, u32[]{:S(2)}, u32[]{:S(2)}) collective-permute-start(bf16[64,256]{1,0:T(8,128)(2,1)S(1)} %get-tuple-element.556), channel_id=1, source_target_pairs={{0,64},{64,128},{128,192},{192,256},{256,320},{320,384},{384,448},... | collective-permute-start | bytes 98312 | tf_op jit(solution)/shard_map/while/body/eval_jaxpr/ppermute | solution.py:211
  78.6 4.6 %collective-permute-start = (bf16[64,256]{1,0:T(8,128)(2,1)S(1)}, bf16[64,256]{1,0:T(8,128)(2,1)S(1)}, u32[]{:S(2)}, u32[]{:S(2)}) collective-permute-start(bf16[64,256]{1,0:T(8,128)(2,1)S(1)} %get-tuple-element.556), channel_id=1, source_target_pairs={{0,64},{64,128},{128,192},{192,256},{256,320},{320,384},{384,448},... | collective-permute-start | bytes 98312 | tf_op jit(solution)/shard_map/while/body/eval_jaxpr/ppermute | solution.py:211
  83.2 4.6 %collective-permute-start = (bf16[64,256]{1,0:T(8,128)(2,1)S(1)}, bf16[64,256]{1,0:T(8,128)(2,1)S(1)}, u32[]{:S(2)}, u32[]{:S(2)}) collective-permute-start(bf16[64,256]{1,0:T(8,128)(2,1)S(1)} %get-tuple-element.556), channel_id=1, source_target_pairs={{0,64},{64,128},{128,192},{192,256},{256,320},{320,384},{384,448},... | collective-permute-start | bytes 98312 | tf_op jit(solution)/shard_map/while/body/eval_jaxpr/ppermute | solution.py:211
  87.9 4.6 %collective-permute-start = (bf16[64,256]{1,0:T(8,128)(2,1)S(1)}, bf16[64,256]{1,0:T(8,128)(2,1)S(1)}, u32[]{:S(2)}, u32[]{:S(2)}) collective-permute-start(bf16[64,256]{1,0:T(8,128)(2,1)S(1)} %get-tuple-element.556), channel_id=1, source_target_pairs={{0,64},{64,128},{128,192},{192,256},{256,320},{320,384},{384,448},... | collective-permute-start | bytes 98312 | tf_op jit(solution)/shard_map/while/body/eval_jaxpr/ppermute | solution.py:211
  92.5 4.8 %collective-permute-start = (bf16[64,256]{1,0:T(8,128)(2,1)S(1)}, bf16[64,256]{1,0:T(8,128)(2,1)S(1)}, u32[]{:S(2)}, u32[]{:S(2)}) collective-permute-start(bf16[64,256]{1,0:T(8,128)(2,1)S(1)} %get-tuple-element.556), channel_id=1, source_target_pairs={{0,64},{64,128},{128,192},{192,256},{256,320},{320,384},{384,448},... | collective-permute-start | bytes 98312 | tf_op jit(solution)/shard_map/while/body/eval_jaxpr/ppermute | solution.py:211
  97.3 5.9 %collective-permute-start = (bf16[64,256]{1,0:T(8,128)(2,1)S(1)}, bf16[64,256]{1,0:T(8,128)(2,1)S(1)}, u32[]{:S(2)}, u32[]{:S(2)}) collective-permute-start(bf16[64,256]{1,0:T(8,128)(2,1)S(1)} %get-tuple-element.556), channel_id=1, source_target_pairs={{0,64},{64,128},{128,192},{192,256},{256,320},{320,384},{384,448},... | collective-permute-start | bytes 98312 | tf_op jit(solution)/shard_map/while/body/eval_jaxpr/ppermute | solution.py:211
  103.2 208.4 %collective-permute-start = (bf16[64,256]{1,0:T(8,128)(2,1)S(1)}, bf16[64,256]{1,0:T(8,128)(2,1)S(1)}, u32[]{:S(2)}, u32[]{:S(2)}) collective-permute-start(bf16[64,256]{1,0:T(8,128)(2,1)S(1)} %get-tuple-element.556), channel_id=1, source_target_pairs={{0,64},{64,128},{128,192},{192,256},{256,320},{320,384},{384,448},... | collective-permute-start | bytes 98312 | tf_op jit(solution)/shard_map/while/body/eval_jaxpr/ppermute | solution.py:211
  328.4 19.9 %copy-start.3 = (bf16[8,256,256]{2,1,0:T(8,128)(2,1)S(1)}, bf16[8,256,256]{2,1,0:T(8,128)(2,1)}, u32[]{:S(2)}) copy-start(bf16[8,256,256]{2,1,0:T(8,128)(2,1)} %get-tuple-element.299.weights) | copy-start | bytes 3145732 | tf_op jit(solution)/shard_map/while/body/eval_jaxpr/cond
  348.6 6.3 %collective-permute-start = (bf16[64,256]{1,0:T(8,128)(2,1)S(1)}, bf16[64,256]{1,0:T(8,128)(2,1)S(1)}, u32[]{:S(2)}, u32[]{:S(2)}) collective-permute-start(bf16[64,256]{1,0:T(8,128)(2,1)S(1)} %get-tuple-element.556), channel_id=1, source_target_pairs={{0,64},{64,128},{128,192},{192,256},{256,320},{320,384},{384,448},... | collective-permute-start | bytes 98312 | tf_op jit(solution)/shard_map/while/body/eval_jaxpr/ppermute | solution.py:211
  371.7 19.9 %copy-start.3 = (bf16[8,256,256]{2,1,0:T(8,128)(2,1)S(1)}, bf16[8,256,256]{2,1,0:T(8,128)(2,1)}, u32[]{:S(2)}) copy-start(bf16[8,256,256]{2,1,0:T(8,128)(2,1)} %get-tuple-element.299.weights) | copy-start | bytes 3145732 | tf_op jit(solution)/shard_map/while/body/eval_jaxpr/cond
  391.9 0.6 copy-start.4

commit v8 on v5

--- a/solution.py
+++ b/solution.py
@@ -52,23 +52,43 @@
 def mixing_kernel(place, rows_ref, gain, shift, query, key, value, masking, out):
     rows, model = rows_ref.shape
     width = 2 * HEAD_DIM
-    spans = [slice(at, at + width) for at in range(0, model, width)]
-    total = jnp.zeros((rows, 1), jnp.float32)
-    for span in spans:
-        total += jnp.sum(rows_ref[:, span].astype(jnp.float32), axis=-1, keepdims=True)
-    average = total / model
-    spread = jnp.zeros_like(average)
-    for span in spans:
-        centered = rows_ref[:, span].astype(jnp.float32) - average
-        spread += jnp.sum(centered * centered, axis=-1, keepdims=True)
-    scale = lax.rsqrt(spread / model + 1e-05)
-    both = jnp.zeros((rows, 2 * HEAD_DIM), jnp.float32)
-    values = jnp.zeros((rows, HEAD_DIM), jnp.float32)
-    for span in spans:
+    step = min(model, 4 * width)
+    steps = model // step
+
+    def parts_of(i):
+        at = pl.multiple_of(i * step, step)
+        return [
+            rows_ref[:, pl.ds(pl.multiple_of(at + inner, width), width)].astype(jnp.float32)
+            for inner in range(0, step, width)
+        ]
+
+    def add_up(i, total):
+        for part in parts_of(i):
+            total += part
+        return total
+
+    zeros = jnp.zeros((rows, width), jnp.float32)
+    total = lax.fori_loop(0, steps, add_up, zeros)
+    average = jnp.sum(total, axis=-1, keepdims=True) / model
+
+    def add_squares(i, total):
+        for part in parts_of(i):
+            total += (part - average) * (part - average)
+        return total
+
+    total = lax.fori_loop(0, steps, add_squares, zeros)
+    scale = lax.rsqrt(jnp.sum(total, axis=-1, keepdims=True) / model + 1e-05)
+
+    def project(i, sums):
+        span = pl.ds(pl.multiple_of(i * step, step), step)
         centered = rows_ref[:, span].astype(jnp.float32) - average
         normed = (centered * scale * gain[:, span] + shift[:, span]).astype(jnp.bfloat16)
-        both += product(normed, jnp.concatenate([query[span], key[span]], axis=1))
-        values += product(normed, value[span])
+        pair = jnp.concatenate([query[span, :], key[span, :]], axis=1)
+        return (sums[0] + product(normed, pair), sums[1] + product(normed, value[span, :]))
+
+    both, values = lax.fori_loop(
+        0, steps, project, (zeros, jnp.zeros((rows, HEAD_DIM), jnp.float32))
+    )
     queries = (both[:, :HEAD_DIM] * HEAD_DIM ** (-0.5)).astype(jnp.bfloat16)
     key_rows = both[:, HEAD_DIM:].astype(jnp.bfloat16)
     scores = lax.dot_general(
@@ -81,13 +101,19 @@
     out[...] = jnp.broadcast_to(mixture[None], out.shape)
 
 
-def leaving_kernel(place, mixed, current, weights, bias, _, out, outputs):
-    total = current[...].astype(jnp.float32) + bias[...]
-    for i in range(0, mixed.shape[0], 2):
-        pair = jnp.concatenate([mixed[i], mixed[i + 1]], axis=1)
-        total += product(pair, weights[i // 2])
+def leaving_kernel(place, mixed, current, weights, bias, held, out, outputs):
+    def add_heads(i, total):
+        for inner in range(2):
+            at = 2 * i + inner
+            pair = jnp.concatenate([mixed[2 * at], mixed[2 * at + 1]], axis=1)
+            total += product(pair, weights[at])
+        return total
+
+    start = current[...].astype(jnp.float32) + bias[...]
+    total = lax.fori_loop(0, weights.shape[0] // 2, add_heads, start)
     result = total.astype(jnp.bfloat16)
     out[...] = result
+    outputs[...] = held[...]
     outputs[place[0]] = result
 
 

time: 389 us -> 398 us (1.023)
  waiting for transfers between devices: 234 us -> 241 us
    ppermute x9, waiting for transfers between devices: 234 us -> 241 us  [advance(): lax.ppermute(previous, 'section', [(s, s + 1) for s in range(sections - 1)])]
where the time goes in v8:
time: 398 us; the launch traced here: 397 us
  waiting for transfers between devices  241 us (61%)
  blocking collectives  122 us (31%)
  starting transfers between devices  11.5 us (3%)
  Pallas kernels  8.49 us (2%)
  local copies, waits for them, and re-layouts  5.72 us (1%)
  other arithmetic  4.37 us (1%)
    ppermute x9, waiting for transfers between devices, advance(): lax.ppermute(previous, 'section', [(s, s + 1) for s in range(sections - 1)])  241 us
    psum x3, blocking collectives, gradients_of(): return lax.psum(lax.psum(lax.psum(packed, 'core'), 'dp'), 'y')  37.6 us
    all_to_all x2, blocking collectives, attend(): mixed = lax.all_to_all(copies, ('y', 'core'), 0, 0, tiled=True)  34.3 us
    all_gather x2, blocking collectives, attend(): whole = lax.all_gather(current, ('y', 'core'), axis=1, tiled=True)  32.2 us
    all_gather x1, blocking collectives, on_device(): lax.all_gather(wave[0].astype(jnp.float32), ('y', 'core'), axis=0, tiled=...  17.9 us
    ppermute x9, starting transfers between devices, advance(): lax.ppermute(previous, 'section', [(s, s + 1) for s in range(sections - 1)])  11.5 us
  transfers between devices with their start and end apart: 9, of which 9 were waited for; matrix products, arithmetic and copies ran while one was open for 0% of the time, Pallas kernels for 0%

profile of v8, /device:TPU:449, one launch (start us, length us, event | category | flops | bytes accessed | tf_op | source)
XLA Modules:
  0.0 397.2 jit_solution(1925346627269804608)
XLA Ops:
  0.7 0.7 copy-done.12
  1.5 0.6 copy-done.17
  2.8 17.9 %all-gather = f32[16,1,40]{2,1,0:T(1,128)S(1)} all-gather(f32[1,1,40]{2,1,0:T(1,128)S(1)} %convert_element_type.85), channel_id=2, replica_groups=mesh['section'=8,'y'=8,'core'=2,'dp'=4] {'y','core'}, dimensions={0}, use_global_device_ids=true | all-gather | bytes 2720 | tf_op jit(solution)/shard_map/all_gather | solution.py:151
  21.1 0.6 copy-done.6
  21.7 43.4 %conditional.3 = (f32[16,512]{1,0:T(8,128)S(1)}) conditional(s32[]{:T(128)} %convert_element_type.82, () %tuple.42, (s32[]{:T(128)}, s32[]{:T(128)}, s32[1,16]{1,0:T(1,128)S(1)}, bf16[1,1,40]{2,1,0:T(2,128)(2,1)S(1)}, bf16[512,10]{0,1:T(8,128)(2,1)S(1)}, /*index=5*/f32[512]{0:T(512)S(1)}, f32[512]{0:T(512)S(1)}, f32[512]{0:T(512)S(1)}, ...), branch_computations={%region_6.7_spmd, %region_7.18_spmd} | conditional | flops 1064623 | bytes 458498 | solution.py:232
  21.7 0.5 broadcast.920
  22.3 0.7 reduce.36
  22.9 0.6 fusion.97
  25.6 0.6 fusion.21
  26.2 0.3 fusion.96
  27.5 3.4 psum.36
  31.0 13.3 %psum.37 = f32[16,512]{1,0:T(8,128)S(1)} all-reduce(f32[16,512]{1,0:T(8,128)S(1)} %psum.36), channel_id=1, replica_groups=mesh['section'=8,'y'=8,'core'=2,'dp'=4] {'dp'}, use_global_device_ids=true, to_apply=%region_16.16 | all-reduce | flops 8192 | bytes 65536 | tf_op jit(solution)/shard_map/cond/branch_1_fun/psum | solution.py:229
  44.3 20.8 %psum.38 = f32[16,512]{1,0:T(8,128)S(1)} all-reduce(f32[16,512]{1,0:T(8,128)S(1)} %psum.37), channel_id=1, replica_groups=mesh['section'=8,'y'=8,'core'=2,'dp'=4] {'y'}, use_global_device_ids=true, to_apply=%region_17.17 | all-reduce | flops 8192 | bytes 65536 | tf_op jit(solution)/shard_map/cond/branch_1_fun/psum | solution.py:229
  65.1 0.3 fusion.101
  65.6 0.8 convert_reduce_fusion
  67.2 0.6 copy-done.4
  67.9 327.5 %while.16 = (s32[]{:T(128)}, bf16[64,256]{1,0:T(8,128)(2,1)S(1)}, bf16[2,64,256]{2,1,0:T(8,128)(2,1)S(1)}, s32[]{:T(128)}, bf16[2,64,256]{2,1,0:T(8,128)(2,1)S(1...) while((s32[]{:T(128)}, bf16[64,256]{1,0:T(8,128)(2,1)S(1)}, ...), condition=%wide.region_21.22_spmd.clone, body=%wide.region_18.21_spmd.clone.sunk | while | flops 32778 | bytes 1348145 | solution.py:256
  67.9 1.3 collective-permute-start
  69.2 3.3 collective-permute-done
  72.5 1.3 collective-permute-start
  73.8 3.3 collective-permute-done
  77.2 1.3 collective-permute-start
  78.5 3.3 collective-permute-done
  81.8 1.3 collective-permute-start
  83.1 3.3 collective-permute-done
  86.5 1.3 collective-permute-start
  87.8 3.3 collective-permute-done
  91.1 1.3 collective-permute-start
  92.4 3.5 collective-permute-done
  95.9 1.3 collective-permute-start
  97.2 4.6 %collective-permute-done = bf16[64,256]{1,0:T(8,128)(2,1)S(1)} collective-permute-done((bf16[64,256]{1,0:T(8,128)(2,1)S(1)}, bf16[64,256]{1,0:T(8,128)(2,1)S(1)}, u32[]{:S(2)}, u32[]{:S(2)}) %collective-permute-start) | collective-permute-done | bytes 32800 | tf_op jit(solution)/shard_map/while/body/eval_jaxpr/ppermute | solution.py:239
  101.7 1.3 collective-permute-start
  103.0 211.0 %collective-permute-done = bf16[64,256]{1,0:T(8,128)(2,1)S(1)} collective-permute-done((bf16[64,256]{1,0:T(8,128)(2,1)S(1)}, bf16[64,256]{1,0:T(8,128)(2,1)S(1)}, u32[]{:S(2)}, u32[]{:S(2)}) %collective-permute-start) | collective-permute-done | bytes 32800 | tf_op jit(solution)/shard_map/while/body/eval_jaxpr/ppermute | solution.py:239
  314.0 37.5 %conditional.7 = ((bf16[64,256]{1,0:T(8,128)(2,1)S(1)}, bf16[2,64,256]{2,1,0:T(8,128)(2,1)S(1)})) conditional(s32[]{:T(128)} %convert_element_type.112, (bf16[64,256]{1,0:T(8,128)(2,1)S(1)}, bf16[2,64,256]{2,1,0:T(8,128)(2,1)S(1)}) %tuple.87, (s32[]{:T(128)}, s32[]{:T(128)}, bf16[2,64,256]{2,1,0:T(8,128)(2,1)S(1)}, bf16[64,256]{1,0:T(8,128)(2,1)S(1)}, ...), branch_computations={%region_19.19_spmd, %region_20.20_spmd} | conditional | flops 32771 | bytes 1216686 | solution.py:248
  314.0 16.1 %all_gather.4.rows_ref = bf16[64,4096]{1,0:T(8,128)(2,1)S(1)} all-gather(bf16[64,256]{1,0:T(8,128)(2,1)S(1)} %bitcast_select_fusion.current), channel_id=1, replica_groups=mesh['section'=8,'y'=8,'core'=2,'dp'=4] {'y','core'}, dimensions={1}, use_global_device_ids=true | all-gather | bytes 557056 | tf_op jit(solution)/shard_map/while/body/eval_jaxpr/cond/branch_1_fun/all_gather | solution.py:199
  330.1 3.5 branch_1_fun.2
  333.7 17.2 %all_to_all.4.mixed = bf16[16,64,128]{2,1,0:T(8,128)(2,1)S(1)} all-to-all(bf16[16,64,128]{2,1,0:T(8,128)(2,1)S(1)} %branch_1_fun.2), channel_id=1, replica_groups=mesh['section'=8,'y'=8,'core'=2,'dp'=4] {'y','core'}, dimensions={0} | all-to-all | bytes 524288 | tf_op jit(solution)/shard_map/while/body/eval_jaxpr/cond/branch_1_fun/all_to_all | solution.py:210
  350.8 0.7 branch_1_fun.3
  351.6 1.3 collective-permute-start
  352.9 5.0 %collective-permute-done = bf16[64,256]{1,0:T(8,128)(2,1)S(1)} collective-permute-done((bf16[64,256]{1,0:T(8,128)(2,1)S(1)}, bf16[64,256]{1,0:T(8,128)(2,1)S(1)}, u32[]{:S(2)}, u32[]{:S(2)}) %collective-permute-start) | collective-permute-done | bytes 32800 | tf_op jit(solution)/shard_map/while/body/eval_jaxpr/ppermute | solution.py:239
  357.8 37.5 %conditional.7 = ((bf16[64,256]{1,0:T(8,128)(2,1)S(1)}, bf16[2,64,256]{2,1,0:T(8,128)(2,1)S(1)})) conditional(s32[]{:T(128)} %convert_element_type.112, (bf16[64,256]{1,0:T(8,128)(2,1)S(1)}, bf16[2,64,256]{2,1,0:T(8,128)(2,1)S(1)}) %tuple.87, (s32[]{:T(128)}, s32[]{:T(128)}, bf16[2,64,256]{2,1,0:T(8,128)(2,1)S(1)}, bf16[64,256]{1,0:T(8,128)(2,1)S(1)}, ...), branch_computations={%region_19.19_spmd, %region_20.20_spmd} | conditional | flops 32771 | bytes 1216686 | solution.py:248
  357.9 16.1 %all_gather.4.rows_ref = bf16[64,4096]{1,0:T(8,128)(2,1)S(1)} all-gather(bf16[64,256]{1,0:T(8,128)(2,1)S(1)} %bitcast_select_fusion.current), channel_id=1, replica_groups=mesh['section'=8,'y'=8,'core'=2,'dp'=4] {'y','core'}, dimensions={1}, use_global_device_ids=true | all-gather | bytes 557056 | tf_op jit(solution)/shard_map/while/body/eval_jaxpr/cond/branch_1_fun/all_gather | solution.py:199
  374.0 3.5 branch_1_fun.2
  377.5 17.2 %all_to_all.4.mixed = bf16[16,64,128]{2,1,0:T(8,128)(2,1)S(1)} all-to-all(bf16[16,64,128]{2,1,0:T(8,128)(2,1)S(1)} %branch_1_fun.2), channel_id=1, replica_groups=mesh['section'=8,'y'=8,'core'=2,'dp'=4] {'y','core'}, dimensions={0} | all-to-all | bytes 524288 | tf_op jit(solution)/shard_map/while/body/eval_jaxpr/cond/branch_1_fun/all_to_all | solution.py:210
  394.7 0.7 branch_1_fun.3
  395.4 0.6 copy-done.3
  396.0 0.6 fusion.100
  396.6 0.6 slice_bitcast_fusion
  (88 shorter events, 3.2 us)
Async XLA Ops:
  0.6 66.2 %copy-start = (bf16[512,256]{1,0:T(8,128)(2,1)S(1)}, bf16[512,256]{1,0:T(8,128)(2,1)}, u32[]{:S(2)}) copy-start(bf16[512,256]{1,0:T(8,128)(2,1)} %param.36) | copy-start | bytes 786436
  0.7 0.7 copy-start.12
  0.7 0.7 copy-start.13
  1.4 0.7 copy-start.17
  20.9 0.7 copy-start.6
  20.9 0.7 copy-start.7
  20.9 0.7 copy-start.8
  20.9 0.7 copy-start.10
  20.9 0.7 copy-start.11
  21.7 45.2 %copy-start.14 = (f32[512]{0:T(512)S(1)}, f32[512]{0:T(512)}, u32[]{:S(2)}) copy-start(f32[512]{0:T(512)} %param.35) | copy-start | bytes 6148
  21.7 45.2 %copy-start.15 = (f32[512]{0:T(512)S(1)}, f32[512]{0:T(512)}, u32[]{:S(2)}) copy-start(f32[512]{0:T(512)} %param.34) | copy-start | bytes 6148
  21.7 45.2 %copy-start.16 = (f32[256]{0:T(256)S(1)}, f32[256]{0:T(256)}, u32[]{:S(2)}) copy-start(f32[256]{0:T(256)} %param.37) | copy-start | bytes 3076
  21.7 45.5 %copy-start.2 = (bf16[1,4096,128]{2,1,0:T(8,128)(2,1)S(1)}, bf16[1,4096,128]{2,1,0:T(8,128)(2,1)}, u32[]{:S(2)}) copy-start(bf16[1,4096,128]{2,1,0:T(8,128)(2,1)} %param.40) | copy-start | bytes 3145732
  65.1 2.1 copy-start.1
  67.1 0.7 copy-start.4
  67.1 0.7 copy-start.5
  67.2 0.7 copy-start.9
  67.9 4.6 %collective-permute-start = (bf16[64,256]{1,0:T(8,128)(2,1)S(1)}, bf16[64,256]{1,0:T(8,128)(2,1)S(1)}, u32[]{:S(2)}, u32[]{:S(2)}) collective-permute-start(bf16[64,256]{1,0:T(8,128)(2,1)S(1)} %get-tuple-element.556), channel_id=1, source_target_pairs={{0,64},{64,128},{128,192},{192,256},{256,320},{320,384},{384,448},... | collective-permute-start | bytes 98312 | tf_op jit(solution)/shard_map/while/body/eval_jaxpr/ppermute | solution.py:239
  72.5 4.6 %collective-permute-start = (bf16[64,256]{1,0:T(8,128)(2,1)S(1)}, bf16[64,256]{1,0:T(8,128)(2,1)S(1)}, u32[]{:S(2)}, u32[]{:S(2)}) collective-permute-start(bf16[64,256]{1,0:T(8,128)(2,1)S(1)} %get-tuple-element.556), channel_id=1, source_target_pairs={{0,64},{64,128},{128,192},{192,256},{256,320},{320,384},{384,448},... | collective-permute-start | bytes 98312 | tf_op jit(solution)/shard_map/while/body/eval_jaxpr/ppermute | solution.py:239
  77.2 4.6 %collective-permute-start = (bf16[64,256]{1,0:T(8,128)(2,1)S(1)}, bf16[64,256]{1,0:T(8,128)(2,1)S(1)}, u32[]{:S(2)}, u32[]{:S(2)}) collective-permute-start(bf16[64,256]{1,0:T(8,128)(2,1)S(1)} %get-tuple-element.556), channel_id=1, source_target_pairs={{0,64},{64,128},{128,192},{192,256},{256,320},{320,384},{384,448},... | collective-permute-start | bytes 98312 | tf_op jit(solution)/shard_map/while/body/eval_jaxpr/ppermute | solution.py:239
  81.8 4.6 %collective-permute-start = (bf16[64,256]{1,0:T(8,128)(2,1)S(1)}, bf16[64,256]{1,0:T(8,128)(2,1)S(1)}, u32[]{:S(2)}, u32[]{:S(2)}) collective-permute-start(bf16[64,256]{1,0:T(8,128)(2,1)S(1)} %get-tuple-element.556), channel_id=1, source_target_pairs={{0,64},{64,128},{128,192},{192,256},{256,320},{320,384},{384,448},... | collective-permute-start | bytes 98312 | tf_op jit(solution)/shard_map/while/body/eval_jaxpr/ppermute | solution.py:239
  86.5 4.6 %collective-permute-start = (bf16[64,256]{1,0:T(8,128)(2,1)S(1)}, bf16[64,256]{1,0:T(8,128)(2,1)S(1)}, u32[]{:S(2)}, u32[]{:S(2)}) collective-permute-start(bf16[64,256]{1,0:T(8,128)(2,1)S(1)} %get-tuple-element.556), channel_id=1, source_target_pairs={{0,64},{64,128},{128,192},{192,256},{256,320},{320,384},{384,448},... | collective-permute-start | bytes 98312 | tf_op jit(solution)/shard_map/while/body/eval_jaxpr/ppermute | solution.py:239
  91.1 4.8 %collective-permute-start = (bf16[64,256]{1,0:T(8,128)(2,1)S(1)}, bf16[64,256]{1,0:T(8,128)(2,1)S(1)}, u32[]{:S(2)}, u32[]{:S(2)}) collective-permute-start(bf16[64,256]{1,0:T(8,128)(2,1)S(1)} %get-tuple-element.556), channel_id=1, source_target_pairs={{0,64},{64,128},{128,192},{192,256},{256,320},{320,384},{384,448},... | collective-permute-start | bytes 98312 | tf_op jit(solution)/shard_map/while/body/eval_jaxpr/ppermute | solution.py:239
  95.9 5.9 %collective-permute-start = (bf16[64,256]{1,0:T(8,128)(2,1)S(1)}, bf16[64,256]{1,0:T(8,128)(2,1)S(1)}, u32[]{:S(2)}, u32[]{:S(2)}) collective-permute-start(bf16[64,256]{1,0:T(8,128)(2,1)S(1)} %get-tuple-element.556), channel_id=1, source_target_pairs={{0,64},{64,128},{128,192},{192,256},{256,320},{320,384},{384,448},... | collective-permute-start | bytes 98312 | tf_op jit(solution)/shard_map/while/body/eval_jaxpr/ppermute | solution.py:239
  101.7 212.3 %collective-permute-start = (bf16[64,256]{1,0:T(8,128)(2,1)S(1)}, bf16[64,256]{1,0:T(8,128)(2,1)S(1)}, u32[]{:S(2)}, u32[]{:S(2)}) collective-permute-start(bf16[64,256]{1,0:T(8,128)(2,1)S(1)} %get-tuple-element.556), channel_id=1, source_target_pairs={{0,64},{64,128},{128,192},{192,256},{256,320},{320,384},{384,448},... | collective-permute-start | bytes 98312 | tf_op jit(solution)/shard_map/while/body/eval_jaxpr/ppermute | solution.py:239
  351.6 6.3 %collective-permute-start = (bf16[64,256]{1,0:T(8,128)(2,1)S(1)}, bf16[64,256]{1,0:T(8,128)(2,1)S(1)}, u32[]{:S(2)}, u32[]{:S(2)}) collective-permute-start(bf16[64,256]{1,0:T(8,128)(2,1)S(1)} %get-tuple-element.556), channel_id=1, source_target_pairs={{0,64},{64,128},{128,192},{192,256},{256,320},{320,384},{384,448},... | collective-permute-start | bytes 98312 | tf_op jit(solution)/shard_map/while/body/eval_jaxpr/ppermute | solution.py:239
  395.4 0.6 copy-start.3

commit v9 on v7

--- a/solution.py
+++ b/solution.py
@@ -49,23 +49,22 @@
     return jnp.dot(left, right, preferred_element_type=jnp.float32)
 
 
-def mixing_kernel(rows_ref, gain, shift, query, key, value, masking, out):
-    rows, model = rows_ref.shape
-    parts, width = query.shape[0], query.shape[1]
-    spans = [slice(i * width, (i + 1) * width) for i in range(parts)]
+def mixing_kernel(place, blocks, gain, shift, query, key, value, masking, out):
+    parts, rows, width = blocks.shape
     total = jnp.zeros((rows, width), jnp.float32)
-    for span in spans:
-        total += rows_ref[:, span].astype(jnp.float32)
-    average = jnp.sum(total, axis=-1, keepdims=True) / model
+    for i in range(parts):
+        total += blocks[i].astype(jnp.float32)
+    average = jnp.sum(total, axis=-1, keepdims=True) / (parts * width)
     total = jnp.zeros((rows, width), jnp.float32)
-    for span in spans:
-        centered = rows_ref[:, span].astype(jnp.float32) - average
+    for i in range(parts):
+        centered = blocks[i].astype(jnp.float32) - average
         total += centered * centered
-    scale = lax.rsqrt(jnp.sum(total, axis=-1, keepdims=True) / model + 1e-05)
+    spread = jnp.sum(total, axis=-1, keepdims=True) / (parts * width)
+    scale = lax.rsqrt(spread + 1e-05)
     both = jnp.zeros((rows, 2 * HEAD_DIM), jnp.float32)
     values = jnp.zeros((rows, HEAD_DIM), jnp.float32)
-    for i, span in enumerate(spans):
-        centered = rows_ref[:, span].astype(jnp.float32) - average
+    for i in range(parts):
+        centered = blocks[i].astype(jnp.float32) - average
         normed = (centered * scale * gain[i] + shift[i]).astype(jnp.bfloat16)
         both += product(normed, jnp.concatenate([query[i], key[i]], axis=1))
         values += product(normed, value[i])
@@ -74,19 +73,21 @@
     scores = lax.dot_general(
         queries, key_rows, (((1,), (1,)), ((), ())), preferred_element_type=jnp.float32
     )
-    scores = jnp.where(masking[...] > 0, scores, -jnp.inf)
+    scores = jnp.where(masking[place[0]] > 0, scores, -jnp.inf)
     raised = jnp.exp(scores - jnp.max(scores, axis=-1, keepdims=True))
     attention = (raised / jnp.sum(raised, axis=-1, keepdims=True)).astype(jnp.bfloat16)
-    out[...] = product(attention, values.astype(jnp.bfloat16)).astype(jnp.bfloat16)
-
-
-def leaving_kernel(place, mixed, current, weights, bias, _, out, outputs):
+    mixture = product(attention, values.astype(jnp.bfloat16)).astype(jnp.bfloat16)
+    out[...] = jnp.broadcast_to(mixture[None], out.shape)
+
+
+def leaving_kernel(place, mixed, current, weights, bias, held, out, outputs):
     total = current[...].astype(jnp.float32) + bias[...]
     for i in range(0, mixed.shape[0], 2):
         pair = jnp.concatenate([mixed[i], mixed[i + 1]], axis=1)
         total += product(pair, weights[i // 2])
     result = total.astype(jnp.bfloat16)
     out[...] = result
+    outputs[...] = held[...]
     outputs[place[0]] = result
 
 
@@ -156,8 +157,8 @@
     smem = pl.BlockSpec(memory_space=pltpu.SMEM)
     mixing = pl.pallas_call(
         mixing_kernel,
-        out_shape=jax.ShapeDtypeStruct((rows, HEAD_DIM), jnp.bfloat16),
-        in_specs=[vmem] * 7,
+        out_shape=jax.ShapeDtypeStruct((group, rows, HEAD_DIM), jnp.bfloat16),
+        in_specs=[smem] + [vmem] * 7,
         out_specs=vmem,
         compiler_params=pltpu.CompilerParams(vmem_limit_bytes=24 * 2**20),
     )
@@ -175,10 +176,8 @@
 
     def attend(current, slot, outputs):
         place = slot.reshape(1)
-        whole = lax.all_gather(current, ("y", "core"), axis=1, tiled=True)
-        masking = lax.dynamic_index_in_dim(maskings, slot, 0, keepdims=False)
-        mixture = mixing(whole, gain, shift, query, key, value, masking)
-        copies = jnp.broadcast_to(mixture[None], (group,) + mixture.shape)
+        whole = lax.all_gather(current, ("y", "core"), axis=0, tiled=False)
+        copies = mixing(place, whole, gain, shift, query, key, value, maskings)
         mixed = lax.all_to_all(copies, ("y", "core"), 0, 0, tiled=True)
         return leaving(place, mixed, current, out_part, out_bias, outputs)
 

time: 396 us -> 388 us (0.980)
  waiting for transfers between devices: 237 us -> 233 us
where the time goes in v9:
time: 388 us; the launch traced here: 387 us
  waiting for transfers between devices  233 us (60%)
  blocking collectives  122 us (31%)
  starting transfers between devices  11.5 us (3%)
  Pallas kernels  6.3 us (2%)
  local copies, waits for them, and re-layouts  5.72 us (1%)
  other arithmetic  4.37 us (1%)
    ppermute x9, waiting for transfers between devices, advance(): lax.ppermute(previous, 'section', [(s, s + 1) for s in range(sections - 1)])  233 us
    psum x3, blocking collectives, gradients_of(): return lax.psum(lax.psum(lax.psum(packed, 'core'), 'dp'), 'y')  37.6 us
    all_to_all x2, blocking collectives, attend(): mixed = lax.all_to_all(copies, ('y', 'core'), 0, 0, tiled=True)  34.3 us
    all_gather x2, blocking collectives, attend(): whole = lax.all_gather(current, ('y', 'core'), axis=0, tiled=False)  32.2 us
    all_gather x1, blocking collectives, on_device(): lax.all_gather(wave[0].astype(jnp.float32), ('y', 'core'), axis=0, tiled=...  17.9 us
    ppermute x9, starting transfers between devices, advance(): lax.ppermute(previous, 'section', [(s, s + 1) for s in range(sections - 1)])  11.5 us
  transfers between devices with their start and end apart: 9, of which 9 were waited for; matrix products, arithmetic and copies ran while one was open for 0% of the time, Pallas kernels for 0%

profile of v9, /device:TPU:449, one launch (start us, length us, event | category | flops | bytes accessed | tf_op | source)
XLA Modules:
  0.0 387.4 jit_solution(16331141485207505094)
XLA Ops:
  0.7 0.7 copy-done.12
  1.5 0.6 copy-done.17
  2.8 17.9 %all-gather.1 = f32[16,1,40]{2,1,0:T(1,128)S(1)} all-gather(f32[1,1,40]{2,1,0:T(1,128)S(1)} %convert_element_type.85), channel_id=3, replica_groups=mesh['section'=8,'y'=8,'core'=2,'dp'=4] {'y','core'}, dimensions={0}, use_global_device_ids=true | all-gather | bytes 2720 | tf_op jit(solution)/shard_map/all_gather | solution.py:125
  21.1 0.6 copy-done.6
  21.7 43.4 %conditional.3 = (f32[16,512]{1,0:T(8,128)S(1)}) conditional(s32[]{:T(128)} %convert_element_type.82, () %tuple.42, (s32[]{:T(128)}, s32[]{:T(128)}, s32[1,16]{1,0:T(1,128)S(1)}, bf16[1,1,40]{2,1,0:T(2,128)(2,1)S(1)}, bf16[512,10]{0,1:T(8,128)(2,1)S(1)}, /*index=5*/f32[512]{0:T(512)S(1)}, f32[512]{0:T(512)S(1)}, f32[512]{0:T(512)S(1)}, ...), branch_computations={%region_6.7_spmd, %region_7.18_spmd} | conditional | flops 1064623 | bytes 458498 | solution.py:203
  21.7 0.5 broadcast.920
  22.3 0.7 reduce.36
  22.9 0.6 fusion.97
  25.6 0.6 fusion.21
  26.2 0.3 fusion.96
  27.5 3.4 psum.36
  31.0 13.3 %psum.37 = f32[16,512]{1,0:T(8,128)S(1)} all-reduce(f32[16,512]{1,0:T(8,128)S(1)} %psum.36), channel_id=1, replica_groups=mesh['section'=8,'y'=8,'core'=2,'dp'=4] {'dp'}, use_global_device_ids=true, to_apply=%region_16.16 | all-reduce | flops 8192 | bytes 65536 | tf_op jit(solution)/shard_map/cond/branch_1_fun/psum | solution.py:200
  44.3 20.8 %psum.38 = f32[16,512]{1,0:T(8,128)S(1)} all-reduce(f32[16,512]{1,0:T(8,128)S(1)} %psum.37), channel_id=1, replica_groups=mesh['section'=8,'y'=8,'core'=2,'dp'=4] {'y'}, use_global_device_ids=true, to_apply=%region_17.17 | all-reduce | flops 8192 | bytes 65536 | tf_op jit(solution)/shard_map/cond/branch_1_fun/psum | solution.py:200
  65.1 0.3 fusion.101
  65.6 0.8 convert_reduce_fusion
  67.2 0.6 copy-done.4
  67.9 317.7 %while.16 = (s32[]{:T(128)}, bf16[64,256]{1,0:T(8,128)(2,1)S(1)}, bf16[2,64,256]{2,1,0:T(8,128)(2,1)S(1)}, s32[]{:T(128)}, bf16[2,64,256]{2,1,0:T(8,128)(2,1)S(1...) while((s32[]{:T(128)}, bf16[64,256]{1,0:T(8,128)(2,1)S(1)}, ...), condition=%wide.region_21.22_spmd.clone, body=%wide.region_18.21_spmd.clone.sunk | while | flops 32778 | bytes 1348145 | solution.py:227
  67.9 1.3 collective-permute-start
  69.2 3.3 collective-permute-done
  72.5 1.3 collective-permute-start
  73.8 3.3 collective-permute-done
  77.2 1.3 collective-permute-start
  78.5 3.3 collective-permute-done
  81.8 1.3 collective-permute-start
  83.1 3.3 collective-permute-done
  86.5 1.3 collective-permute-start
  87.8 3.3 collective-permute-done
  91.1 1.3 collective-permute-start
  92.4 3.5 collective-permute-done
  95.9 1.3 collective-permute-start
  97.2 4.6 %collective-permute-done = bf16[64,256]{1,0:T(8,128)(2,1)S(1)} collective-permute-done((bf16[64,256]{1,0:T(8,128)(2,1)S(1)}, bf16[64,256]{1,0:T(8,128)(2,1)S(1)}, u32[]{:S(2)}, u32[]{:S(2)}) %collective-permute-start) | collective-permute-done | bytes 32800 | tf_op jit(solution)/shard_map/while/body/eval_jaxpr/ppermute | solution.py:210
  101.7 1.3 collective-permute-start
  103.0 203.3 %collective-permute-done = bf16[64,256]{1,0:T(8,128)(2,1)S(1)} collective-permute-done((bf16[64,256]{1,0:T(8,128)(2,1)S(1)}, bf16[64,256]{1,0:T(8,128)(2,1)S(1)}, u32[]{:S(2)}, u32[]{:S(2)}) %collective-permute-start) | collective-permute-done | bytes 32800 | tf_op jit(solution)/shard_map/while/body/eval_jaxpr/ppermute | solution.py:210
  306.4 36.4 %conditional.7 = ((bf16[64,256]{1,0:T(8,128)(2,1)S(1)}, bf16[2,64,256]{2,1,0:T(8,128)(2,1)S(1)})) conditional(s32[]{:T(128)} %convert_element_type.112, (bf16[64,256]{1,0:T(8,128)(2,1)S(1)}, bf16[2,64,256]{2,1,0:T(8,128)(2,1)S(1)}) %tuple.87, (s32[]{:T(128)}, s32[]{:T(128)}, bf16[2,64,256]{2,1,0:T(8,128)(2,1)S(1)}, bf16[64,256]{1,0:T(8,128)(2,1)S(1)}, ...), branch_computations={%region_19.19_spmd, %region_20.20_spmd} | conditional | flops 32771 | bytes 1216686 | solution.py:219
  306.4 16.1 %all-gather = bf16[1024,256]{1,0:T(8,128)(2,1)S(1)} all-gather(bf16[64,256]{1,0:T(8,128)(2,1)S(1)} %bitcast_select_fusion.current), channel_id=2, replica_groups=mesh['section'=8,'y'=8,'core'=2,'dp'=4] {'y','core'}, dimensions={0}, use_global_device_ids=true | all-gather | bytes 557056 | tf_op jit(solution)/shard_map/while/body/eval_jaxpr/cond/branch_1_fun/all_gather | solution.py:179
  322.5 2.8 branch_1_fun.2
  325.3 17.2 %all_to_all.4.mixed = bf16[16,64,128]{2,1,0:T(8,128)(2,1)S(1)} all-to-all(bf16[16,64,128]{2,1,0:T(8,128)(2,1)S(1)} %branch_1_fun.2), channel_id=1, replica_groups=mesh['section'=8,'y'=8,'core'=2,'dp'=4] {'y','core'}, dimensions={0} | all-to-all | bytes 524288 | tf_op jit(solution)/shard_map/while/body/eval_jaxpr/cond/branch_1_fun/all_to_all | solution.py:181
  342.5 0.3 branch_1_fun.3
  342.8 1.3 collective-permute-start
  344.1 5.0 %collective-permute-done = bf16[64,256]{1,0:T(8,128)(2,1)S(1)} collective-permute-done((bf16[64,256]{1,0:T(8,128)(2,1)S(1)}, bf16[64,256]{1,0:T(8,128)(2,1)S(1)}, u32[]{:S(2)}, u32[]{:S(2)}) %collective-permute-start) | collective-permute-done | bytes 32800 | tf_op jit(solution)/shard_map/while/body/eval_jaxpr/ppermute | solution.py:210
  349.1 36.4 %conditional.7 = ((bf16[64,256]{1,0:T(8,128)(2,1)S(1)}, bf16[2,64,256]{2,1,0:T(8,128)(2,1)S(1)})) conditional(s32[]{:T(128)} %convert_element_type.112, (bf16[64,256]{1,0:T(8,128)(2,1)S(1)}, bf16[2,64,256]{2,1,0:T(8,128)(2,1)S(1)}) %tuple.87, (s32[]{:T(128)}, s32[]{:T(128)}, bf16[2,64,256]{2,1,0:T(8,128)(2,1)S(1)}, bf16[64,256]{1,0:T(8,128)(2,1)S(1)}, ...), branch_computations={%region_19.19_spmd, %region_20.20_spmd} | conditional | flops 32771 | bytes 1216686 | solution.py:219
  349.1 16.1 %all-gather = bf16[1024,256]{1,0:T(8,128)(2,1)S(1)} all-gather(bf16[64,256]{1,0:T(8,128)(2,1)S(1)} %bitcast_select_fusion.current), channel_id=2, replica_groups=mesh['section'=8,'y'=8,'core'=2,'dp'=4] {'y','core'}, dimensions={0}, use_global_device_ids=true | all-gather | bytes 557056 | tf_op jit(solution)/shard_map/while/body/eval_jaxpr/cond/branch_1_fun/all_gather | solution.py:179
  365.2 2.8 branch_1_fun.2
  368.1 17.2 %all_to_all.4.mixed = bf16[16,64,128]{2,1,0:T(8,128)(2,1)S(1)} all-to-all(bf16[16,64,128]{2,1,0:T(8,128)(2,1)S(1)} %branch_1_fun.2), channel_id=1, replica_groups=mesh['section'=8,'y'=8,'core'=2,'dp'=4] {'y','core'}, dimensions={0} | all-to-all | bytes 524288 | tf_op jit(solution)/shard_map/while/body/eval_jaxpr/cond/branch_1_fun/all_to_all | solution.py:181
  385.2 0.3 branch_1_fun.3
  385.6 0.6 copy-done.3
  386.2 0.6 fusion.100
  386.8 0.6 slice_bitcast_fusion
  (88 shorter events, 3.2 us)
Async XLA Ops:
  0.6 66.2 %copy-start = (bf16[512,256]{1,0:T(8,128)(2,1)S(1)}, bf16[512,256]{1,0:T(8,128)(2,1)}, u32[]{:S(2)}) copy-start(bf16[512,256]{1,0:T(8,128)(2,1)} %param.36) | copy-start | bytes 786436
  0.7 0.7 copy-start.12
  0.7 0.7 copy-start.13
  1.4 0.7 copy-start.17
  20.9 0.7 copy-start.6
  20.9 0.7 copy-start.7
  20.9 0.7 copy-start.8
  20.9 0.7 copy-start.10
  20.9 0.7 copy-start.11
  21.7 45.2 %copy-start.14 = (f32[512]{0:T(512)S(1)}, f32[512]{0:T(512)}, u32[]{:S(2)}) copy-start(f32[512]{0:T(512)} %param.35) | copy-start | bytes 6148
  21.7 45.2 %copy-start.15 = (f32[512]{0:T(512)S(1)}, f32[512]{0:T(512)}, u32[]{:S(2)}) copy-start(f32[512]{0:T(512)} %param.34) | copy-start | bytes 6148
  21.7 45.2 %copy-start.16 = (f32[256]{0:T(256)S(1)}, f32[256]{0:T(256)}, u32[]{:S(2)}) copy-start(f32[256]{0:T(256)} %param.37) | copy-start | bytes 3076
  21.7 45.5 %copy-start.2 = (bf16[1,4096,128]{2,1,0:T(8,128)(2,1)S(1)}, bf16[1,4096,128]{2,1,0:T(8,128)(2,1)}, u32[]{:S(2)}) copy-start(bf16[1,4096,128]{2,1,0:T(8,128)(2,1)} %param.40) | copy-start | bytes 3145732
  65.1 2.1 copy-start.1
  67.1 0.7 copy-start.4
  67.1 0.7 copy-start.5
  67.2 0.7 copy-start.9
  67.9 4.6 %collective-permute-start = (bf16[64,256]{1,0:T(8,128)(2,1)S(1)}, bf16[64,256]{1,0:T(8,128)(2,1)S(1)}, u32[]{:S(2)}, u32[]{:S(2)}) collective-permute-start(bf16[64,256]{1,0:T(8,128)(2,1)S(1)} %get-tuple-element.556), channel_id=1, source_target_pairs={{0,64},{64,128},{128,192},{192,256},{256,320},{320,384},{384,448},... | collective-permute-start | bytes 98312 | tf_op jit(solution)/shard_map/while/body/eval_jaxpr/ppermute | solution.py:210
  72.5 4.6 %collective-permute-start = (bf16[64,256]{1,0:T(8,128)(2,1)S(1)}, bf16[64,256]{1,0:T(8,128)(2,1)S(1)}, u32[]{:S(2)}, u32[]{:S(2)}) collective-permute-start(bf16[64,256]{1,0:T(8,128)(2,1)S(1)} %get-tuple-element.556), channel_id=1, source_target_pairs={{0,64},{64,128},{128,192},{192,256},{256,320},{320,384},{384,448},... | collective-permute-start | bytes 98312 | tf_op jit(solution)/shard_map/while/body/eval_jaxpr/ppermute | solution.py:210
  77.2 4.6 %collective-permute-start = (bf16[64,256]{1,0:T(8,128)(2,1)S(1)}, bf16[64,256]{1,0:T(8,128)(2,1)S(1)}, u32[]{:S(2)}, u32[]{:S(2)}) collective-permute-start(bf16[64,256]{1,0:T(8,128)(2,1)S(1)} %get-tuple-element.556), channel_id=1, source_target_pairs={{0,64},{64,128},{128,192},{192,256},{256,320},{320,384},{384,448},... | collective-permute-start | bytes 98312 | tf_op jit(solution)/shard_map/while/body/eval_jaxpr/ppermute | solution.py:210
  81.8 4.6 %collective-permute-start = (bf16[64,256]{1,0:T(8,128)(2,1)S(1)}, bf16[64,256]{1,0:T(8,128)(2,1)S(1)}, u32[]{:S(2)}, u32[]{:S(2)}) collective-permute-start(bf16[64,256]{1,0:T(8,128)(2,1)S(1)} %get-tuple-element.556), channel_id=1, source_target_pairs={{0,64},{64,128},{128,192},{192,256},{256,320},{320,384},{384,448},... | collective-permute-start | bytes 98312 | tf_op jit(solution)/shard_map/while/body/eval_jaxpr/ppermute | solution.py:210
  86.5 4.6 %collective-permute-start = (bf16[64,256]{1,0:T(8,128)(2,1)S(1)}, bf16[64,256]{1,0:T(8,128)(2,1)S(1)}, u32[]{:S(2)}, u32[]{:S(2)}) collective-permute-start(bf16[64,256]{1,0:T(8,128)(2,1)S(1)} %get-tuple-element.556), channel_id=1, source_target_pairs={{0,64},{64,128},{128,192},{192,256},{256,320},{320,384},{384,448},... | collective-permute-start | bytes 98312 | tf_op jit(solution)/shard_map/while/body/eval_jaxpr/ppermute | solution.py:210
  91.1 4.8 %collective-permute-start = (bf16[64,256]{1,0:T(8,128)(2,1)S(1)}, bf16[64,256]{1,0:T(8,128)(2,1)S(1)}, u32[]{:S(2)}, u32[]{:S(2)}) collective-permute-start(bf16[64,256]{1,0:T(8,128)(2,1)S(1)} %get-tuple-element.556), channel_id=1, source_target_pairs={{0,64},{64,128},{128,192},{192,256},{256,320},{320,384},{384,448},... | collective-permute-start | bytes 98312 | tf_op jit(solution)/shard_map/while/body/eval_jaxpr/ppermute | solution.py:210
  95.9 5.9 %collective-permute-start = (bf16[64,256]{1,0:T(8,128)(2,1)S(1)}, bf16[64,256]{1,0:T(8,128)(2,1)S(1)}, u32[]{:S(2)}, u32[]{:S(2)}) collective-permute-start(bf16[64,256]{1,0:T(8,128)(2,1)S(1)} %get-tuple-element.556), channel_id=1, source_target_pairs={{0,64},{64,128},{128,192},{192,256},{256,320},{320,384},{384,448},... | collective-permute-start | bytes 98312 | tf_op jit(solution)/shard_map/while/body/eval_jaxpr/ppermute | solution.py:210
  101.7 204.6 %collective-permute-start = (bf16[64,256]{1,0:T(8,128)(2,1)S(1)}, bf16[64,256]{1,0:T(8,128)(2,1)S(1)}, u32[]{:S(2)}, u32[]{:S(2)}) collective-permute-start(bf16[64,256]{1,0:T(8,128)(2,1)S(1)} %get-tuple-element.556), channel_id=1, source_target_pairs={{0,64},{64,128},{128,192},{192,256},{256,320},{320,384},{384,448},... | collective-permute-start | bytes 98312 | tf_op jit(solution)/shard_map/while/body/eval_jaxpr/ppermute | solution.py:210
  342.8 6.3 %collective-permute-start = (bf16[64,256]{1,0:T(8,128)(2,1)S(1)}, bf16[64,256]{1,0:T(8,128)(2,1)S(1)}, u32[]{:S(2)}, u32[]{:S(2)}) collective-permute-start(bf16[64,256]{1,0:T(8,128)(2,1)S(1)} %get-tuple-element.556), channel_id=1, source_target_pairs={{0,64},{64,128},{128,192},{192,256},{256,320},{320,384},{384,448},... | collective-permute-start | bytes 98312 | tf_op jit(solution)/shard_map/while/body/eval_jaxpr/ppermute | solution.py:210
  385.6 0.6 copy-start.3

commit v10 on v9

--- a/solution.py
+++ b/solution.py
@@ -51,16 +51,15 @@
 
 def mixing_kernel(place, blocks, gain, shift, query, key, value, masking, out):
     parts, rows, width = blocks.shape
-    total = jnp.zeros((rows, width), jnp.float32)
+    total = jnp.zeros((rows, 1), jnp.float32)
     for i in range(parts):
-        total += blocks[i].astype(jnp.float32)
-    average = jnp.sum(total, axis=-1, keepdims=True) / (parts * width)
-    total = jnp.zeros((rows, width), jnp.float32)
+        total += jnp.sum(blocks[i].astype(jnp.float32), axis=-1, keepdims=True)
+    average = total / (parts * width)
+    spread = jnp.zeros_like(average)
     for i in range(parts):
         centered = blocks[i].astype(jnp.float32) - average
-        total += centered * centered
-    spread = jnp.sum(total, axis=-1, keepdims=True) / (parts * width)
-    scale = lax.rsqrt(spread + 1e-05)
+        spread += jnp.sum(centered * centered, axis=-1, keepdims=True)
+    scale = lax.rsqrt(spread / (parts * width) + 1e-05)
     both = jnp.zeros((rows, 2 * HEAD_DIM), jnp.float32)
     values = jnp.zeros((rows, HEAD_DIM), jnp.float32)
     for i in range(parts):

time: 388 us -> 389 us (level)
  no operation moved by 1% of the time
where the time goes in v10:
time: 389 us; the launch traced here: 388 us
  waiting for transfers between devices  234 us (60%)
  blocking collectives  122 us (31%)
  starting transfers between devices  11.5 us (3%)
  Pallas kernels  6.48 us (2%)
  local copies, waits for them, and re-layouts  5.72 us (1%)
  other arithmetic  4.37 us (1%)
    ppermute x9, waiting for transfers between devices, advance(): lax.ppermute(previous, 'section', [(s, s + 1) for s in range(sections - 1)])  234 us
    psum x3, blocking collectives, gradients_of(): return lax.psum(lax.psum(lax.psum(packed, 'core'), 'dp'), 'y')  37.6 us
    all_to_all x2, blocking collectives, attend(): mixed = lax.all_to_all(copies, ('y', 'core'), 0, 0, tiled=True)  34.3 us
    all_gather x2, blocking collectives, attend(): whole = lax.all_gather(current, ('y', 'core'), axis=0, tiled=False)  32.2 us
    all_gather x1, blocking collectives, on_device(): lax.all_gather(wave[0].astype(jnp.float32), ('y', 'core'), axis=0, tiled=...  17.9 us
    ppermute x9, starting transfers between devices, advance(): lax.ppermute(previous, 'section', [(s, s + 1) for s in range(sections - 1)])  11.5 us
  transfers between devices with their start and end apart: 9, of which 9 were waited for; matrix products, arithmetic and copies ran while one was open for 0% of the time, Pallas kernels for 0%

profile of v10, /device:TPU:449, one launch (start us, length us, event | category | flops | bytes accessed | tf_op | source)
XLA Modules:
  0.0 388.2 jit_solution(9779749130056280141)
XLA Ops:
  0.7 0.7 copy-done.12
  1.5 0.6 copy-done.17
  2.8 17.9 %all-gather.1 = f32[16,1,40]{2,1,0:T(1,128)S(1)} all-gather(f32[1,1,40]{2,1,0:T(1,128)S(1)} %convert_element_type.85), channel_id=3, replica_groups=mesh['section'=8,'y'=8,'core'=2,'dp'=4] {'y','core'}, dimensions={0}, use_global_device_ids=true | all-gather | bytes 2720 | tf_op jit(solution)/shard_map/all_gather | solution.py:124
  21.1 0.6 copy-done.6
  21.7 43.4 %conditional.3 = (f32[16,512]{1,0:T(8,128)S(1)}) conditional(s32[]{:T(128)} %convert_element_type.82, () %tuple.42, (s32[]{:T(128)}, s32[]{:T(128)}, s32[1,16]{1,0:T(1,128)S(1)}, bf16[1,1,40]{2,1,0:T(2,128)(2,1)S(1)}, bf16[512,10]{0,1:T(8,128)(2,1)S(1)}, /*index=5*/f32[512]{0:T(512)S(1)}, f32[512]{0:T(512)S(1)}, f32[512]{0:T(512)S(1)}, ...), branch_computations={%region_6.7_spmd, %region_7.18_spmd} | conditional | flops 1064623 | bytes 458498 | solution.py:202
  21.7 0.5 broadcast.920
  22.3 0.7 reduce.36
  22.9 0.6 fusion.97
  25.6 0.6 fusion.21
  26.2 0.3 fusion.96
  27.5 3.4 psum.36
  31.0 13.3 %psum.37 = f32[16,512]{1,0:T(8,128)S(1)} all-reduce(f32[16,512]{1,0:T(8,128)S(1)} %psum.36), channel_id=1, replica_groups=mesh['section'=8,'y'=8,'core'=2,'dp'=4] {'dp'}, use_global_device_ids=true, to_apply=%region_16.16 | all-reduce | flops 8192 | bytes 65536 | tf_op jit(solution)/shard_map/cond/branch_1_fun/psum | solution.py:199
  44.3 20.8 %psum.38 = f32[16,512]{1,0:T(8,128)S(1)} all-reduce(f32[16,512]{1,0:T(8,128)S(1)} %psum.37), channel_id=1, replica_groups=mesh['section'=8,'y'=8,'core'=2,'dp'=4] {'y'}, use_global_device_ids=true, to_apply=%region_17.17 | all-reduce | flops 8192 | bytes 65536 | tf_op jit(solution)/shard_map/cond/branch_1_fun/psum | solution.py:199
  65.1 0.3 fusion.101
  65.6 0.8 convert_reduce_fusion
  67.2 0.6 copy-done.4
  67.9 318.5 %while.16 = (s32[]{:T(128)}, bf16[64,256]{1,0:T(8,128)(2,1)S(1)}, bf16[2,64,256]{2,1,0:T(8,128)(2,1)S(1)}, s32[]{:T(128)}, bf16[2,64,256]{2,1,0:T(8,128)(2,1)S(1...) while((s32[]{:T(128)}, bf16[64,256]{1,0:T(8,128)(2,1)S(1)}, ...), condition=%wide.region_21.22_spmd.clone, body=%wide.region_18.21_spmd.clone.sunk | while | flops 32778 | bytes 1348145 | solution.py:226
  67.9 1.3 collective-permute-start
  69.2 3.3 collective-permute-done
  72.5 1.3 collective-permute-start
  73.8 3.3 collective-permute-done
  77.2 1.3 collective-permute-start
  78.5 3.3 collective-permute-done
  81.8 1.3 collective-permute-start
  83.1 3.3 collective-permute-done
  86.5 1.3 collective-permute-start
  87.8 3.3 collective-permute-done
  91.1 1.3 collective-permute-start
  92.4 3.5 collective-permute-done
  95.9 1.3 collective-permute-start
  97.2 4.6 %collective-permute-done = bf16[64,256]{1,0:T(8,128)(2,1)S(1)} collective-permute-done((bf16[64,256]{1,0:T(8,128)(2,1)S(1)}, bf16[64,256]{1,0:T(8,128)(2,1)S(1)}, u32[]{:S(2)}, u32[]{:S(2)}) %collective-permute-start) | collective-permute-done | bytes 32800 | tf_op jit(solution)/shard_map/while/body/eval_jaxpr/ppermute | solution.py:209
  101.7 1.3 collective-permute-start
  103.0 203.9 %collective-permute-done = bf16[64,256]{1,0:T(8,128)(2,1)S(1)} collective-permute-done((bf16[64,256]{1,0:T(8,128)(2,1)S(1)}, bf16[64,256]{1,0:T(8,128)(2,1)S(1)}, u32[]{:S(2)}, u32[]{:S(2)}) %collective-permute-start) | collective-permute-done | bytes 32800 | tf_op jit(solution)/shard_map/while/body/eval_jaxpr/ppermute | solution.py:209
  307.0 36.5 %conditional.7 = ((bf16[64,256]{1,0:T(8,128)(2,1)S(1)}, bf16[2,64,256]{2,1,0:T(8,128)(2,1)S(1)})) conditional(s32[]{:T(128)} %convert_element_type.112, (bf16[64,256]{1,0:T(8,128)(2,1)S(1)}, bf16[2,64,256]{2,1,0:T(8,128)(2,1)S(1)}) %tuple.87, (s32[]{:T(128)}, s32[]{:T(128)}, bf16[2,64,256]{2,1,0:T(8,128)(2,1)S(1)}, bf16[64,256]{1,0:T(8,128)(2,1)S(1)}, ...), branch_computations={%region_19.19_spmd, %region_20.20_spmd} | conditional | flops 32771 | bytes 1216686 | solution.py:218
  307.0 16.1 %all-gather = bf16[1024,256]{1,0:T(8,128)(2,1)S(1)} all-gather(bf16[64,256]{1,0:T(8,128)(2,1)S(1)} %bitcast_select_fusion.current), channel_id=2, replica_groups=mesh['section'=8,'y'=8,'core'=2,'dp'=4] {'y','core'}, dimensions={0}, use_global_device_ids=true | all-gather | bytes 557056 | tf_op jit(solution)/shard_map/while/body/eval_jaxpr/cond/branch_1_fun/all_gather | solution.py:178
  323.1 2.9 branch_1_fun.2
  326.0 17.2 %all_to_all.4.mixed = bf16[16,64,128]{2,1,0:T(8,128)(2,1)S(1)} all-to-all(bf16[16,64,128]{2,1,0:T(8,128)(2,1)S(1)} %branch_1_fun.2), channel_id=1, replica_groups=mesh['section'=8,'y'=8,'core'=2,'dp'=4] {'y','core'}, dimensions={0} | all-to-all | bytes 524288 | tf_op jit(solution)/shard_map/while/body/eval_jaxpr/cond/branch_1_fun/all_to_all | solution.py:180
  343.2 0.3 branch_1_fun.3
  343.5 1.3 collective-permute-start
  344.8 5.0 %collective-permute-done = bf16[64,256]{1,0:T(8,128)(2,1)S(1)} collective-permute-done((bf16[64,256]{1,0:T(8,128)(2,1)S(1)}, bf16[64,256]{1,0:T(8,128)(2,1)S(1)}, u32[]{:S(2)}, u32[]{:S(2)}) %collective-permute-start) | collective-permute-done | bytes 32800 | tf_op jit(solution)/shard_map/while/body/eval_jaxpr/ppermute | solution.py:209
  349.8 36.5 %conditional.7 = ((bf16[64,256]{1,0:T(8,128)(2,1)S(1)}, bf16[2,64,256]{2,1,0:T(8,128)(2,1)S(1)})) conditional(s32[]{:T(128)} %convert_element_type.112, (bf16[64,256]{1,0:T(8,128)(2,1)S(1)}, bf16[2,64,256]{2,1,0:T(8,128)(2,1)S(1)}) %tuple.87, (s32[]{:T(128)}, s32[]{:T(128)}, bf16[2,64,256]{2,1,0:T(8,128)(2,1)S(1)}, bf16[64,256]{1,0:T(8,128)(2,1)S(1)}, ...), branch_computations={%region_19.19_spmd, %region_20.20_spmd} | conditional | flops 32771 | bytes 1216686 | solution.py:218
  349.8 16.1 %all-gather = bf16[1024,256]{1,0:T(8,128)(2,1)S(1)} all-gather(bf16[64,256]{1,0:T(8,128)(2,1)S(1)} %bitcast_select_fusion.current), channel_id=2, replica_groups=mesh['section'=8,'y'=8,'core'=2,'dp'=4] {'y','core'}, dimensions={0}, use_global_device_ids=true | all-gather | bytes 557056 | tf_op jit(solution)/shard_map/while/body/eval_jaxpr/cond/branch_1_fun/all_gather | solution.py:178
  365.9 2.9 branch_1_fun.2
  368.9 17.2 %all_to_all.4.mixed = bf16[16,64,128]{2,1,0:T(8,128)(2,1)S(1)} all-to-all(bf16[16,64,128]{2,1,0:T(8,128)(2,1)S(1)} %branch_1_fun.2), channel_id=1, replica_groups=mesh['section'=8,'y'=8,'core'=2,'dp'=4] {'y','core'}, dimensions={0} | all-to-all | bytes 524288 | tf_op jit(solution)/shard_map/while/body/eval_jaxpr/cond/branch_1_fun/all_to_all | solution.py:180
  386.0 0.3 branch_1_fun.3
  386.4 0.6 copy-done.3
  387.0 0.6 fusion.100
  387.6 0.6 slice_bitcast_fusion
  (88 shorter events, 3.2 us)
Async XLA Ops:
  0.6 66.2 %copy-start = (bf16[512,256]{1,0:T(8,128)(2,1)S(1)}, bf16[512,256]{1,0:T(8,128)(2,1)}, u32[]{:S(2)}) copy-start(bf16[512,256]{1,0:T(8,128)(2,1)} %param.36) | copy-start | bytes 786436
  0.7 0.7 copy-start.12
  0.7 0.7 copy-start.13
  1.4 0.7 copy-start.17
  20.9 0.7 copy-start.6
  20.9 0.7 copy-start.7
  20.9 0.7 copy-start.8
  20.9 0.7 copy-start.10
  20.9 0.7 copy-start.11
  21.7 45.2 %copy-start.14 = (f32[512]{0:T(512)S(1)}, f32[512]{0:T(512)}, u32[]{:S(2)}) copy-start(f32[512]{0:T(512)} %param.35) | copy-start | bytes 6148
  21.7 45.2 %copy-start.15 = (f32[512]{0:T(512)S(1)}, f32[512]{0:T(512)}, u32[]{:S(2)}) copy-start(f32[512]{0:T(512)} %param.34) | copy-start | bytes 6148
  21.7 45.2 %copy-start.16 = (f32[256]{0:T(256)S(1)}, f32[256]{0:T(256)}, u32[]{:S(2)}) copy-start(f32[256]{0:T(256)} %param.37) | copy-start | bytes 3076
  21.7 45.5 %copy-start.2 = (bf16[1,4096,128]{2,1,0:T(8,128)(2,1)S(1)}, bf16[1,4096,128]{2,1,0:T(8,128)(2,1)}, u32[]{:S(2)}) copy-start(bf16[1,4096,128]{2,1,0:T(8,128)(2,1)} %param.40) | copy-start | bytes 3145732
  65.1 2.1 copy-start.1
  67.1 0.7 copy-start.4
  67.1 0.7 copy-start.5
  67.2 0.7 copy-start.9
  67.9 4.6 %collective-permute-start = (bf16[64,256]{1,0:T(8,128)(2,1)S(1)}, bf16[64,256]{1,0:T(8,128)(2,1)S(1)}, u32[]{:S(2)}, u32[]{:S(2)}) collective-permute-start(bf16[64,256]{1,0:T(8,128)(2,1)S(1)} %get-tuple-element.556), channel_id=1, source_target_pairs={{0,64},{64,128},{128,192},{192,256},{256,320},{320,384},{384,448},... | collective-permute-start | bytes 98312 | tf_op jit(solution)/shard_map/while/body/eval_jaxpr/ppermute | solution.py:209
  72.5 4.6 %collective-permute-start = (bf16[64,256]{1,0:T(8,128)(2,1)S(1)}, bf16[64,256]{1,0:T(8,128)(2,1)S(1)}, u32[]{:S(2)}, u32[]{:S(2)}) collective-permute-start(bf16[64,256]{1,0:T(8,128)(2,1)S(1)} %get-tuple-element.556), channel_id=1, source_target_pairs={{0,64},{64,128},{128,192},{192,256},{256,320},{320,384},{384,448},... | collective-permute-start | bytes 98312 | tf_op jit(solution)/shard_map/while/body/eval_jaxpr/ppermute | solution.py:209
  77.2 4.6 %collective-permute-start = (bf16[64,256]{1,0:T(8,128)(2,1)S(1)}, bf16[64,256]{1,0:T(8,128)(2,1)S(1)}, u32[]{:S(2)}, u32[]{:S(2)}) collective-permute-start(bf16[64,256]{1,0:T(8,128)(2,1)S(1)} %get-tuple-element.556), channel_id=1, source_target_pairs={{0,64},{64,128},{128,192},{192,256},{256,320},{320,384},{384,448},... | collective-permute-start | bytes 98312 | tf_op jit(solution)/shard_map/while/body/eval_jaxpr/ppermute | solution.py:209
  81.8 4.6 %collective-permute-start = (bf16[64,256]{1,0:T(8,128)(2,1)S(1)}, bf16[64,256]{1,0:T(8,128)(2,1)S(1)}, u32[]{:S(2)}, u32[]{:S(2)}) collective-permute-start(bf16[64,256]{1,0:T(8,128)(2,1)S(1)} %get-tuple-element.556), channel_id=1, source_target_pairs={{0,64},{64,128},{128,192},{192,256},{256,320},{320,384},{384,448},... | collective-permute-start | bytes 98312 | tf_op jit(solution)/shard_map/while/body/eval_jaxpr/ppermute | solution.py:209
  86.5 4.6 %collective-permute-start = (bf16[64,256]{1,0:T(8,128)(2,1)S(1)}, bf16[64,256]{1,0:T(8,128)(2,1)S(1)}, u32[]{:S(2)}, u32[]{:S(2)}) collective-permute-start(bf16[64,256]{1,0:T(8,128)(2,1)S(1)} %get-tuple-element.556), channel_id=1, source_target_pairs={{0,64},{64,128},{128,192},{192,256},{256,320},{320,384},{384,448},... | collective-permute-start | bytes 98312 | tf_op jit(solution)/shard_map/while/body/eval_jaxpr/ppermute | solution.py:209
  91.1 4.8 %collective-permute-start = (bf16[64,256]{1,0:T(8,128)(2,1)S(1)}, bf16[64,256]{1,0:T(8,128)(2,1)S(1)}, u32[]{:S(2)}, u32[]{:S(2)}) collective-permute-start(bf16[64,256]{1,0:T(8,128)(2,1)S(1)} %get-tuple-element.556), channel_id=1, source_target_pairs={{0,64},{64,128},{128,192},{192,256},{256,320},{320,384},{384,448},... | collective-permute-start | bytes 98312 | tf_op jit(solution)/shard_map/while/body/eval_jaxpr/ppermute | solution.py:209
  95.9 5.9 %collective-permute-start = (bf16[64,256]{1,0:T(8,128)(2,1)S(1)}, bf16[64,256]{1,0:T(8,128)(2,1)S(1)}, u32[]{:S(2)}, u32[]{:S(2)}) collective-permute-start(bf16[64,256]{1,0:T(8,128)(2,1)S(1)} %get-tuple-element.556), channel_id=1, source_target_pairs={{0,64},{64,128},{128,192},{192,256},{256,320},{320,384},{384,448},... | collective-permute-start | bytes 98312 | tf_op jit(solution)/shard_map/while/body/eval_jaxpr/ppermute | solution.py:209
  101.7 205.2 %collective-permute-start = (bf16[64,256]{1,0:T(8,128)(2,1)S(1)}, bf16[64,256]{1,0:T(8,128)(2,1)S(1)}, u32[]{:S(2)}, u32[]{:S(2)}) collective-permute-start(bf16[64,256]{1,0:T(8,128)(2,1)S(1)} %get-tuple-element.556), channel_id=1, source_target_pairs={{0,64},{64,128},{128,192},{192,256},{256,320},{320,384},{384,448},... | collective-permute-start | bytes 98312 | tf_op jit(solution)/shard_map/while/body/eval_jaxpr/ppermute | solution.py:209
  343.5 6.3 %collective-permute-start = (bf16[64,256]{1,0:T(8,128)(2,1)S(1)}, bf16[64,256]{1,0:T(8,128)(2,1)S(1)}, u32[]{:S(2)}, u32[]{:S(2)}) collective-permute-start(bf16[64,256]{1,0:T(8,128)(2,1)S(1)} %get-tuple-element.556), channel_id=1, source_target_pairs={{0,64},{64,128},{128,192},{192,256},{256,320},{320,384},{384,448},... | collective-permute-start | bytes 98312 | tf_op jit(solution)/shard_map/while/body/eval_jaxpr/ppermute | solution.py:209
  386.4 0.6 copy-start.3

commit v11 on v9

--- a/solution.py
+++ b/solution.py
@@ -77,7 +77,7 @@
     raised = jnp.exp(scores - jnp.max(scores, axis=-1, keepdims=True))
     attention = (raised / jnp.sum(raised, axis=-1, keepdims=True)).astype(jnp.bfloat16)
     mixture = product(attention, values.astype(jnp.bfloat16)).astype(jnp.bfloat16)
-    out[...] = jnp.broadcast_to(mixture[None], out.shape)
+    out[...] = mixture
 
 
 def leaving_kernel(place, mixed, current, weights, bias, held, out, outputs):
@@ -157,7 +157,7 @@
     smem = pl.BlockSpec(memory_space=pltpu.SMEM)
     mixing = pl.pallas_call(
         mixing_kernel,
-        out_shape=jax.ShapeDtypeStruct((group, rows, HEAD_DIM), jnp.bfloat16),
+        out_shape=jax.ShapeDtypeStruct((rows, HEAD_DIM), jnp.bfloat16),
         in_specs=[smem] + [vmem] * 7,
         out_specs=vmem,
         compiler_params=pltpu.CompilerParams(vmem_limit_bytes=24 * 2**20),
@@ -177,8 +177,8 @@
     def attend(current, slot, outputs):
         place = slot.reshape(1)
         whole = lax.all_gather(current, ("y", "core"), axis=0, tiled=False)
-        copies = mixing(place, whole, gain, shift, query, key, value, maskings)
-        mixed = lax.all_to_all(copies, ("y", "core"), 0, 0, tiled=True)
+        mixture = mixing(place, whole, gain, shift, query, key, value, maskings)
+        mixed = lax.all_gather(mixture, ("y", "core"), axis=0, tiled=False)
         return leaving(place, mixed, current, out_part, out_bias, outputs)
 
     def gradients_of():

time: 388 us -> 386 us (level)
    all_to_all x2 -> x0, blocking collectives: 34.3 us -> none  [attend(): mixed = lax.all_to_all(copies, ('y', 'core'), 0, 0, tiled=True)]
    all_gather x0 -> x2, blocking collectives: none -> 31.8 us  [attend(): mixed = lax.all_gather(mixture, ('y', 'core'), axis=0, tiled=False)]
where the time goes in v11:
time: 386 us
  waiting for transfers between devices  231 us (60%)
  blocking collectives  122 us (32%)
  starting transfers between devices  11.5 us (3%)
  Pallas kernels  6.26 us (2%)
  local copies, waits for them, and re-layouts  5.72 us (1%)
  other arithmetic  4.37 us (1%)
    ppermute x9, waiting for transfers between devices, advance(): lax.ppermute(previous, 'section', [(s, s + 1) for s in range(sections - 1)])  231 us
    psum x3, blocking collectives, gradients_of(): return lax.psum(lax.psum(lax.psum(packed, 'core'), 'dp'), 'y')  37.6 us
    all_gather x2, blocking collectives, attend(): whole = lax.all_gather(current, ('y', 'core'), axis=0, tiled=False)  34.8 us
    all_gather x2, blocking collectives, attend(): mixed = lax.all_gather(mixture, ('y', 'core'), axis=0, tiled=False)  31.8 us
    all_gather x1, blocking collectives, on_device(): lax.all_gather(wave[0].astype(jnp.float32), ('y', 'core'), axis=0, tiled=...  17.9 us
    ppermute x9, starting transfers between devices, advance(): lax.ppermute(previous, 'section', [(s, s + 1) for s in range(sections - 1)])  11.5 us
  transfers between devices with their start and end apart: 9, of which 9 were waited for; matrix products, arithmetic and copies ran while one was open for 0% of the time, Pallas kernels for 0%

profile of v11, /device:TPU:449, one launch (start us, length us, event | category | flops | bytes accessed | tf_op | source)
XLA Modules:
  0.0 385.7 jit_solution(7999726379176767173)
XLA Ops:
  0.7 0.7 copy-done.12
  1.5 0.6 copy-done.17
  2.8 17.9 %all-gather.2 = f32[16,1,40]{2,1,0:T(1,128)S(1)} all-gather(f32[1,1,40]{2,1,0:T(1,128)S(1)} %convert_element_type.85), channel_id=4, replica_groups=mesh['section'=8,'y'=8,'core'=2,'dp'=4] {'y','core'}, dimensions={0}, use_global_device_ids=true | all-gather | bytes 2720 | tf_op jit(solution)/shard_map/all_gather | solution.py:125
  21.1 0.6 copy-done.6
  21.7 43.4 %conditional.3 = (f32[16,512]{1,0:T(8,128)S(1)}) conditional(s32[]{:T(128)} %convert_element_type.82, () %tuple.42, (s32[]{:T(128)}, s32[]{:T(128)}, s32[1,16]{1,0:T(1,128)S(1)}, bf16[1,1,40]{2,1,0:T(2,128)(2,1)S(1)}, bf16[512,10]{0,1:T(8,128)(2,1)S(1)}, /*index=5*/f32[512]{0:T(512)S(1)}, f32[512]{0:T(512)S(1)}, f32[512]{0:T(512)S(1)}, ...), branch_computations={%region_6.7_spmd, %region_7.18_spmd} | conditional | flops 1064623 | bytes 458498 | solution.py:203
  21.7 0.5 broadcast.920
  22.3 0.7 reduce.36
  22.9 0.6 fusion.97
  25.6 0.6 fusion.21
  26.2 0.3 fusion.96
  27.5 3.4 psum.36
  31.0 13.3 %psum.37 = f32[16,512]{1,0:T(8,128)S(1)} all-reduce(f32[16,512]{1,0:T(8,128)S(1)} %psum.36), channel_id=1, replica_groups=mesh['section'=8,'y'=8,'core'=2,'dp'=4] {'dp'}, use_global_device_ids=true, to_apply=%region_16.16 | all-reduce | flops 8192 | bytes 65536 | tf_op jit(solution)/shard_map/cond/branch_1_fun/psum | solution.py:200
  44.3 20.8 %psum.38 = f32[16,512]{1,0:T(8,128)S(1)} all-reduce(f32[16,512]{1,0:T(8,128)S(1)} %psum.37), channel_id=1, replica_groups=mesh['section'=8,'y'=8,'core'=2,'dp'=4] {'y'}, use_global_device_ids=true, to_apply=%region_17.17 | all-reduce | flops 8192 | bytes 65536 | tf_op jit(solution)/shard_map/cond/branch_1_fun/psum | solution.py:200
  65.1 0.3 fusion.101
  65.6 0.8 convert_reduce_fusion
  67.2 0.6 copy-done.4
  67.9 316.0 %while.16 = (s32[]{:T(128)}, bf16[64,256]{1,0:T(8,128)(2,1)S(1)}, bf16[2,64,256]{2,1,0:T(8,128)(2,1)S(1)}, s32[]{:T(128)}, bf16[2,64,256]{2,1,0:T(8,128)(2,1)S(1...) while((s32[]{:T(128)}, bf16[64,256]{1,0:T(8,128)(2,1)S(1)}, ...), condition=%wide.region_21.22_spmd.clone, body=%wide.region_18.21_spmd.clone.sunk | while | flops 32778 | bytes 1102385 | solution.py:227
  67.9 1.3 collective-permute-start
  69.2 3.3 collective-permute-done
  72.5 1.3 collective-permute-start
  73.8 3.3 collective-permute-done
  77.2 1.3 collective-permute-start
  78.5 3.3 collective-permute-done
  81.8 1.3 collective-permute-start
  83.1 3.3 collective-permute-done
  86.5 1.3 collective-permute-start
  87.8 3.3 collective-permute-done
  91.1 1.3 collective-permute-start
  92.4 3.5 collective-permute-done
  95.9 1.3 collective-permute-start
  97.2 4.6 %collective-permute-done = bf16[64,256]{1,0:T(8,128)(2,1)S(1)} collective-permute-done((bf16[64,256]{1,0:T(8,128)(2,1)S(1)}, bf16[64,256]{1,0:T(8,128)(2,1)S(1)}, u32[]{:S(2)}, u32[]{:S(2)}) %collective-permute-start) | collective-permute-done | bytes 32800 | tf_op jit(solution)/shard_map/while/body/eval_jaxpr/ppermute | solution.py:210
  101.7 1.3 collective-permute-start
  103.0 201.8 %collective-permute-done = bf16[64,256]{1,0:T(8,128)(2,1)S(1)} collective-permute-done((bf16[64,256]{1,0:T(8,128)(2,1)S(1)}, bf16[64,256]{1,0:T(8,128)(2,1)S(1)}, u32[]{:S(2)}, u32[]{:S(2)}) %collective-permute-start) | collective-permute-done | bytes 32800 | tf_op jit(solution)/shard_map/while/body/eval_jaxpr/ppermute | solution.py:210
  304.9 36.4 %conditional.7 = ((bf16[64,256]{1,0:T(8,128)(2,1)S(1)}, bf16[2,64,256]{2,1,0:T(8,128)(2,1)S(1)})) conditional(s32[]{:T(128)} %convert_element_type.112, (bf16[64,256]{1,0:T(8,128)(2,1)S(1)}, bf16[2,64,256]{2,1,0:T(8,128)(2,1)S(1)}) %tuple.87, (s32[]{:T(128)}, s32[]{:T(128)}, bf16[2,64,256]{2,1,0:T(8,128)(2,1)S(1)}, bf16[64,256]{1,0:T(8,128)(2,1)S(1)}, ...), branch_computations={%region_19.19_spmd, %region_20.20_spmd} | conditional | flops 32771 | bytes 970926 | solution.py:219
  304.9 17.4 %all-gather = bf16[1024,256]{1,0:T(8,128)(2,1)S(1)} all-gather(bf16[64,256]{1,0:T(8,128)(2,1)S(1)} %bitcast_select_fusion.current), channel_id=2, replica_groups=mesh['section'=8,'y'=8,'core'=2,'dp'=4] {'y','core'}, dimensions={0}, use_global_device_ids=true | all-gather | bytes 557056 | tf_op jit(solution)/shard_map/while/body/eval_jaxpr/cond/branch_1_fun/all_gather | solution.py:179
  322.3 2.8 branch_1_fun.2
  325.1 15.9 %all-gather.1 = bf16[1024,128]{1,0:T(8,128)(2,1)S(1)} all-gather(bf16[64,128]{1,0:T(8,128)(2,1)S(1)} %branch_1_fun.2), channel_id=3, replica_groups=mesh['section'=8,'y'=8,'core'=2,'dp'=4] {'y','core'}, dimensions={0}, use_global_device_ids=true | all-gather | bytes 278528 | tf_op jit(solution)/shard_map/while/body/eval_jaxpr/cond/branch_1_fun/all_gather | solution.py:181
  341.0 0.3 branch_1_fun.3
  341.3 1.3 collective-permute-start
  342.6 4.8 %collective-permute-done = bf16[64,256]{1,0:T(8,128)(2,1)S(1)} collective-permute-done((bf16[64,256]{1,0:T(8,128)(2,1)S(1)}, bf16[64,256]{1,0:T(8,128)(2,1)S(1)}, u32[]{:S(2)}, u32[]{:S(2)}) %collective-permute-start) | collective-permute-done | bytes 32800 | tf_op jit(solution)/shard_map/while/body/eval_jaxpr/ppermute | solution.py:210
  347.5 36.4 %conditional.7 = ((bf16[64,256]{1,0:T(8,128)(2,1)S(1)}, bf16[2,64,256]{2,1,0:T(8,128)(2,1)S(1)})) conditional(s32[]{:T(128)} %convert_element_type.112, (bf16[64,256]{1,0:T(8,128)(2,1)S(1)}, bf16[2,64,256]{2,1,0:T(8,128)(2,1)S(1)}) %tuple.87, (s32[]{:T(128)}, s32[]{:T(128)}, bf16[2,64,256]{2,1,0:T(8,128)(2,1)S(1)}, bf16[64,256]{1,0:T(8,128)(2,1)S(1)}, ...), branch_computations={%region_19.19_spmd, %region_20.20_spmd} | conditional | flops 32771 | bytes 970926 | solution.py:219
  347.5 17.4 %all-gather = bf16[1024,256]{1,0:T(8,128)(2,1)S(1)} all-gather(bf16[64,256]{1,0:T(8,128)(2,1)S(1)} %bitcast_select_fusion.current), channel_id=2, replica_groups=mesh['section'=8,'y'=8,'core'=2,'dp'=4] {'y','core'}, dimensions={0}, use_global_device_ids=true | all-gather | bytes 557056 | tf_op jit(solution)/shard_map/while/body/eval_jaxpr/cond/branch_1_fun/all_gather | solution.py:179
  364.9 2.8 branch_1_fun.2
  367.7 15.9 %all-gather.1 = bf16[1024,128]{1,0:T(8,128)(2,1)S(1)} all-gather(bf16[64,128]{1,0:T(8,128)(2,1)S(1)} %branch_1_fun.2), channel_id=3, replica_groups=mesh['section'=8,'y'=8,'core'=2,'dp'=4] {'y','core'}, dimensions={0}, use_global_device_ids=true | all-gather | bytes 278528 | tf_op jit(solution)/shard_map/while/body/eval_jaxpr/cond/branch_1_fun/all_gather | solution.py:181
  383.6 0.3 branch_1_fun.3
  383.9 0.6 copy-done.3
  384.5 0.6 fusion.100
  385.1 0.6 slice_bitcast_fusion
  (88 shorter events, 3.2 us)
Async XLA Ops:
  0.6 66.2 %copy-start = (bf16[512,256]{1,0:T(8,128)(2,1)S(1)}, bf16[512,256]{1,0:T(8,128)(2,1)}, u32[]{:S(2)}) copy-start(bf16[512,256]{1,0:T(8,128)(2,1)} %param.36) | copy-start | bytes 786436
  0.7 0.7 copy-start.12
  0.7 0.7 copy-start.13
  1.4 0.7 copy-start.17
  20.9 0.7 copy-start.6
  20.9 0.7 copy-start.7
  20.9 0.7 copy-start.8
  20.9 0.7 copy-start.10
  20.9 0.7 copy-start.11
  21.7 45.2 %copy-start.14 = (f32[512]{0:T(512)S(1)}, f32[512]{0:T(512)}, u32[]{:S(2)}) copy-start(f32[512]{0:T(512)} %param.35) | copy-start | bytes 6148
  21.7 45.2 %copy-start.15 = (f32[512]{0:T(512)S(1)}, f32[512]{0:T(512)}, u32[]{:S(2)}) copy-start(f32[512]{0:T(512)} %param.34) | copy-start | bytes 6148
  21.7 45.2 %copy-start.16 = (f32[256]{0:T(256)S(1)}, f32[256]{0:T(256)}, u32[]{:S(2)}) copy-start(f32[256]{0:T(256)} %param.37) | copy-start | bytes 3076
  21.7 45.5 %copy-start.2 = (bf16[1,4096,128]{2,1,0:T(8,128)(2,1)S(1)}, bf16[1,4096,128]{2,1,0:T(8,128)(2,1)}, u32[]{:S(2)}) copy-start(bf16[1,4096,128]{2,1,0:T(8,128)(2,1)} %param.40) | copy-start | bytes 3145732
  65.1 2.1 copy-start.1
  67.1 0.7 copy-start.4
  67.1 0.7 copy-start.5
  67.2 0.7 copy-start.9
  67.9 4.6 %collective-permute-start = (bf16[64,256]{1,0:T(8,128)(2,1)S(1)}, bf16[64,256]{1,0:T(8,128)(2,1)S(1)}, u32[]{:S(2)}, u32[]{:S(2)}) collective-permute-start(bf16[64,256]{1,0:T(8,128)(2,1)S(1)} %get-tuple-element.556), channel_id=1, source_target_pairs={{0,64},{64,128},{128,192},{192,256},{256,320},{320,384},{384,448},... | collective-permute-start | bytes 98312 | tf_op jit(solution)/shard_map/while/body/eval_jaxpr/ppermute | solution.py:210
  72.5 4.6 %collective-permute-start = (bf16[64,256]{1,0:T(8,128)(2,1)S(1)}, bf16[64,256]{1,0:T(8,128)(2,1)S(1)}, u32[]{:S(2)}, u32[]{:S(2)}) collective-permute-start(bf16[64,256]{1,0:T(8,128)(2,1)S(1)} %get-tuple-element.556), channel_id=1, source_target_pairs={{0,64},{64,128},{128,192},{192,256},{256,320},{320,384},{384,448},... | collective-permute-start | bytes 98312 | tf_op jit(solution)/shard_map/while/body/eval_jaxpr/ppermute | solution.py:210
  77.2 4.6 %collective-permute-start = (bf16[64,256]{1,0:T(8,128)(2,1)S(1)}, bf16[64,256]{1,0:T(8,128)(2,1)S(1)}, u32[]{:S(2)}, u32[]{:S(2)}) collective-permute-start(bf16[64,256]{1,0:T(8,128)(2,1)S(1)} %get-tuple-element.556), channel_id=1, source_target_pairs={{0,64},{64,128},{128,192},{192,256},{256,320},{320,384},{384,448},... | collective-permute-start | bytes 98312 | tf_op jit(solution)/shard_map/while/body/eval_jaxpr/ppermute | solution.py:210
  81.8 4.6 %collective-permute-start = (bf16[64,256]{1,0:T(8,128)(2,1)S(1)}, bf16[64,256]{1,0:T(8,128)(2,1)S(1)}, u32[]{:S(2)}, u32[]{:S(2)}) collective-permute-start(bf16[64,256]{1,0:T(8,128)(2,1)S(1)} %get-tuple-element.556), channel_id=1, source_target_pairs={{0,64},{64,128},{128,192},{192,256},{256,320},{320,384},{384,448},... | collective-permute-start | bytes 98312 | tf_op jit(solution)/shard_map/while/body/eval_jaxpr/ppermute | solution.py:210
  86.5 4.6 %collective-permute-start = (bf16[64,256]{1,0:T(8,128)(2,1)S(1)}, bf16[64,256]{1,0:T(8,128)(2,1)S(1)}, u32[]{:S(2)}, u32[]{:S(2)}) collective-permute-start(bf16[64,256]{1,0:T(8,128)(2,1)S(1)} %get-tuple-element.556), channel_id=1, source_target_pairs={{0,64},{64,128},{128,192},{192,256},{256,320},{320,384},{384,448},... | collective-permute-start | bytes 98312 | tf_op jit(solution)/shard_map/while/body/eval_jaxpr/ppermute | solution.py:210
  91.1 4.8 %collective-permute-start = (bf16[64,256]{1,0:T(8,128)(2,1)S(1)}, bf16[64,256]{1,0:T(8,128)(2,1)S(1)}, u32[]{:S(2)}, u32[]{:S(2)}) collective-permute-start(bf16[64,256]{1,0:T(8,128)(2,1)S(1)} %get-tuple-element.556), channel_id=1, source_target_pairs={{0,64},{64,128},{128,192},{192,256},{256,320},{320,384},{384,448},... | collective-permute-start | bytes 98312 | tf_op jit(solution)/shard_map/while/body/eval_jaxpr/ppermute | solution.py:210
  95.9 5.9 %collective-permute-start = (bf16[64,256]{1,0:T(8,128)(2,1)S(1)}, bf16[64,256]{1,0:T(8,128)(2,1)S(1)}, u32[]{:S(2)}, u32[]{:S(2)}) collective-permute-start(bf16[64,256]{1,0:T(8,128)(2,1)S(1)} %get-tuple-element.556), channel_id=1, source_target_pairs={{0,64},{64,128},{128,192},{192,256},{256,320},{320,384},{384,448},... | collective-permute-start | bytes 98312 | tf_op jit(solution)/shard_map/while/body/eval_jaxpr/ppermute | solution.py:210
  101.7 203.1 %collective-permute-start = (bf16[64,256]{1,0:T(8,128)(2,1)S(1)}, bf16[64,256]{1,0:T(8,128)(2,1)S(1)}, u32[]{:S(2)}, u32[]{:S(2)}) collective-permute-start(bf16[64,256]{1,0:T(8,128)(2,1)S(1)} %get-tuple-element.556), channel_id=1, source_target_pairs={{0,64},{64,128},{128,192},{192,256},{256,320},{320,384},{384,448},... | collective-permute-start | bytes 98312 | tf_op jit(solution)/shard_map/while/body/eval_jaxpr/ppermute | solution.py:210
  341.3 6.1 %collective-permute-start = (bf16[64,256]{1,0:T(8,128)(2,1)S(1)}, bf16[64,256]{1,0:T(8,128)(2,1)S(1)}, u32[]{:S(2)}, u32[]{:S(2)}) collective-permute-start(bf16[64,256]{1,0:T(8,128)(2,1)S(1)} %get-tuple-element.556), channel_id=1, source_target_pairs={{0,64},{64,128},{128,192},{192,256},{256,320},{320,384},{384,448},... | collective-permute-start | bytes 98312 | tf_op jit(solution)/shard_map/while/body/eval_jaxpr/ppermute | solution.py:210
  383.9 0.6 copy-start.3
